TPU v7x, 128 devices: a whole 4x4x4 slice. The times are simulated.
128 devices in a mesh: branch: 4 (over x), subtree: 32 (over z, y, core).
Axes of the slice: x: 4, y: 4, z: 4, core: 2. Of those that a mesh axis runs over, the one named last changes fastest.
Arguments:
- vectors: float32 [64, 1048576], P(None, ('branch', 'subtree')), may hold values from -6 to 6
- basis: float32 [32, 1048576], P(None, ('branch', 'subtree')), may hold values from -0.75 to 0.75
- transfer: float32 [16384, 1024], P(('branch', 'subtree')), may hold values from -0.375 to 0.375
- leaf_coupling: float32 [16384, 32, 512], P(('branch', 'subtree')), may hold values from -0.25 to 0.25
- leaf_list: int32 [16384, 16], P(('branch', 'subtree')), may hold values from 0 to 16383, as said below
- leaf_mask: int32 [16384, 16], P(('branch', 'subtree')), may hold values 0 or 1
- parent_coupling: float32 [2048, 32, 1024], P(('branch', 'subtree')), may hold values from -0.1875 to 0.1875
- parent_list: int32 [2048, 32], P(('branch', 'subtree')), may hold values from 0 to 2047, as said below
- parent_mask: int32 [2048, 32], P(('branch', 'subtree')), may hold values 0 or 1
Outputs:
- product: float32 [64, 1048576], P(None, ('branch', 'subtree'))
Inputs may be any that keep to these rules, and one draw needn't show every extreme that they name: `leaf_list`: leaf clusters g * 128 to (g + 1) * 128 - 1 belong to device g, g counted over branch then subtree. The 128 rows of one device name leaves of devices of its own branch group only, each of those 32 devices in exactly 64 slots, padded slots included. `parent_list`: parent clusters g * 16 to (g + 1) * 16 - 1 belong to device g, g counted over branch then subtree. The 16 rows of one device name parents of devices with its own subtree index only, those of each of the 4 branch groups in exactly 128 slots, padded slots included.
All inputs are finite; a program needn't handle non-finite values. No bound on the sum of `leaf_mask` or of `parent_mask` on one device may be relied on, other than what follows from the above.
Results may differ from a plain program's by a relative error of at most 0.000065.
Values sent between devices are 32-bit elements; how exact they have to be, the bound alone decides.
No kernel may reach another device: no remote copies, remote signals or barrier semaphores. Data moves between devices by JAX's collectives and lax.ppermute only.
A program may use at most 256 MiB of HBM per device.

v0:
```python
import functools

import jax
import jax.numpy as jnp
from jax import lax
from jax.experimental import pallas as pl
from jax.experimental.pallas import tpu as pltpu
from jax.sharding import PartitionSpec as P

PTS = 64
K = 32
NV = 64
CHILD = 8
HALF = K // 2
LANES = 2 * NV

HIGHEST = lax.Precision.HIGHEST


def split(x):
    high = x.astype(jnp.bfloat16)
    low = (x - high.astype(jnp.float32)).astype(jnp.bfloat16)
    return high, low


def left_lanes(rows):
    return lax.broadcasted_iota(jnp.int32, (rows, LANES), 1) < NV


def coef_kernel(basis_ref, vectors_ref, out_ref):
    pairs = basis_ref.shape[1] // LANES
    left_v = left_lanes(NV)
    left_h = left_lanes(HALF)
    for pair in range(pairs):
        lanes = slice(pair * LANES, (pair + 1) * LANES)
        basis_high, basis_low = split(basis_ref[:, lanes])
        vec_high, vec_low = split(vectors_ref[:, lanes])
        zero = jnp.zeros_like(vec_high)
        weights = jnp.concatenate(
            [
                jnp.where(left_v, vec_high, zero),
                jnp.where(left_v, zero, vec_high),
                jnp.where(left_v, vec_low, zero),
                jnp.where(left_v, zero, vec_low),
            ],
            axis=0,
        )
        both = lax.dot_general(
            jnp.concatenate([basis_high, basis_low], axis=0),
            weights,
            (((1,), (1,)), ((), ())),
            preferred_element_type=jnp.float32,
        )
        summed = both[:K, :LANES] + (both[:K, LANES:] + both[K:, :LANES])
        upper, lower = summed[:HALF], summed[HALF:]
        out_ref[2 * pair] = jnp.where(left_h, upper, pltpu.roll(lower, NV, 1))
        out_ref[2 * pair + 1] = jnp.where(left_h, pltpu.roll(upper, NV, 1), lower)


def leaf_coefs(basis, vectors, block):
    leaves = basis.shape[1] // PTS
    return pl.pallas_call(
        coef_kernel,
        out_shape=jax.ShapeDtypeStruct((leaves, HALF, LANES), jnp.float32),
        grid=(leaves // block,),
        in_specs=[
            pl.BlockSpec((K, block * PTS), lambda i: (0, i)),
            pl.BlockSpec((NV, block * PTS), lambda i: (0, i)),
        ],
        out_specs=pl.BlockSpec((block, HALF, LANES), lambda i: (i, 0, 0)),
        compiler_params=pltpu.CompilerParams(vmem_limit_bytes=32 * 2**20),
        name="leaf_coef",
    )(basis, vectors)


def field_kernel(slots, where_ref, mask_ref, group_ref, coupling_ref, down_ref, basis_ref, out_ref):
    block = coupling_ref.shape[0]
    first = pl.program_id(0) * block
    left_h = left_lanes(HALF)
    left_k = left_lanes(K)
    left_v = left_lanes(NV)

    def leaf_field(leaf):
        parts = []
        for slot in range(slots):
            entry = (first + leaf) * slots + slot
            picked = group_ref[where_ref[entry]] * mask_ref[entry].astype(jnp.float32)
            high = picked.astype(jnp.bfloat16)
            high32 = high.astype(jnp.float32)
            low = pltpu.roll(picked - high32, NV, 1)
            parts.append(jnp.where(left_h, high32, low).astype(jnp.bfloat16))
            parts.append(jnp.where(left_h, low, high32).astype(jnp.bfloat16))
        both = jnp.dot(
            jnp.concatenate(split(coupling_ref[leaf]), axis=0),
            jnp.concatenate(parts, axis=0),
            preferred_element_type=jnp.float32,
        )
        summed = both[:K] + both[K:]
        return summed + pltpu.roll(summed, NV, 1)

    def one_pair(pair):
        total = jnp.where(left_k, leaf_field(2 * pair), leaf_field(2 * pair + 1)) + down_ref[pair]
        lanes = pl.ds(pl.multiple_of(pair * LANES, LANES), LANES)
        total_high, total_low = split(total)
        basis_high, basis_low = split(basis_ref[:, lanes])
        both = lax.dot_general(
            jnp.concatenate([total_high, total_low, total_high], axis=0),
            jnp.concatenate([basis_high, basis_high, basis_low], axis=0),
            (((0,), (0,)), ((), ())),
            preferred_element_type=jnp.float32,
        )
        out_ref[:, lanes] = jnp.where(left_v, both[:NV], both[NV:])

    @pl.loop(0, block // 4)
    def _(quad):
        one_pair(2 * quad)
        one_pair(2 * quad + 1)


def products(where, mask, group, coupling, down, basis, block):
    leaves, _, width = coupling.shape
    slots = width // K
    smem = pl.BlockSpec(memory_space=pltpu.SMEM)
    return pl.pallas_call(
        functools.partial(field_kernel, slots),
        out_shape=jax.ShapeDtypeStruct((NV, leaves * PTS), jnp.float32),
        grid=(leaves // block,),
        in_specs=[
            smem,
            smem,
            pl.BlockSpec(memory_space=pltpu.VMEM),
            pl.BlockSpec((block, K, width), lambda i: (i, 0, 0)),
            pl.BlockSpec((block // 2, K, LANES), lambda i: (i, 0, 0)),
            pl.BlockSpec((K, block * PTS), lambda i: (0, i)),
        ],
        out_specs=pl.BlockSpec((NV, block * PTS), lambda i: (0, i)),
        compiler_params=pltpu.CompilerParams(vmem_limit_bytes=56 * 2**20),
        name="leaf_field_product",
    )(where, mask, group, coupling, down, basis)


def coupled(coupling, picked, masks):
    count, slots = masks.shape
    masked = picked * masks.reshape(count * slots).astype(jnp.float32)[:, None, None]
    stacked = masked.reshape(count, slots * K, NV)
    return lax.dot_general(
        coupling,
        stacked,
        (((2,), (1,)), ((0,), (0,))),
        precision=HIGHEST,
        preferred_element_type=jnp.float32,
    )


def per_device(
    vectors,
    basis,
    transfer,
    leaf_coupling,
    leaf_list,
    leaf_mask,
    parent_coupling,
    parent_list,
    parent_mask,
):
    leaf_count = leaf_list.shape[0]
    parent_count = parent_list.shape[0]
    subtrees = lax.axis_size("subtree")
    coef = leaf_coefs(basis, vectors, 32)
    group_all = lax.all_gather(coef, "subtree", axis=0, tiled=True)

    natural = coef.reshape(parent_count, CHILD, HALF, 2, NV).transpose(0, 1, 3, 2, 4).reshape(parent_count, CHILD, K, NV)
    transfers = transfer.reshape(parent_count, CHILD, K, K)
    parent_coef = jnp.einsum("pcab,pcav->pbv", transfers, natural, precision=HIGHEST)
    parent_all = lax.all_gather(parent_coef, "branch", axis=0, tiled=True)
    parent_owner = parent_list // parent_count
    position = parent_owner // subtrees * parent_count + parent_list % parent_count
    parent_picked = parent_all[position.reshape(-1)]
    parent_field = coupled(parent_coupling, parent_picked, parent_mask)
    downward = jnp.einsum("pcab,pbv->pcav", transfers, parent_field, precision=HIGHEST)
    down_pairs = downward.reshape(leaf_count // 2, 2, K, NV).transpose(0, 2, 1, 3).reshape(leaf_count // 2, K, LANES)

    where = (leaf_list % (subtrees * leaf_count)).reshape(-1)
    return products(where, leaf_mask.reshape(-1), group_all, leaf_coupling, down_pairs, basis, 16)


def solution(mesh):
    return jax.shard_map(
        per_device,
        mesh=mesh,
        in_specs=(
            P(None, ("branch", "subtree")),
            P(None, ("branch", "subtree")),
            P(("branch", "subtree"), None),
            P(("branch", "subtree"), None, None),
            P(("branch", "subtree"), None),
            P(("branch", "subtree"), None),
            P(("branch", "subtree"), None, None),
            P(("branch", "subtree"), None),
            P(("branch", "subtree"), None),
        ),
        out_specs=P(None, ("branch", "subtree")),
        check_vma=False,
    )
```

profile of v0, /device:TPU:1, one launch (start us, length us, event | category | flops | bytes accessed | tf_op | source)
XLA Modules:
  0.0 176.6 jit_solution(17318920385483819752)
XLA Ops:
  6.5 0.0 copy-start
  6.5 0.0 all-gather.2.cloned.1.call-start
  6.5 0.0 copy-start.2
  6.5 1.4 copy-done.2
  7.9 0.0 copy-start.3
  7.9 1.6 copy-done.3
  9.5 3.3 %leaf_coef.1 = f32[128,16,128]{2,1,0:T(8,128)} custom-call(f32[32,8192]{1,0:T(8,128)S(1)} %copy-done.2, f32[64,8192]{1,0:T(8,128)S(1)} %copy-done.3), custom_call_target="tpu_custom_call" | custom-call | tf_op jit(solution)/shard_map/leaf_coef/pallas_call | solution.py:62
  12.8 0.0 all-gather.2.cloned.1.call-update
  12.8 3.3 %reshape.65 = f32[16,8,16,2,64]{4,3,2,1,0:T(2,128)} reshape(f32[128,16,128]{2,1,0:T(8,128)} %leaf_coef.1) | data formatting | bytes 2097152 | tf_op jit(solution)/shard_map/reshape | solution.py:172
  16.1 0.0 copy-start.5
  16.1 3.2 %copy.20 = f32[16,8,2,16,64]{4,3,2,1,0:T(8,128)} copy(f32[16,8,2,16,64]{4,2,3,1,0:T(2,128)} %bitcast.28) | data formatting | bytes 2097152 | tf_op jit(solution)/shard_map/transpose | solution.py:172
  19.3 0.0 copy-done.5
  19.4 0.0 copy-start.7
  19.4 2.0 %reshape.67 = f32[16,8,32,32]{3,2,1,0:T(8,128)} reshape(f32[128,1024]{1,0:T(8,128)S(1)} %copy-done.5) | data formatting | bytes 1048576 | tf_op jit(solution)/shard_map/reshape | solution.py:173
  21.4 0.0 copy-done.7
  21.4 0.1 reshape.68
  21.5 5.7 %convolution_bitcast_fusion = f32[16,32,64]{2,1,0:T(8,128)S(1)} fusion(f32[16,8,32,64]{3,2,1,0:T(8,128)} %bitcast.25, f32[16,8,32,32]{3,2,1,0:T(8,128)} %reshape.67), kind=kOutput, calls=%fused_computation.6 | convolution fusion | flops 100663296 | bytes 1703936 | tf_op jit(solution)/shard_map/pcab,pcav->pbv/dot_general | solution.py:174
  27.2 14.6 %all_gather.7 = f32[64,32,64]{2,1,0:T(8,128)S(1)} all-gather(f32[16,32,64]{2,1,0:T(8,128)S(1)} %convolution_bitcast_fusion), channel_id=1, replica_groups=mesh['branch'=4,'subtree'=32] {'branch'}, dimensions={0}, use_global_device_ids=true | all-gather | bytes 655360 | tf_op jit(solution)/shard_map/all_gather | solution.py:175
  41.8 4.4 %gather_fusion = f32[512,32,64]{2,1,0:T(8,128)} fusion(f32[64,32,64]{2,1,0:T(8,128)S(1)} %all_gather.7, s32[1024]{0:T(1024)S(1)} %pad_clamp_fusion), kind=kCustom, calls=%fused_computation | custom fusion | bytes 8390656 | tf_op jit(solution)/shard_map/gather | solution.py:178
  46.2 0.0 copy-start.8
  46.2 6.8 %copy.22 = f32[16,1024,64]{1,2,0:T(8,128)} copy(f32[16,1024,64]{2,1,0:T(8,128)} %bitcast.24) | data formatting | bytes 8388608 | tf_op jit(solution)/shard_map/gather | solution.py:178
  52.9 0.0 copy-done.8
  52.9 0.1 mul.18
  53.1 0.1 mul.19
  53.2 0.0 copy-done
  53.2 0.0 copy-start.4
  53.2 5.7 %fusion.3 = f32[16,64,32,1]{1,2,3,0:T(8,128)S(1)} fusion(f32[16,32,1024]{2,1,0:T(8,128)S(1)} %copy-done, f32[16,1024,64]{1,2,0:T(8,128)} %copy.22, f32[16,1024]{1,0:T(8,128)S(1)} %mul.19), kind=kOutput, calls=%fused_computation.5 | convolution fusion | flops 403701760 | bytes 6488064 | tf_op jit(solution)/shard_map/dot_general | solution.py:146
  59.0 0.0 copy-done.4
  59.0 1.8 %fusion.13 = f32[16,64,8,32]{1,3,2,0:T(8,128)S(1)} fusion(f32[16,64,32,1]{1,2,3,0:T(8,128)S(1)} %fusion.3, f32[16,8,32,32]{3,2,1,0:T(8,128)S(1)} %copy-done.4), kind=kOutput, calls=%fused_computation.30 | convolution fusion | flops 100663296 | bytes 1703936 | tf_op jit(solution)/shard_map/pcab,pbv->pcav/dot_general | solution.py:180
  60.8 3.2 %copy.28 = f32[64,2,32,64]{3,1,2,0:T(2,128)} copy(f32[64,2,32,64]{3,2,1,0:T(8,128)S(1)} %bitcast.26) | data formatting | bytes 2097152 | tf_op jit(solution)/shard_map/reshape | solution.py:181
  64.0 0.0 copy-start.9
  64.0 0.0 copy-start.6
  64.0 3.4 %reshape.70.down_ref = f32[64,32,128]{2,1,0:T(8,128)} reshape(f32[64,32,2,64]{3,2,1,0:T(2,128)} %bitcast.27) | data formatting | bytes 2097152 | tf_op jit(solution)/shard_map/reshape | solution.py:181
  67.4 0.0 copy-done.9
  67.4 0.1 copy.18
  67.5 0.7 reshape.63.where_ref
  68.2 0.0 copy-done.6
  68.2 0.1 copy.19
  68.3 0.7 reshape.64.mask_ref
  68.9 61.6 %all-gather.2.cloned.1.call-done.group_ref = f32[4096,16,128]{2,1,0:T(8,128)} async-done(((f32[128,16,128]{2,1,0:T(8,128)}), f32[4096,16,128]{2,1,0:T(8,128)}) %all-gather.2.cloned.1.call-update) | async-done | bytes 33554448 | tf_op jit(solution)/shard_map/all_gather | solution.py:170
  130.5 0.0 copy-start.1
  130.5 39.2 %leaf_field_product.1 = f32[64,8192]{1,0:T(8,128)} custom-call(s32[2048]{0:T(1024)} %reshape.63.where_ref, s32[2048]{0:T(1024)} %reshape.64.mask_ref, f32[4096,16,128]{2,1,0:T(8,128)} %all-gather.2.cloned.1.call-done.group_ref, f32[128,32,512]{2,1,0:T(8,128)} %coupling_ref.1, f32[64,32,128]{2,1,0:T(8,128)} %reshape.70.down_ref, f32[32,8192]{1,0:T(8,128)} %basis_ref.3), custom_call_target="tpu_custom_call" | custom-call | tf_op jit(solution)/shard_map/leaf_field_product/pallas_call | solution.py:124
  169.7 0.0 copy-done.1
  (5 shorter events, 0.0 us)
Async XLA Ops:
  6.5 46.7 %copy-start = (f32[16,32,1024]{2,1,0:T(8,128)S(1)}, f32[16,32,1024]{2,1,0:T(8,128)}, u32[]{:S(2)}) copy-start(f32[16,32,1024]{2,1,0:T(8,128)} %param.15) | copy-start | bytes 6291460
  6.5 124.0 %all-gather.2.cloned.1.call-start = ((), (), s32[]{:S(2)}) async-start(), calls=%async_computation | async-start | bytes 34603008 | tf_op jit(solution)/shard_map/all_gather | solution.py:170
  6.5 1.4 copy-start.2
  7.9 1.6 copy-start.3
  16.1 3.2 %copy-start.5 = (f32[128,1024]{1,0:T(8,128)S(1)}, f32[128,1024]{1,0:T(8,128)}, u32[]{:S(2)}) copy-start(f32[128,1024]{1,0:T(8,128)} %param.11) | copy-start | bytes 1572868
  19.4 2.0 %copy-start.7 = (s32[16,32]{1,0:T(8,128)S(1)}, s32[16,32]{1,0:T(8,128)}, u32[]{:S(2)}) copy-start(s32[16,32]{1,0:T(8,128)} %param.16) | copy-start | bytes 6148
  46.2 6.8 %copy-start.8 = (s32[16,32]{1,0:T(8,128)S(1)}, s32[16,32]{1,0:T(8,128)}, u32[]{:S(2)}) copy-start(s32[16,32]{1,0:T(8,128)} %param.17) | copy-start | bytes 6148
  53.2 5.7 %copy-start.4 = (f32[16,8,32,32]{3,2,1,0:T(8,128)S(1)}, f32[16,8,32,32]{3,2,1,0:T(8,128)}, u32[]{:S(2)}) copy-start(f32[16,8,32,32]{3,2,1,0:T(8,128)} %reshape.67) | copy-start | bytes 1572868
  64.0 3.4 %copy-start.9 = (s32[128,16]{0,1:T(8,128)S(1)}, s32[128,16]{0,1:T(8,128)}, u32[]{:S(2)}) copy-start(s32[128,16]{0,1:T(8,128)} %param.13) | copy-start | bytes 24580
  64.0 4.2 %copy-start.6 = (s32[128,16]{0,1:T(8,128)S(1)}, s32[128,16]{0,1:T(8,128)}, u32[]{:S(2)}) copy-start(s32[128,16]{0,1:T(8,128)} %param.14) | copy-start | bytes 24580
  130.5 39.2 %copy-start.1 = (f32[16,32,1024]{2,1,0:T(8,128)S(1)}, f32[16,32,1024]{2,1,0:T(8,128)}, u32[]{:S(2)}) copy-start(f32[16,32,1024]{2,1,0:T(8,128)} %param.15) | copy-start | bytes 6291460
Sparse Core Ops, SparseCore 0:
  12.9 117.5 all-gather.1
where the time goes:
time: 177 us
  waiting for transfers between devices  61.6 us (35%)
  Pallas kernels  42.5 us (24%)
  local copies, waits for them, and re-layouts  31.2 us (18%)
  blocking collectives  14.6 us (8%)
  between operations  13.5 us (8%)
  matrix products  13.2 us (7%)
    all_gather x1, waiting for transfers between devices, per_device(): group_all = lax.all_gather(coef, 'subtree', axis=0, tiled=True)  61.6 us
    pallas_call x1, Pallas kernels, products(): pl.pallas_call(functools.partial(field_kernel, slots), out_shape=jax.Shap...  39.2 us
    all_gather x1, blocking collectives, per_device(): parent_all = lax.all_gather(parent_coef, 'branch', axis=0, tiled=True)  14.6 us
    gather x2, local copies, waits for them, and re-layouts, per_device(): parent_picked = parent_all[position.reshape(-1)]  11.1 us
    reshape x2, local copies, waits for them, and re-layouts, per_device(): downward.reshape(leaf_count // 2, 2, K, NV).transpose(0, 2, 1, 3)  6.57 us
    dot_general x1, matrix products, per_device(): jnp.einsum('pcab,pcav->pbv', transfers, natural, precision=HIGHEST)  5.72 us
    dot_general x1, matrix products, coupled(): lax.dot_general(coupling, stacked, (((2,), (1,)), ((0,), (0,))), precisio...  5.71 us
  transfers between devices with their start and end apart: 1, of which 1 were waited for; matrix products, arithmetic and copies ran while one was open for 23% of the time, Pallas kernels for 0%

commit v1 on v0

v1 whole, which is shorter than its diff:
```python
import functools

import jax
import jax.numpy as jnp
from jax import lax
from jax.experimental import pallas as pl
from jax.experimental.pallas import tpu as pltpu
from jax.sharding import PartitionSpec as P

PTS = 64
K = 32
NV = 64
CHILD = 8
ROWS = 8
TILE = 16
LANES = 2 * NV
CAP = 64
VMEM_LIMIT = 60 * 2**20
BRIEF = pl.CostEstimate(flops=0, bytes_accessed=0, transcendentals=0)
BRANCHES = 4

def split(x):
    high = x.astype(jnp.bfloat16)
    low = (x - high.astype(jnp.float32)).astype(jnp.bfloat16)
    return high, low


def left_lanes(rows):
    return lax.broadcasted_iota(jnp.int32, (rows, LANES), 1) < NV


def coef_kernel(basis_ref, vectors_ref, coef_ref, pair_ref):
    left_v = left_lanes(NV)
    left_r = left_lanes(ROWS)
    for pair in range(basis_ref.shape[1] // LANES):
        lanes = slice(pair * LANES, (pair + 1) * LANES)
        basis_high, basis_low = split(basis_ref[:, lanes])
        vec_high, vec_low = split(vectors_ref[:, lanes])
        zero = jnp.zeros_like(vec_high)
        weights = jnp.concatenate(
            [
                jnp.where(left_v, vec_high, zero),
                jnp.where(left_v, zero, vec_high),
                jnp.where(left_v, vec_low, zero),
                jnp.where(left_v, zero, vec_low),
            ],
            axis=0,
        )
        both = lax.dot_general(
            jnp.concatenate([basis_high, basis_low], axis=0),
            weights,
            (((1,), (1,)), ((), ())),
            preferred_element_type=jnp.float32,
        )
        summed = both[:K, :LANES] + (both[:K, LANES:] + both[K:, :LANES])
        pair_ref[pair] = summed
        for half in (0, 1):
            first = summed[half * TILE : half * TILE + ROWS]
            second = summed[half * TILE + ROWS : (half + 1) * TILE]
            rows = slice(half * ROWS, (half + 1) * ROWS)
            coef_ref[2 * pair, rows] = jnp.where(left_r, first, pltpu.roll(second, NV, 1))
            coef_ref[2 * pair + 1, rows] = jnp.where(left_r, pltpu.roll(first, NV, 1), second)


def leaf_coefs(basis, vectors, block):
    leaves = basis.shape[1] // PTS
    return pl.pallas_call(
        coef_kernel,
        out_shape=(
            jax.ShapeDtypeStruct((leaves, TILE, LANES), jnp.float32),
            jax.ShapeDtypeStruct((leaves // 2, K, LANES), jnp.float32),
        ),
        grid=(leaves // block,),
        in_specs=[
            pl.BlockSpec((K, block * PTS), lambda i: (0, i)),
            pl.BlockSpec((NV, block * PTS), lambda i: (0, i)),
        ],
        out_specs=(
            pl.BlockSpec((block, TILE, LANES), lambda i: (i, 0, 0)),
            pl.BlockSpec((block // 2, K, LANES), lambda i: (i, 0, 0)),
        ),
        compiler_params=pltpu.CompilerParams(vmem_limit_bytes=VMEM_LIMIT),
        name="leaf_coef",
    )(basis, vectors)


def pick_slot(x, live, left_r):
    x = x * live.astype(jnp.float32)
    high = x.astype(jnp.bfloat16).astype(jnp.float32)
    low = pltpu.roll(x - high, NV, 1)
    return jnp.concatenate([jnp.where(left_r, high, low), jnp.where(left_r, low, high)], axis=0).astype(jnp.bfloat16)


DEPTH = 8
UNROLL = 64


def field_kernel(slots, block, pos_ref, val_ref, group_ref, coupling_ref, down_ref, basis_ref, out_ref, tiles, buf, sem):
    step = pl.program_id(0)
    first = step * block
    left_k, left_r, left_v = left_lanes(K), left_lanes(ROWS), left_lanes(NV)

    @pl.when(step == 0)
    def _():
        leaves = buf.shape[1]
        devices = group_ref.shape[0] // leaves

        def chunk(device):
            at = pl.multiple_of(device * leaves, leaves)
            return pltpu.make_async_copy(
                group_ref.at[pl.ds(at, leaves)], buf.at[lax.rem(device, DEPTH)], sem.at[lax.rem(device, DEPTH)]
            )

        for device in range(DEPTH - 1):
            chunk(device).start()

        @pl.loop(0, devices)
        def _(device):
            @pl.when(device + DEPTH - 1 < devices)
            def _():
                chunk(device + DEPTH - 1).start()

            chunk(device).wait()

            @pl.loop(0, CAP // UNROLL)
            def _(part):
                for n in range(UNROLL):
                    entry = device * CAP + part * UNROLL + n
                    code = val_ref[device, part * UNROLL + n]
                    both = buf[lax.rem(device, DEPTH), code >> 1]
                    tiles[entry, :TILE] = pick_slot(both[:ROWS], code & 1, left_r)
                    tiles[entry, TILE:] = pick_slot(both[ROWS:], code & 1, left_r)

    def leaf_field(leaf):
        parts = [tiles[pos_ref[first + leaf, slot]] for slot in range(slots)]
        both = jnp.dot(
            jnp.concatenate(split(coupling_ref[leaf]), axis=0),
            jnp.concatenate(parts, axis=0),
            preferred_element_type=jnp.float32,
        )
        summed = both[:K] + both[K:]
        return summed + pltpu.roll(summed, NV, 1)

    def pair_total(pair):
        return jnp.where(left_k, leaf_field(2 * pair), leaf_field(2 * pair + 1)) + down_ref[pair]

    def diagonal(x):
        rows = []
        for g in range(4):
            row = [x[:, n * LANES : (n + 1) * LANES] if n == g else jnp.zeros((K, LANES), x.dtype) for n in range(4)]
            rows.append(jnp.concatenate(row, axis=1))
        return jnp.concatenate(rows, axis=0)

    @pl.loop(0, block // 8)
    def _(quad):
        total = jnp.concatenate([pair_total(4 * quad + n) for n in range(4)], axis=0)
        high, low = split(total.T)
        at = pl.multiple_of(quad * 4 * LANES, 4 * LANES)
        basis_high, basis_low = split(basis_ref[:, pl.ds(at, 4 * LANES)])
        spread = diagonal(basis_high)
        both = jnp.dot(
            jnp.concatenate([high, low], axis=1),
            jnp.concatenate([spread, spread], axis=0),
            preferred_element_type=jnp.float32,
        )
        both += jnp.dot(high, diagonal(basis_low), preferred_element_type=jnp.float32)
        for n in range(4):
            square = both[:, n * LANES : (n + 1) * LANES]
            out_ref[:, pl.ds(pl.multiple_of(at + n * LANES, LANES), LANES)] = jnp.where(
                left_v, square[:NV], square[NV:]
            )


def products(pos, codes, group, coupling, down, basis, block):
    leaves, _, width = coupling.shape
    slots = width // K
    smem = pl.BlockSpec(memory_space=pltpu.SMEM)
    return pl.pallas_call(
        functools.partial(field_kernel, slots, block),
        out_shape=jax.ShapeDtypeStruct((NV, leaves * PTS), jnp.float32),
        grid=(leaves // block,),
        in_specs=[
            smem,
            smem,
            pl.BlockSpec(memory_space=pl.ANY),
            pl.BlockSpec((block, K, width), lambda i: (i, 0, 0)),
            pl.BlockSpec((block // 2, K, LANES), lambda i: (i, 0, 0)),
            pl.BlockSpec((K, block * PTS), lambda i: (0, i)),
        ],
        out_specs=pl.BlockSpec((NV, block * PTS), lambda i: (0, i)),
        scratch_shapes=[
            pltpu.VMEM((leaves * slots, K, LANES), jnp.bfloat16),
            pltpu.VMEM((DEPTH, leaves, TILE, LANES), jnp.float32),
            pltpu.SemaphoreType.DMA((DEPTH,)),
        ],
        compiler_params=pltpu.CompilerParams(vmem_limit_bytes=VMEM_LIMIT),
        name="leaf_field_product",
    )(pos, codes, group, coupling, down, basis)


def order_kernel(list_ref, mask_ref, pos_ref, code_ref):
    leaves, slots = list_ref.shape
    devices = code_ref.shape[0]
    names = list_ref[...]
    owner = lax.rem(names // leaves, devices)
    code = (lax.rem(names, leaves) * 2 + mask_ref[...]).astype(jnp.float32)
    row = lax.broadcasted_iota(jnp.int32, (leaves, LANES), 0)
    lane = lax.broadcasted_iota(jnp.int32, (leaves, LANES), 1)
    below = (row > lane).astype(jnp.bfloat16)
    used = jnp.zeros((1, LANES), jnp.float32)
    sorted_codes = jnp.zeros((LANES, LANES), jnp.float32)
    places = jnp.zeros((leaves, LANES), jnp.float32)
    for slot in range(slots):
        named = (owner[:, slot : slot + 1] == lane).astype(jnp.float32)
        before = jnp.dot(below, named.astype(jnp.bfloat16), preferred_element_type=jnp.float32) + used
        used = used + jnp.sum(named, axis=0, keepdims=True)
        index = jnp.sum(named * before, axis=1, keepdims=True)
        rank = jnp.sum(named * lane.astype(jnp.float32), axis=1, keepdims=True)
        places = jnp.where(lane == slot, rank * CAP + index, places)
        spread = (lane.astype(jnp.float32) == index).astype(jnp.bfloat16)
        sorted_codes = sorted_codes + lax.dot_general(
            (named * code[:, slot : slot + 1]).astype(jnp.bfloat16),
            spread,
            (((0,), (0,)), ((), ())),
            preferred_element_type=jnp.float32,
        )
    pos_ref[...] = places[:, :slots].astype(jnp.int32)
    code_ref[...] = sorted_codes[:devices].astype(jnp.int32)


def slot_order(leaf_list, leaf_mask, devices):
    return pl.pallas_call(
        order_kernel,
        out_shape=(
            jax.ShapeDtypeStruct(leaf_list.shape, jnp.int32),
            jax.ShapeDtypeStruct((devices, LANES), jnp.int32),
        ),
        compiler_params=pltpu.CompilerParams(vmem_limit_bytes=VMEM_LIMIT),
        cost_estimate=BRIEF,
        name="slot_order",
    )(leaf_list, leaf_mask)


def parent_coef_kernel(pair_ref, transfer_ref, out_ref):
    left_r = left_lanes(ROWS)
    for parent in range(out_ref.shape[0]):
        blocks = []
        for leaf in range(CHILD):
            pair = parent * CHILD // 2 + leaf // 2
            x = [pair_ref[pair, pl.ds(a4, ROWS, stride=4), :] for a4 in range(4)]
            if leaf % 2 == 0:
                tiles = [jnp.where(left_r, x[n], pltpu.roll(x[n + 1], NV, 1)) for n in (0, 2)]
            else:
                tiles = [jnp.where(left_r, pltpu.roll(x[n], NV, 1), x[n + 1]) for n in (0, 2)]
            blocks.append(jnp.concatenate(tiles, axis=1))
        coef_high, coef_low = split(jnp.concatenate(blocks, axis=0))
        rows = CHILD * ROWS
        high, low = split(transfer_ref[parent * rows : (parent + 1) * rows])
        full = lax.dot_general(
            jnp.concatenate([high, low, high], axis=0),
            jnp.concatenate([coef_high, coef_high, coef_low], axis=0),
            (((0,), (0,)), ((), ())),
            preferred_element_type=jnp.float32,
        )
        even = full[:K, :LANES] + full[2 * K : 3 * K, LANES:]
        odd = full[K : 2 * K, :LANES] + full[3 * K :, LANES:]
        total = even + pltpu.roll(odd, NV, 1)
        for half in (0, 1):
            first = total[half * TILE : half * TILE + ROWS]
            second = total[half * TILE + ROWS : (half + 1) * TILE]
            out_ref[parent, half * ROWS : (half + 1) * ROWS] = jnp.where(left_r, first, pltpu.roll(second, NV, 1))


def parent_coefs(coef_pairs, rows):
    parents = coef_pairs.shape[0] * 2 // CHILD
    return pl.pallas_call(
        parent_coef_kernel,
        out_shape=jax.ShapeDtypeStruct((parents, TILE, LANES), jnp.float32),
        compiler_params=pltpu.CompilerParams(vmem_limit_bytes=VMEM_LIMIT),
        cost_estimate=BRIEF,
        name="parent_coef",
    )(coef_pairs, rows)


def parent_field_kernel(group, list_ref, mask_ref, branch_ref, *refs):
    coef_refs, (coupling_ref, transfer_ref, down_ref, coef_ref) = refs[:BRANCHES], refs[BRANCHES:]
    parents = coef_ref.shape[0] // BRANCHES
    slots = list_ref.shape[1]
    parent = pl.program_id(0)
    left_k, left_r = left_lanes(K), left_lanes(ROWS)

    @pl.when(parent == 0)
    def _():
        for number, ref in enumerate(coef_refs):
            coef_ref[number * parents : (number + 1) * parents] = ref[...]

    parts = []
    for slot in range(slots):
        name = list_ref[parent, slot]
        at = lax.rem(name // group - branch_ref[0] + BRANCHES, BRANCHES) * parents + lax.rem(name, parents)
        both = coef_ref[at]
        live = mask_ref[parent, slot]
        parts += [pick_slot(both[:ROWS], live, left_r), pick_slot(both[ROWS:], live, left_r)]
    both = jnp.dot(
        jnp.concatenate(split(coupling_ref[0]), axis=0),
        jnp.concatenate(parts, axis=0),
        preferred_element_type=jnp.float32,
    )
    summed = both[:K] + both[K:]
    field = summed + pltpu.roll(summed, NV, 1)
    zero = jnp.zeros_like(field)
    left, right = jnp.where(left_k, field, zero), jnp.where(left_k, zero, field)
    spread = jnp.concatenate(
        [
            jnp.concatenate([left, right, zero, zero], axis=0),
            jnp.concatenate([zero, zero, left, right], axis=0),
        ],
        axis=1,
    )
    spread_high, spread_low = split(spread)
    high, low = split(transfer_ref[...])
    full = jnp.dot(
        jnp.concatenate([high, low, high], axis=1),
        jnp.concatenate([spread_high, spread_high, spread_low], axis=0),
        preferred_element_type=jnp.float32,
    )
    for pair in range(CHILD // 2):
        for a4 in range(4):
            lanes = slice(a4 // 2 * LANES, (a4 // 2 + 1) * LANES)
            even = full[2 * pair * ROWS : (2 * pair + 1) * ROWS, lanes]
            odd = full[(2 * pair + 1) * ROWS : (2 * pair + 2) * ROWS, lanes]
            if a4 % 2 == 0:
                odd = pltpu.roll(odd, NV, 1)
            else:
                even = pltpu.roll(even, NV, 1)
            down_ref[pair, pl.ds(a4, ROWS, stride=4), :] = jnp.where(left_r, even, odd)


def downward_pairs(parent_list, parent_mask, branch, group, coef_all, coupling, rows):
    parents, _, width = coupling.shape
    smem = pl.BlockSpec(memory_space=pltpu.SMEM)
    return pl.pallas_call(
        functools.partial(parent_field_kernel, group),
        out_shape=jax.ShapeDtypeStruct((parents * CHILD // 2, K, LANES), jnp.float32),
        grid=(parents,),
        in_specs=[
            smem,
            smem,
            smem,
        ]
        + [pl.BlockSpec(memory_space=pltpu.VMEM)] * BRANCHES
        + [
            pl.BlockSpec((1, K, width), lambda i: (i, 0, 0)),
            pl.BlockSpec((CHILD * ROWS, LANES), lambda i: (i, 0)),
        ],
        out_specs=pl.BlockSpec((CHILD // 2, K, LANES), lambda i: (i, 0, 0)),
        scratch_shapes=[pltpu.VMEM((BRANCHES * parents, TILE, LANES), jnp.float32)],
        compiler_params=pltpu.CompilerParams(vmem_limit_bytes=VMEM_LIMIT),
        cost_estimate=BRIEF,
        name="parent_field",
    )(parent_list, parent_mask, branch, *coef_all, coupling, rows)


def per_device(
    vectors,
    basis,
    transfer,
    leaf_coupling,
    leaf_list,
    leaf_mask,
    parent_coupling,
    parent_list,
    parent_mask,
):
    leaf_count = leaf_list.shape[0]
    parent_count = parent_list.shape[0]
    subtrees = lax.axis_size("subtree")
    branches = lax.axis_size("branch")

    coef, coef_pairs = leaf_coefs(basis, vectors, 32)
    group = lax.all_gather(coef, "subtree", axis=0, tiled=True)
    pos, codes = slot_order(leaf_list, leaf_mask, subtrees)

    rows = transfer.reshape(parent_count * CHILD * ROWS, LANES)
    branch = lax.axis_index("branch").astype(jnp.int32)[None]
    parent_coef = parent_coefs(coef_pairs, rows)
    coef_all = [parent_coef] + [
        lax.ppermute(parent_coef, "branch", [(i, (i - by) % branches) for i in range(branches)])
        for by in range(1, branches)
    ]
    down = downward_pairs(parent_list, parent_mask, branch, parent_count * subtrees, coef_all, parent_coupling, rows)
    return products(pos, codes, group, leaf_coupling, down, basis, 32)


def solution(mesh):
    return jax.shard_map(
        per_device,
        mesh=mesh,
        in_specs=(
            P(None, ("branch", "subtree")),
            P(None, ("branch", "subtree")),
            P(("branch", "subtree"), None),
            P(("branch", "subtree"), None, None),
            P(("branch", "subtree"), None),
            P(("branch", "subtree"), None),
            P(("branch", "subtree"), None, None),
            P(("branch", "subtree"), None),
            P(("branch", "subtree"), None),
        ),
        out_specs=P(None, ("branch", "subtree")),
        check_vma=False,
    )
```

time: 177 us -> 161 us (0.910)
  local copies, waits for them, and re-layouts: 31.2 us -> 3.06 us
  waiting for transfers between devices: 61.6 us -> 82.4 us
  blocking collectives: 14.6 us -> 0 us
  Pallas kernels: 42.5 us -> 56 us
  matrix products: 13.2 us -> 0 us
  starting transfers between devices: 0.01 us -> 5.65 us
    all_gather x1, waiting for transfers between devices: 61.6 us -> 82.4 us  [per_device(): group = lax.all_gather(coef, 'subtree', axis=0, tiled=True)]
    all_gather x1 -> x0, blocking collectives: 14.6 us -> none  [per_device(): parent_all = lax.all_gather(parent_coef, 'branch', axis=0, tiled=True)]
    pallas_call x2 -> x5, Pallas kernels: 42.5 us -> 56 us  [the longest x1 24.5 us: products(): pl.pallas_call(functools.partial(field_kernel, slots, block), out_shape=j...]
    dot_general x3 -> x0, matrix products: 13.2 us -> none  [the longest x1 5.72 us: per_device(): jnp.einsum('pcab,pcav->pbv', transfers, natural, precision=HIGHEST)]
    reshape x7 -> x1, local copies, waits for them, and re-layouts: 13.4 us -> 0.91 us  [per_device(): rows = transfer.reshape(parent_count * CHILD * ROWS, LANES)]
    gather x2 -> x0, local copies, waits for them, and re-layouts: 11.1 us -> none  [per_device(): parent_picked = parent_all[position.reshape(-1)]]
    ppermute x0 -> x3, starting transfers between devices: none -> 5.64 us  [per_device(): lax.ppermute(parent_coef, 'branch', [(i, (i - by) % branches) for i in ra...]
    transpose x1 -> x0, local copies, waits for them, and re-layouts: 3.21 us -> none  [per_device(): coef.reshape(parent_count, CHILD, HALF, 2, NV).transpose(0, 1, 3, 2, 4)]
  transfers between devices with their start and end apart: 1 -> 4, of which waited for: 1 -> 1; matrix products, arithmetic and copies ran while one was open for 23% -> 1% of each run, Pallas kernels for 0% -> 17%
where the time goes in v1:
time: 161 us
  waiting for transfers between devices  82.4 us (51%)
  Pallas kernels  56 us (35%)
  between operations  13.5 us (8%)
  starting transfers between devices  5.65 us (4%)
  local copies, waits for them, and re-layouts  3.06 us (2%)
    all_gather x1, waiting for transfers between devices, per_device(): group = lax.all_gather(coef, 'subtree', axis=0, tiled=True)  82.4 us
    pallas_call x1, Pallas kernels, products(): pl.pallas_call(functools.partial(field_kernel, slots, block), out_shape=j...  24.5 us
    pallas_call x1, Pallas kernels, downward_pairs(): pl.pallas_call(functools.partial(parent_field_kernel, group), out_shape=j...  16.2 us
    pallas_call x1, Pallas kernels, slot_order(): pl.pallas_call(order_kernel, out_shape=(jax.ShapeDtypeStruct(leaf_list.sh...  5.93 us
    ppermute x3, starting transfers between devices, per_device(): lax.ppermute(parent_coef, 'branch', [(i, (i - by) % branches) for i in ra...  5.64 us
    pallas_call x1, Pallas kernels, leaf_coefs(): pl.pallas_call(coef_kernel, out_shape=(jax.ShapeDtypeStruct((leaves, TILE...  4.91 us
    pallas_call x1, Pallas kernels, parent_coefs(): pl.pallas_call(parent_coef_kernel, out_shape=jax.ShapeDtypeStruct((parent...  4.45 us
  transfers between devices with their start and end apart: 4, of which 1 were waited for; matrix products, arithmetic and copies ran while one was open for 1% of the time, Pallas kernels for 17%

profile of v1, /device:TPU:1, one launch (start us, length us, event | category | flops | bytes accessed | tf_op | source)
XLA Modules:
  0.0 160.6 jit_solution(6503323424716130398)
XLA Ops:
  6.5 0.0 copy-start
  6.5 0.0 all-gather.2.cloned.1.call-start
  6.5 4.9 %leaf_coef.1 = (f32[128,16,128]{2,1,0:T(8,128)}, f32[64,32,128]{2,1,0:T(8,128)}) custom-call(f32[32,8192]{1,0:T(8,128)} %basis_ref.3, f32[64,8192]{1,0:T(8,128)} %vectors_ref.1), custom_call_target="tpu_custom_call" | custom-call | tf_op jit(solution)/shard_map/leaf_coef/pallas_call | solution.py:67
  11.5 0.0 copy-start.4
  11.5 0.0 copy-start.5
  11.5 0.0 all-gather.2.cloned.1.call-update
  11.5 0.0 copy-done
  11.5 0.9 reshape.3.transfer_ref.refs_5_
  12.4 4.5 %parent_coef.1.refs_0_ = f32[16,16,128]{2,1,0:T(8,128)} custom-call(f32[64,32,128]{2,1,0:T(8,128)} %get-tuple-element.12.pair_ref, f32[1024,128]{1,0:T(8,128)} %reshape.3.transfer_ref.refs_5_), custom_call_target="tpu_custom_call" | custom-call | tf_op jit(solution)/shard_map/parent_coef/pallas_call | solution.py:276
  16.9 2.0 %collective-permute-start.2 = (f32[16,16,128]{2,1,0:T(8,128)}, f32[16,16,128]{2,1,0:T(8,128)S(1)}, u32[]{:S(2)}, u32[]{:S(2)}) collective-permute-start(f32[16,16,128]{2,1,0:T(8,128)} %parent_coef.1.refs_0_), channel_id=1, source_target_pairs={{0,32},{32,64},{64,96},{96,0},{1,33},{33,65},{65,97},{97,1},{2,34}... | collective-permute-start | bytes 393224 | tf_op jit(solution)/shard_map/ppermute | solution.py:388
  18.9 2.5 %collective-permute-start.1 = (f32[16,16,128]{2,1,0:T(8,128)}, f32[16,16,128]{2,1,0:T(8,128)S(1)}, u32[]{:S(2)}, u32[]{:S(2)}) collective-permute-start(f32[16,16,128]{2,1,0:T(8,128)} %parent_coef.1.refs_0_), channel_id=1, source_target_pairs={{0,64},{32,96},{64,0},{96,32},{1,65},{33,97},{65,1},{97,33},{2,66}... | collective-permute-start | bytes 393224 | tf_op jit(solution)/shard_map/ppermute | solution.py:388
  21.3 1.2 collective-permute-start
  22.5 0.0 copy-done.4
  22.5 0.7 copy.12.list_ref
  23.2 0.0 copy-done.5
  23.2 0.7 copy.13.mask_ref
  23.9 5.9 %slot_order.1 = (s32[128,16]{1,0:T(8,128)}, s32[32,128]{1,0:T(8,128)}) custom-call(s32[128,16]{1,0:T(8,128)} %copy.12.list_ref, s32[128,16]{1,0:T(8,128)} %copy.13.mask_ref), custom_call_target="tpu_custom_call" | custom-call | tf_op jit(solution)/shard_map/slot_order/pallas_call | solution.py:232
  29.9 0.0 collective-permute-done.2.refs_3_
  29.9 0.0 copy-start.1
  29.9 0.0 collective-permute-done.1.refs_2_
  29.9 0.0 copy-start.2
  29.9 0.0 collective-permute-done.refs_1_
  29.9 0.0 copy-start.3
  29.9 0.6 copy-done.1
  30.5 0.0 copy-done.2
  30.6 0.0 copy-done.3
  30.6 16.2 %parent_field.1.down_ref = f32[64,32,128]{2,1,0:T(8,128)} custom-call(s32[16,32]{1,0:T(8,128)} %list_ref.2, s32[16,32]{1,0:T(8,128)} %mask_ref.2, s32[1]{0:T(128)} %bitcast.branch_ref, f32[16,16,128]{2,1,0:T(8,128)} %parent_coef.1.refs_0_, f32[16,16,128]{2,1,0:T(8,128)} %copy-done.3, f32[16,16,128]{2,1,0:T(8,128)} %copy-done.2, f32[16,16,128]{2,1,0:T(8,128)} %copy-done.1, ...), custom_call_target="tpu_custom_call" | custom-call | tf_op jit(solution)/shard_map/parent_field/pallas_call | solution.py:342
  46.8 82.4 %all-gather.2.cloned.1.call-done.group_ref = f32[4096,16,128]{2,1,0:T(8,128)} async-done(((f32[128,16,128]{2,1,0:T(8,128)}), f32[4096,16,128]{2,1,0:T(8,128)}) %all-gather.2.cloned.1.call-update) | async-done | bytes 33554448 | tf_op jit(solution)/shard_map/all_gather | solution.py:381
  129.2 24.5 %leaf_field_product.1 = f32[64,8192]{1,0:T(8,128)} custom-call(s32[128,16]{1,0:T(8,128)} %get-tuple-element.9.pos_ref, s32[32,128]{1,0:T(8,128)} %get-tuple-element.10.val_ref, f32[4096,16,128]{2,1,0:T(8,128)} %all-gather.2.cloned.1.call-done.group_ref, f32[128,32,512]{2,1,0:T(8,128)} %coupling_ref.1, f32[64,32,128]{2,1,0:T(8,128)} %parent_field.1.down_ref, ...), custom_call_target="tpu_custom_call" | custom-call | tf_op jit(solution)/shard_map/leaf_field_product/pallas_call | solution.py:178
Async XLA Ops:
  6.5 5.0 %copy-start = (f32[128,1024]{1,0:T(8,128)S(1)}, f32[128,1024]{1,0:T(8,128)}, u32[]{:S(2)}) copy-start(f32[128,1024]{1,0:T(8,128)} %param.11) | copy-start | bytes 1572868
  6.5 122.7 %all-gather.2.cloned.1.call-start = ((), (), s32[]{:S(2)}) async-start(), calls=%async_computation | async-start | bytes 34603008 | tf_op jit(solution)/shard_map/all_gather | solution.py:381
  11.5 11.1 %copy-start.4 = (s32[128,16]{0,1:T(8,128)S(1)}, s32[128,16]{0,1:T(8,128)}, u32[]{:S(2)}) copy-start(s32[128,16]{0,1:T(8,128)} %param.13) | copy-start | bytes 24580
  11.5 11.8 %copy-start.5 = (s32[128,16]{0,1:T(8,128)S(1)}, s32[128,16]{0,1:T(8,128)}, u32[]{:S(2)}) copy-start(s32[128,16]{0,1:T(8,128)} %param.14) | copy-start | bytes 24580
  16.9 13.0 %collective-permute-start.2 = (f32[16,16,128]{2,1,0:T(8,128)}, f32[16,16,128]{2,1,0:T(8,128)S(1)}, u32[]{:S(2)}, u32[]{:S(2)}) collective-permute-start(f32[16,16,128]{2,1,0:T(8,128)} %parent_coef.1.refs_0_), channel_id=1, source_target_pairs={{0,32},{32,64},{64,96},{96,0},{1,33},{33,65},{65,97},{97,1},{2,34}... | collective-permute-start | bytes 393224 | tf_op jit(solution)/shard_map/ppermute | solution.py:388
  18.9 11.0 %collective-permute-start.1 = (f32[16,16,128]{2,1,0:T(8,128)}, f32[16,16,128]{2,1,0:T(8,128)S(1)}, u32[]{:S(2)}, u32[]{:S(2)}) collective-permute-start(f32[16,16,128]{2,1,0:T(8,128)} %parent_coef.1.refs_0_), channel_id=1, source_target_pairs={{0,64},{32,96},{64,0},{96,32},{1,65},{33,97},{65,1},{97,33},{2,66}... | collective-permute-start | bytes 393224 | tf_op jit(solution)/shard_map/ppermute | solution.py:388
  21.3 8.6 %collective-permute-start = (f32[16,16,128]{2,1,0:T(8,128)}, f32[16,16,128]{2,1,0:T(8,128)S(1)}, u32[]{:S(2)}, u32[]{:S(2)}) collective-permute-start(f32[16,16,128]{2,1,0:T(8,128)} %parent_coef.1.refs_0_), channel_id=1, source_target_pairs={{0,96},{32,0},{64,32},{96,64},{1,97},{33,1},{65,33},{97,65},{2,98}... | collective-permute-start | bytes 393224 | tf_op jit(solution)/shard_map/ppermute | solution.py:388
  29.9 0.7 copy-start.1
  29.9 0.7 copy-start.2
  29.9 0.7 copy-start.3
Sparse Core Ops, SparseCore 0:
  11.6 117.5 all-gather.1

commit v2 on v1

--- a/solution.py
+++ b/solution.py
@@ -30,36 +30,29 @@
 
 
 def coef_kernel(basis_ref, vectors_ref, coef_ref, pair_ref):
-    left_v = left_lanes(NV)
+    left_k = left_lanes(K)
     left_r = left_lanes(ROWS)
     for pair in range(basis_ref.shape[1] // LANES):
         lanes = slice(pair * LANES, (pair + 1) * LANES)
-        basis_high, basis_low = split(basis_ref[:, lanes])
-        vec_high, vec_low = split(vectors_ref[:, lanes])
-        zero = jnp.zeros_like(vec_high)
-        weights = jnp.concatenate(
-            [
-                jnp.where(left_v, vec_high, zero),
-                jnp.where(left_v, zero, vec_high),
-                jnp.where(left_v, vec_low, zero),
-                jnp.where(left_v, zero, vec_low),
-            ],
-            axis=0,
-        )
+        rows = []
+        for part in split(basis_ref[:, lanes]):
+            zero = jnp.zeros_like(part)
+            rows += [jnp.where(left_k, part, zero), jnp.where(left_k, zero, part)]
         both = lax.dot_general(
-            jnp.concatenate([basis_high, basis_low], axis=0),
-            weights,
+            jnp.concatenate(rows, axis=0),
+            jnp.concatenate(split(vectors_ref[:, lanes]), axis=0),
             (((1,), (1,)), ((), ())),
             preferred_element_type=jnp.float32,
         )
-        summed = both[:K, :LANES] + (both[:K, LANES:] + both[K:, :LANES])
-        pair_ref[pair] = summed
+        even, odd = both[:K] + both[2 * K : 3 * K], both[K : 2 * K] + both[3 * K :]
+        even, odd = even + pltpu.roll(even, NV, 1), odd + pltpu.roll(odd, NV, 1)
+        pair_ref[pair] = jnp.where(left_k, even, odd)
         for half in (0, 1):
-            first = summed[half * TILE : half * TILE + ROWS]
-            second = summed[half * TILE + ROWS : (half + 1) * TILE]
+            first = slice(half * TILE, half * TILE + ROWS)
+            second = slice(half * TILE + ROWS, (half + 1) * TILE)
             rows = slice(half * ROWS, (half + 1) * ROWS)
-            coef_ref[2 * pair, rows] = jnp.where(left_r, first, pltpu.roll(second, NV, 1))
-            coef_ref[2 * pair + 1, rows] = jnp.where(left_r, pltpu.roll(first, NV, 1), second)
+            coef_ref[2 * pair, rows] = jnp.where(left_r, even[first], even[second])
+            coef_ref[2 * pair + 1, rows] = jnp.where(left_r, odd[first], odd[second])
 
 
 def leaf_coefs(basis, vectors, block):
@@ -95,7 +88,7 @@
 UNROLL = 64
 
 
-def field_kernel(slots, block, pos_ref, val_ref, group_ref, coupling_ref, down_ref, basis_ref, out_ref, tiles, buf, sem):
+def field_kernel(slots, block, pos_ref, val_ref, group_ref, coupling_ref, down_ref, basis_ref, out_ref, tiles, buf, totals, sem):
     step = pl.program_id(0)
     first = step * block
     left_k, left_r, left_v = left_lanes(K), left_lanes(ROWS), left_lanes(NV)
@@ -151,9 +144,7 @@
             rows.append(jnp.concatenate(row, axis=1))
         return jnp.concatenate(rows, axis=0)
 
-    @pl.loop(0, block // 8)
-    def _(quad):
-        total = jnp.concatenate([pair_total(4 * quad + n) for n in range(4)], axis=0)
+    def product(quad, total):
         high, low = split(total.T)
         at = pl.multiple_of(quad * 4 * LANES, 4 * LANES)
         basis_high, basis_low = split(basis_ref[:, pl.ds(at, 4 * LANES)])
@@ -170,6 +161,26 @@
                 left_v, square[:NV], square[NV:]
             )
 
+    quads = block // 8
+    totals_first = step * quads
+
+    @pl.when(step == 0)
+    def _():
+        totals[...] = jnp.zeros_like(totals)
+
+    @pl.loop(0, quads // 2)
+    def _(turn):
+        for n in (0, 1):
+            quad = totals_first + 2 * turn + n
+            before = totals[1 - n]
+            for pair in range(4):
+                totals[n, pair * K : (pair + 1) * K] = pair_total(8 * turn + 4 * n + pair)
+            product(jnp.maximum(quad - 1, 0), before)
+
+    @pl.when(step == pl.num_programs(0) - 1)
+    def _():
+        product(totals_first + quads - 1, totals[1])
+
 
 def products(pos, codes, group, coupling, down, basis, block):
     leaves, _, width = coupling.shape
@@ -185,12 +196,13 @@
             pl.BlockSpec(memory_space=pl.ANY),
             pl.BlockSpec((block, K, width), lambda i: (i, 0, 0)),
             pl.BlockSpec((block // 2, K, LANES), lambda i: (i, 0, 0)),
-            pl.BlockSpec((K, block * PTS), lambda i: (0, i)),
+            pl.BlockSpec((K, leaves * PTS), lambda i: (0, 0)),
         ],
-        out_specs=pl.BlockSpec((NV, block * PTS), lambda i: (0, i)),
+        out_specs=pl.BlockSpec((NV, leaves * PTS), lambda i: (0, 0)),
         scratch_shapes=[
             pltpu.VMEM((leaves * slots, K, LANES), jnp.bfloat16),
             pltpu.VMEM((DEPTH, leaves, TILE, LANES), jnp.float32),
+            pltpu.VMEM((2, 4 * K, LANES), jnp.float32),
             pltpu.SemaphoreType.DMA((DEPTH,)),
         ],
         compiler_params=pltpu.CompilerParams(vmem_limit_bytes=VMEM_LIMIT),
@@ -377,7 +389,7 @@
     subtrees = lax.axis_size("subtree")
     branches = lax.axis_size("branch")
 
-    coef, coef_pairs = leaf_coefs(basis, vectors, 32)
+    coef, coef_pairs = leaf_coefs(basis, vectors, 64)
     group = lax.all_gather(coef, "subtree", axis=0, tiled=True)
     pos, codes = slot_order(leaf_list, leaf_mask, subtrees)
 

time: 161 us -> 157 us (0.975)
  Pallas kernels: 56 us -> 51.4 us
    pallas_call x1, Pallas kernels: 24.5 us -> 20.5 us  [products(): pl.pallas_call(functools.partial(field_kernel, slots, block), out_shape=j...]
  transfers between devices with their start and end apart: 4 -> 4, of which waited for: 1 -> 1; matrix products, arithmetic and copies ran while one was open for 1% -> 2% of each run, Pallas kernels for 17% -> 17%
where the time goes in v2:
time: 157 us; the launch traced here: 156 us
  waiting for transfers between devices  82.4 us (52%)
  Pallas kernels  51.4 us (33%)
  between operations  13.5 us (9%)
  starting transfers between devices  5.65 us (4%)
  local copies, waits for them, and re-layouts  3.06 us (2%)
    all_gather x1, waiting for transfers between devices, per_device(): group = lax.all_gather(coef, 'subtree', axis=0, tiled=True)  82.4 us
    pallas_call x1, Pallas kernels, products(): pl.pallas_call(functools.partial(field_kernel, slots, block), out_shape=j...  20.5 us
    pallas_call x1, Pallas kernels, downward_pairs(): pl.pallas_call(functools.partial(parent_field_kernel, group), out_shape=j...  16.2 us
    pallas_call x1, Pallas kernels, slot_order(): pl.pallas_call(order_kernel, out_shape=(jax.ShapeDtypeStruct(leaf_list.sh...  5.93 us
    ppermute x3, starting transfers between devices, per_device(): lax.ppermute(parent_coef, 'branch', [(i, (i - by) % branches) for i in ra...  5.64 us
    pallas_call x1, Pallas kernels, parent_coefs(): pl.pallas_call(parent_coef_kernel, out_shape=jax.ShapeDtypeStruct((parent...  4.45 us
    pallas_call x1, Pallas kernels, leaf_coefs(): pl.pallas_call(coef_kernel, out_shape=(jax.ShapeDtypeStruct((leaves, TILE...  4.3 us
  transfers between devices with their start and end apart: 4, of which 1 were waited for; matrix products, arithmetic and copies ran while one was open for 2% of the time, Pallas kernels for 17%

profile of v2, /device:TPU:1, one launch (start us, length us, event | category | flops | bytes accessed | tf_op | source)
XLA Modules:
  0.0 156.0 jit_solution(12134152003188923220)
XLA Ops:
  6.5 0.0 copy-start
  6.5 0.0 all-gather.2.cloned.1.call-start
  6.5 4.3 %leaf_coef.1 = (f32[128,16,128]{2,1,0:T(8,128)}, f32[64,32,128]{2,1,0:T(8,128)}) custom-call(f32[32,8192]{1,0:T(8,128)} %basis_ref.3, f32[64,8192]{1,0:T(8,128)} %vectors_ref.1), custom_call_target="tpu_custom_call" | custom-call | tf_op jit(solution)/shard_map/leaf_coef/pallas_call | solution.py:60
  10.8 0.0 copy-start.4
  10.8 0.0 copy-start.5
  10.8 0.0 all-gather.2.cloned.1.call-update
  10.9 0.0 copy-done
  10.9 0.9 reshape.3.transfer_ref.refs_5_
  11.8 4.5 %parent_coef.1.refs_0_ = f32[16,16,128]{2,1,0:T(8,128)} custom-call(f32[64,32,128]{2,1,0:T(8,128)} %get-tuple-element.12.pair_ref, f32[1024,128]{1,0:T(8,128)} %reshape.3.transfer_ref.refs_5_), custom_call_target="tpu_custom_call" | custom-call | tf_op jit(solution)/shard_map/parent_coef/pallas_call | solution.py:288
  16.2 2.1 %collective-permute-start.2 = (f32[16,16,128]{2,1,0:T(8,128)}, f32[16,16,128]{2,1,0:T(8,128)S(1)}, u32[]{:S(2)}, u32[]{:S(2)}) collective-permute-start(f32[16,16,128]{2,1,0:T(8,128)} %parent_coef.1.refs_0_), channel_id=1, source_target_pairs={{0,32},{32,64},{64,96},{96,0},{1,33},{33,65},{65,97},{97,1},{2,34}... | collective-permute-start | bytes 393224 | tf_op jit(solution)/shard_map/ppermute | solution.py:400
  18.3 2.4 %collective-permute-start.1 = (f32[16,16,128]{2,1,0:T(8,128)}, f32[16,16,128]{2,1,0:T(8,128)S(1)}, u32[]{:S(2)}, u32[]{:S(2)}) collective-permute-start(f32[16,16,128]{2,1,0:T(8,128)} %parent_coef.1.refs_0_), channel_id=1, source_target_pairs={{0,64},{32,96},{64,0},{96,32},{1,65},{33,97},{65,1},{97,33},{2,66}... | collective-permute-start | bytes 393224 | tf_op jit(solution)/shard_map/ppermute | solution.py:400
  20.7 1.2 collective-permute-start
  21.9 0.0 copy-done.4
  21.9 0.7 copy.12.list_ref
  22.6 0.0 copy-done.5
  22.6 0.7 copy.13.mask_ref
  23.3 5.9 %slot_order.1 = (s32[128,16]{1,0:T(8,128)}, s32[32,128]{1,0:T(8,128)}) custom-call(s32[128,16]{1,0:T(8,128)} %copy.12.list_ref, s32[128,16]{1,0:T(8,128)} %copy.13.mask_ref), custom_call_target="tpu_custom_call" | custom-call | tf_op jit(solution)/shard_map/slot_order/pallas_call | solution.py:244
  29.3 0.0 collective-permute-done.2.refs_3_
  29.3 0.0 copy-start.1
  29.3 0.0 collective-permute-done.1.refs_2_
  29.3 0.0 copy-start.2
  29.3 0.0 collective-permute-done.refs_1_
  29.3 0.0 copy-start.3
  29.3 0.6 copy-done.1
  29.9 0.0 copy-done.2
  30.0 0.0 copy-done.3
  30.0 16.2 %parent_field.1.down_ref = f32[64,32,128]{2,1,0:T(8,128)} custom-call(s32[16,32]{1,0:T(8,128)} %list_ref.2, s32[16,32]{1,0:T(8,128)} %mask_ref.2, s32[1]{0:T(128)} %bitcast.branch_ref, f32[16,16,128]{2,1,0:T(8,128)} %parent_coef.1.refs_0_, f32[16,16,128]{2,1,0:T(8,128)} %copy-done.3, f32[16,16,128]{2,1,0:T(8,128)} %copy-done.2, f32[16,16,128]{2,1,0:T(8,128)} %copy-done.1, ...), custom_call_target="tpu_custom_call" | custom-call | tf_op jit(solution)/shard_map/parent_field/pallas_call | solution.py:354
  46.2 82.4 %all-gather.2.cloned.1.call-done.group_ref = f32[4096,16,128]{2,1,0:T(8,128)} async-done(((f32[128,16,128]{2,1,0:T(8,128)}), f32[4096,16,128]{2,1,0:T(8,128)}) %all-gather.2.cloned.1.call-update) | async-done | bytes 33554448 | tf_op jit(solution)/shard_map/all_gather | solution.py:393
  128.6 20.5 %leaf_field_product.1 = f32[64,8192]{1,0:T(8,128)} custom-call(s32[128,16]{1,0:T(8,128)} %get-tuple-element.9.pos_ref, s32[32,128]{1,0:T(8,128)} %get-tuple-element.10.val_ref, f32[4096,16,128]{2,1,0:T(8,128)} %all-gather.2.cloned.1.call-done.group_ref, f32[128,32,512]{2,1,0:T(8,128)} %coupling_ref.1, f32[64,32,128]{2,1,0:T(8,128)} %parent_field.1.down_ref, ...), custom_call_target="tpu_custom_call" | custom-call | tf_op jit(solution)/shard_map/leaf_field_product/pallas_call | solution.py:189
Async XLA Ops:
  6.5 4.3 %copy-start = (f32[128,1024]{1,0:T(8,128)S(1)}, f32[128,1024]{1,0:T(8,128)}, u32[]{:S(2)}) copy-start(f32[128,1024]{1,0:T(8,128)} %param.11) | copy-start | bytes 1572868
  6.5 122.1 %all-gather.2.cloned.1.call-start = ((), (), s32[]{:S(2)}) async-start(), calls=%async_computation | async-start | bytes 34603008 | tf_op jit(solution)/shard_map/all_gather | solution.py:393
  10.8 11.0 %copy-start.4 = (s32[128,16]{0,1:T(8,128)S(1)}, s32[128,16]{0,1:T(8,128)}, u32[]{:S(2)}) copy-start(s32[128,16]{0,1:T(8,128)} %param.13) | copy-start | bytes 24580
  10.8 11.8 %copy-start.5 = (s32[128,16]{0,1:T(8,128)S(1)}, s32[128,16]{0,1:T(8,128)}, u32[]{:S(2)}) copy-start(s32[128,16]{0,1:T(8,128)} %param.14) | copy-start | bytes 24580
  16.2 13.0 %collective-permute-start.2 = (f32[16,16,128]{2,1,0:T(8,128)}, f32[16,16,128]{2,1,0:T(8,128)S(1)}, u32[]{:S(2)}, u32[]{:S(2)}) collective-permute-start(f32[16,16,128]{2,1,0:T(8,128)} %parent_coef.1.refs_0_), channel_id=1, source_target_pairs={{0,32},{32,64},{64,96},{96,0},{1,33},{33,65},{65,97},{97,1},{2,34}... | collective-permute-start | bytes 393224 | tf_op jit(solution)/shard_map/ppermute | solution.py:400
  18.3 11.0 %collective-permute-start.1 = (f32[16,16,128]{2,1,0:T(8,128)}, f32[16,16,128]{2,1,0:T(8,128)S(1)}, u32[]{:S(2)}, u32[]{:S(2)}) collective-permute-start(f32[16,16,128]{2,1,0:T(8,128)} %parent_coef.1.refs_0_), channel_id=1, source_target_pairs={{0,64},{32,96},{64,0},{96,32},{1,65},{33,97},{65,1},{97,33},{2,66}... | collective-permute-start | bytes 393224 | tf_op jit(solution)/shard_map/ppermute | solution.py:400
  20.7 8.6 %collective-permute-start = (f32[16,16,128]{2,1,0:T(8,128)}, f32[16,16,128]{2,1,0:T(8,128)S(1)}, u32[]{:S(2)}, u32[]{:S(2)}) collective-permute-start(f32[16,16,128]{2,1,0:T(8,128)} %parent_coef.1.refs_0_), channel_id=1, source_target_pairs={{0,96},{32,0},{64,32},{96,64},{1,97},{33,1},{65,33},{97,65},{2,98}... | collective-permute-start | bytes 393224 | tf_op jit(solution)/shard_map/ppermute | solution.py:400
  29.3 0.7 copy-start.1
  29.3 0.7 copy-start.2
  29.3 0.7 copy-start.3
Sparse Core Ops, SparseCore 0:
  11.0 117.5 all-gather.1

commit v3 on v2

--- a/solution.py
+++ b/solution.py
@@ -15,9 +15,23 @@
 TILE = 16
 LANES = 2 * NV
 CAP = 64
-VMEM_LIMIT = 60 * 2**20
+SIDE = 4
+QUARTERS = 4
+BRANCHES = 4
+
 BRIEF = pl.CostEstimate(flops=0, bytes_accessed=0, transcendentals=0)
-BRANCHES = 4
+FINAL_LIMIT = 44 * 2**20
+SMALL_LIMIT = 20 * 2**20
+LONG = pl.CostEstimate(flops=10**11, bytes_accessed=10**9, transcendentals=0)
+
+CROSS = [(0, 0)]
+STEP1 = [(1, 0), (3, 0), (0, 1), (0, 3)]
+STEP2 = [(1, 1), (1, 3), (3, 1), (3, 3), (2, 0), (0, 2)]
+STEP3 = [(2, 1), (2, 3), (1, 2), (3, 2)]
+STEP4 = [(2, 2)]
+STAGES = [CROSS + STEP1, STEP2, STEP3, STEP4]
+ORDER = [(dy, dz, flip) for stage in STAGES for flip in (0, 1) for dy, dz in stage]
+
 
 def split(x):
     high = x.astype(jnp.bfloat16)
@@ -72,7 +86,7 @@
             pl.BlockSpec((block, TILE, LANES), lambda i: (i, 0, 0)),
             pl.BlockSpec((block // 2, K, LANES), lambda i: (i, 0, 0)),
         ),
-        compiler_params=pltpu.CompilerParams(vmem_limit_bytes=VMEM_LIMIT),
+        compiler_params=pltpu.CompilerParams(vmem_limit_bytes=SMALL_LIMIT),
         name="leaf_coef",
     )(basis, vectors)
 
@@ -84,45 +98,114 @@
     return jnp.concatenate([jnp.where(left_r, high, low), jnp.where(left_r, low, high)], axis=0).astype(jnp.bfloat16)
 
 
-DEPTH = 8
-UNROLL = 64
-
-
-def field_kernel(slots, block, pos_ref, val_ref, group_ref, coupling_ref, down_ref, basis_ref, out_ref, tiles, buf, totals, sem):
+def pick_kernel(plan, first, code_ref, *refs):
+    sources, out_ref, held, sem = refs[:-3], refs[-3], refs[-2], refs[-1]
+    step = pl.program_id(0)
+    left_r = left_lanes(ROWS)
+
+    @pl.when(step == 0)
+    def _():
+        for device, source, start, target, count in plan:
+            pltpu.make_async_copy(
+                sources[source].at[pl.ds(start, count)],
+                held.at[device, pl.ds(target, count)],
+                sem.at[device],
+            ).start()
+
+    pltpu.make_async_copy(held.at[step], held.at[step], sem.at[step]).wait()
+
+    @pl.loop(0, CAP // 32)
+    def _(part):
+        for n in range(32):
+            slot = part * 32 + n
+            code = code_ref[first + step, slot]
+            both = held[step, code >> 1]
+            out_ref[slot, :TILE] = pick_slot(both[:ROWS], code & 1, left_r)
+            out_ref[slot, TILE:] = pick_slot(both[ROWS:], code & 1, left_r)
+
+
+def picked_slots(devices, codes, pieces, unit, leaves):
+    first = ORDER.index(devices[0])
+    arrays, plan = [], []
+    for device, key in enumerate(devices):
+        for quarter in range(QUARTERS):
+            piece, at = next((p, p[1].index(key + (quarter,))) for p in pieces if key + (quarter,) in p[1])
+            index = next((i for i, a in enumerate(arrays) if a is piece[0]), None)
+            if index is None:
+                index = len(arrays)
+                arrays.append(piece[0])
+            last = plan[-1] if plan else None
+            if last and last[0] == device and last[1] == index and last[2] + last[4] == at * unit:
+                plan[-1] = last[:4] + (last[4] + unit,)
+            else:
+                plan.append((device, index, at * unit, quarter * unit, unit))
+    count = len(devices)
+    return pl.pallas_call(
+        functools.partial(pick_kernel, plan, first),
+        out_shape=jax.ShapeDtypeStruct((count * CAP, K, LANES), jnp.bfloat16),
+        grid=(count,),
+        in_specs=[pl.BlockSpec(memory_space=pltpu.SMEM)] + [pl.BlockSpec(memory_space=pl.ANY)] * len(arrays),
+        out_specs=pl.BlockSpec((CAP, K, LANES), lambda i: (i, 0, 0)),
+        scratch_shapes=[
+            pltpu.VMEM((count, leaves, TILE, LANES), jnp.float32),
+            pltpu.SemaphoreType.DMA((count,)),
+        ],
+        compiler_params=pltpu.CompilerParams(vmem_limit_bytes=SMALL_LIMIT),
+        cost_estimate=BRIEF,
+        name="pick",
+    )(codes, *arrays)
+
+
+def arrival_plan(devices, pieces, unit):
+    arrays, plan = [], []
+    for rank, key in enumerate(devices):
+        for quarter in range(QUARTERS):
+            piece, at = next((p, p[1].index(key + (quarter,))) for p in pieces if key + (quarter,) in p[1])
+            index = next((i for i, a in enumerate(arrays) if a is piece[0]), None)
+            if index is None:
+                index = len(arrays)
+                arrays.append(piece[0])
+            last = plan[-1] if plan else None
+            if last and last[:2] == (rank, index) and last[2] + last[4] == at * unit:
+                plan[-1] = last[:4] + (last[4] + unit,)
+            else:
+                plan.append((rank, index, at * unit, quarter * unit, unit))
+    return arrays, plan
+
+
+def field_kernel(slots, block, plan, ready, count, pos_ref, code_ref, *refs):
+    pieces, sources = refs[:ready], refs[ready : ready + count]
+    coupling_ref, down_ref, basis_ref, out_ref, tiles, held, totals, sem, held_sem = refs[ready + count :]
     step = pl.program_id(0)
     first = step * block
     left_k, left_r, left_v = left_lanes(K), left_lanes(ROWS), left_lanes(NV)
 
     @pl.when(step == 0)
     def _():
-        leaves = buf.shape[1]
-        devices = group_ref.shape[0] // leaves
-
-        def chunk(device):
-            at = pl.multiple_of(device * leaves, leaves)
-            return pltpu.make_async_copy(
-                group_ref.at[pl.ds(at, leaves)], buf.at[lax.rem(device, DEPTH)], sem.at[lax.rem(device, DEPTH)]
-            )
-
-        for device in range(DEPTH - 1):
-            chunk(device).start()
-
-        @pl.loop(0, devices)
+        for device, source, start, target, size in plan:
+            pltpu.make_async_copy(
+                sources[source].at[pl.ds(start, size)], held.at[device, pl.ds(target, size)], held_sem.at[device]
+            ).start()
+        copies, at = [], 0
+        for piece in pieces:
+            copies.append(pltpu.make_async_copy(piece, tiles.at[pl.ds(at, piece.shape[0])], sem.at[len(copies)]))
+            at += piece.shape[0]
+        for copy in copies:
+            copy.start()
+        early = at // CAP
+
+        @pl.loop(0, held.shape[0])
         def _(device):
-            @pl.when(device + DEPTH - 1 < devices)
-            def _():
-                chunk(device + DEPTH - 1).start()
-
-            chunk(device).wait()
-
-            @pl.loop(0, CAP // UNROLL)
-            def _(part):
-                for n in range(UNROLL):
-                    entry = device * CAP + part * UNROLL + n
-                    code = val_ref[device, part * UNROLL + n]
-                    both = buf[lax.rem(device, DEPTH), code >> 1]
-                    tiles[entry, :TILE] = pick_slot(both[:ROWS], code & 1, left_r)
-                    tiles[entry, TILE:] = pick_slot(both[ROWS:], code & 1, left_r)
+            pltpu.make_async_copy(held.at[device], held.at[device], held_sem.at[device]).wait()
+            for slot in range(CAP):
+                code = code_ref[early + device, slot]
+                both = held[device, code >> 1]
+                place = (early + device) * CAP + slot
+                tiles[place, :TILE] = pick_slot(both[:ROWS], code & 1, left_r)
+                tiles[place, TILE:] = pick_slot(both[ROWS:], code & 1, left_r)
+
+        for copy in copies:
+            copy.wait()
 
     def leaf_field(leaf):
         parts = [tiles[pos_ref[first + leaf, slot]] for slot in range(slots)]
@@ -182,18 +265,18 @@
         product(totals_first + quads - 1, totals[1])
 
 
-def products(pos, codes, group, coupling, down, basis, block):
+def products(pos, codes, tiles, late, pieces, coupling, down, basis, block):
     leaves, _, width = coupling.shape
     slots = width // K
-    smem = pl.BlockSpec(memory_space=pltpu.SMEM)
+    arrays, plan = arrival_plan(late, pieces, leaves // QUARTERS)
+    smem, hbm = pl.BlockSpec(memory_space=pltpu.SMEM), pl.BlockSpec(memory_space=pl.ANY)
     return pl.pallas_call(
-        functools.partial(field_kernel, slots, block),
+        functools.partial(field_kernel, slots, block, plan, len(tiles), len(arrays)),
         out_shape=jax.ShapeDtypeStruct((NV, leaves * PTS), jnp.float32),
         grid=(leaves // block,),
-        in_specs=[
-            smem,
-            smem,
-            pl.BlockSpec(memory_space=pl.ANY),
+        in_specs=[smem, smem]
+        + [hbm] * (len(tiles) + len(arrays))
+        + [
             pl.BlockSpec((block, K, width), lambda i: (i, 0, 0)),
             pl.BlockSpec((block // 2, K, LANES), lambda i: (i, 0, 0)),
             pl.BlockSpec((K, leaves * PTS), lambda i: (0, 0)),
@@ -201,29 +284,166 @@
         out_specs=pl.BlockSpec((NV, leaves * PTS), lambda i: (0, 0)),
         scratch_shapes=[
             pltpu.VMEM((leaves * slots, K, LANES), jnp.bfloat16),
-            pltpu.VMEM((DEPTH, leaves, TILE, LANES), jnp.float32),
+            pltpu.VMEM((len(late), leaves, TILE, LANES), jnp.float32),
             pltpu.VMEM((2, 4 * K, LANES), jnp.float32),
-            pltpu.SemaphoreType.DMA((DEPTH,)),
+            pltpu.SemaphoreType.DMA((len(tiles),)),
+            pltpu.SemaphoreType.DMA((len(late),)),
         ],
-        compiler_params=pltpu.CompilerParams(vmem_limit_bytes=VMEM_LIMIT),
+        compiler_params=pltpu.CompilerParams(vmem_limit_bytes=FINAL_LIMIT),
+        cost_estimate=BRIEF,
         name="leaf_field_product",
-    )(pos, codes, group, coupling, down, basis)
-
-
-def order_kernel(list_ref, mask_ref, pos_ref, code_ref):
+    )(pos, codes, *tiles, *arrays, coupling, down, basis)
+
+
+def subtree_index(dy, dz, flip, z, y, core):
+    return (z + dz) % SIDE * (2 * SIDE) + (y + dy) % SIDE * 2 + (core + flip) % 2
+
+
+def moved(piece, axis, by, send):
+    array, segs = piece
+    perm, out = [], []
+    for z in range(SIDE):
+        for y in range(SIDE):
+            for core in range(2):
+                step = {"y": (by, 0, 0), "z": (0, by, 0), "core": (0, 0, 1)}[axis]
+                perm.append((subtree_index(0, 0, 0, z, y, core), subtree_index(*step, z, y, core)))
+    for dy, dz, flip, quarter in segs:
+        if axis == "y":
+            out.append(((dy - by) % SIDE, dz, flip, quarter))
+        elif axis == "z":
+            out.append((dy, (dz - by) % SIDE, flip, quarter))
+        else:
+            out.append((dy, dz, 1 - flip, quarter))
+    return send(array, "subtree", perm), out
+
+
+class Turns:
+    def __init__(self):
+        self.last = None
+
+    def __call__(self, array, axis, perm, after=()):
+        if self.last is not None:
+            array, _ = lax.optimization_barrier((array, (self.last, after)))
+        self.last = lax.ppermute(array, axis, perm)
+        return self.last
+
+
+def pack_kernel(plan, count, *refs):
+    sources, targets, (held, read_sem, write_sem) = refs[:count], refs[count:-3], refs[-3:]
+    reads, writes, base = [], [], 0
+    for number, (source, start, target, at, size) in enumerate(plan):
+        place = held.at[pl.ds(base, size)]
+        reads.append(pltpu.make_async_copy(sources[source].at[pl.ds(start, size)], place, read_sem.at[number]))
+        writes.append(pltpu.make_async_copy(place, targets[target].at[pl.ds(at, size)], write_sem.at[number]))
+        base += size
+    for read in reads:
+        read.start()
+    for read, write in zip(reads, writes, strict=True):
+        read.wait()
+        write.start()
+    for write in writes:
+        write.wait()
+
+
+def packed(pieces, wanted, unit, cost=BRIEF):
+    arrays, plan = [], []
+    for target, keys in enumerate(wanted):
+        for at, key in enumerate(keys):
+            piece = next(p for p in pieces if key in p[1])
+            source = next((i for i, a in enumerate(arrays) if a is piece[0]), None)
+            if source is None:
+                source = len(arrays)
+                arrays.append(piece[0])
+            start = piece[1].index(key) * unit
+            last = plan[-1] if plan else None
+            if last and last[0] == source and last[2] == target and last[1] + last[4] == start:
+                plan[-1] = last[:4] + (last[4] + unit,)
+            else:
+                plan.append((source, start, target, at * unit, unit))
+    shapes = tuple(
+        jax.ShapeDtypeStruct((len(keys) * unit,) + arrays[0].shape[1:], arrays[0].dtype) for keys in wanted
+    )
+    any_space = pl.BlockSpec(memory_space=pl.ANY)
+    out = pl.pallas_call(
+        functools.partial(pack_kernel, plan, len(arrays)),
+        out_shape=shapes,
+        in_specs=[any_space] * len(arrays),
+        out_specs=(any_space,) * len(shapes),
+        scratch_shapes=[
+            pltpu.VMEM((sum(shape.shape[0] for shape in shapes),) + arrays[0].shape[1:], arrays[0].dtype),
+            pltpu.SemaphoreType.DMA((len(plan),)),
+            pltpu.SemaphoreType.DMA((len(plan),)),
+        ],
+        compiler_params=pltpu.CompilerParams(vmem_limit_bytes=SMALL_LIMIT),
+        cost_estimate=cost,
+        name="pack",
+    )(*arrays)
+    return [(array, list(keys)) for array, keys in zip(out, wanted, strict=True)]
+
+
+def segs(dy, dz, quarters):
+    return [(dy % SIDE, dz % SIDE, 0, q) for q in quarters]
+
+
+FIRST, SECOND = (0, 1), (2, 3)
+SENDS = [
+    [("y", 1, segs(0, 0, range(4))), ("y", -1, segs(0, 0, range(4))), ("z", 1, segs(0, 0, range(4))), ("z", -1, segs(0, 0, range(4)))],
+    [
+        ("z", 1, segs(1, 0, FIRST) + segs(-1, 0, FIRST) + segs(0, -1, FIRST)),
+        ("z", -1, segs(1, 0, FIRST) + segs(-1, 0, FIRST) + segs(0, 1, SECOND)),
+        ("y", 1, segs(0, 1, SECOND) + segs(0, -1, SECOND) + segs(-1, 0, FIRST)),
+        ("y", -1, segs(0, 1, SECOND) + segs(0, -1, SECOND) + segs(1, 0, SECOND)),
+    ],
+    [
+        ("z", 1, segs(2, 0, FIRST) + segs(1, -1, (0,)) + segs(-1, -1, (0,))),
+        ("z", -1, segs(2, 0, FIRST) + segs(1, 1, (1,)) + segs(-1, 1, (1,))),
+        ("y", 1, segs(0, 2, SECOND) + segs(-1, 1, (2,)) + segs(-1, -1, (2,))),
+        ("y", -1, segs(0, 2, SECOND) + segs(1, 1, (3,)) + segs(1, -1, (3,))),
+    ],
+    [("z", 1, segs(2, -1, (0,))), ("z", -1, segs(2, 1, (1,))), ("y", 1, segs(-1, 2, (2,))), ("y", -1, segs(1, 2, (3,)))],
+]
+
+
+def ring(own, leaves, turns, beside):
+    unit = leaves // QUARTERS
+    mine = (own, segs(0, 0, range(QUARTERS)))
+    have, others, fresh, done = [mine], [], [mine], []
+    payloads = [mine] * len(SENDS[0])
+    for number, sends in enumerate(SENDS):
+        new = [moved(p, axis, by, lax.ppermute) for p, (axis, by, _) in zip(payloads, sends, strict=True)]
+        joined = fresh[0]
+        if number > 0:
+            joined = packed(fresh, [[key for p in fresh for key in p[1]]], unit)[0]
+        swapped = moved(joined, "core", 1, turns)
+        done = beside[number](have, others, done)
+        wanted = [[key for p in new for key in p[1]]]
+        if number + 1 < len(SENDS):
+            wanted = [keys for _, _, keys in SENDS[number + 1]]
+        following = packed(have + new, wanted, unit, LONG)
+        arrays, ahead, other, done = lax.optimization_barrier(
+            ([p[0] for p in new], [p[0] for p in following], swapped[0], done)
+        )
+        fresh = [(array, p[1]) for array, p in zip(arrays, new, strict=True)]
+        payloads = [(array, p[1]) for array, p in zip(ahead, following, strict=True)]
+        have, others = have + fresh, others + [(other, swapped[1])]
+    return have + others + [moved(payloads[0], "core", 1, lax.ppermute)], done
+
+
+def order_kernel(own_ref, list_ref, mask_ref, pos_ref, code_ref):
     leaves, slots = list_ref.shape
-    devices = code_ref.shape[0]
+    devices = len(ORDER)
     names = list_ref[...]
     owner = lax.rem(names // leaves, devices)
     code = (lax.rem(names, leaves) * 2 + mask_ref[...]).astype(jnp.float32)
     row = lax.broadcasted_iota(jnp.int32, (leaves, LANES), 0)
     lane = lax.broadcasted_iota(jnp.int32, (leaves, LANES), 1)
     below = (row > lane).astype(jnp.bfloat16)
+    own = jnp.broadcast_to(own_ref[...], (leaves, LANES))
     used = jnp.zeros((1, LANES), jnp.float32)
     sorted_codes = jnp.zeros((LANES, LANES), jnp.float32)
     places = jnp.zeros((leaves, LANES), jnp.float32)
     for slot in range(slots):
-        named = (owner[:, slot : slot + 1] == lane).astype(jnp.float32)
+        named = (owner[:, slot : slot + 1] == own).astype(jnp.float32)
         before = jnp.dot(below, named.astype(jnp.bfloat16), preferred_element_type=jnp.float32) + used
         used = used + jnp.sum(named, axis=0, keepdims=True)
         index = jnp.sum(named * before, axis=1, keepdims=True)
@@ -240,17 +460,17 @@
     code_ref[...] = sorted_codes[:devices].astype(jnp.int32)
 
 
-def slot_order(leaf_list, leaf_mask, devices):
+def slot_order(leaf_list, leaf_mask, own):
     return pl.pallas_call(
         order_kernel,
         out_shape=(
             jax.ShapeDtypeStruct(leaf_list.shape, jnp.int32),
-            jax.ShapeDtypeStruct((devices, LANES), jnp.int32),
+            jax.ShapeDtypeStruct((len(ORDER), LANES), jnp.int32),
         ),
-        compiler_params=pltpu.CompilerParams(vmem_limit_bytes=VMEM_LIMIT),
+        compiler_params=pltpu.CompilerParams(vmem_limit_bytes=SMALL_LIMIT),
         cost_estimate=BRIEF,
         name="slot_order",
-    )(leaf_list, leaf_mask)
+    )(own, leaf_list, leaf_mask)
 
 
 def parent_coef_kernel(pair_ref, transfer_ref, out_ref):
@@ -288,7 +508,7 @@
     return pl.pallas_call(
         parent_coef_kernel,
         out_shape=jax.ShapeDtypeStruct((parents, TILE, LANES), jnp.float32),
-        compiler_params=pltpu.CompilerParams(vmem_limit_bytes=VMEM_LIMIT),
+        compiler_params=pltpu.CompilerParams(vmem_limit_bytes=SMALL_LIMIT),
         cost_estimate=BRIEF,
         name="parent_coef",
     )(coef_pairs, rows)
@@ -367,7 +587,7 @@
         ],
         out_specs=pl.BlockSpec((CHILD // 2, K, LANES), lambda i: (i, 0, 0)),
         scratch_shapes=[pltpu.VMEM((BRANCHES * parents, TILE, LANES), jnp.float32)],
-        compiler_params=pltpu.CompilerParams(vmem_limit_bytes=VMEM_LIMIT),
+        compiler_params=pltpu.CompilerParams(vmem_limit_bytes=SMALL_LIMIT),
         cost_estimate=BRIEF,
         name="parent_field",
     )(parent_list, parent_mask, branch, *coef_all, coupling, rows)
@@ -388,20 +608,52 @@
     parent_count = parent_list.shape[0]
     subtrees = lax.axis_size("subtree")
     branches = lax.axis_size("branch")
-
+    me = lax.axis_index("subtree")
+    here = (me // (2 * SIDE), me // 2 % SIDE, me % 2)
+
+    own = jnp.stack([subtree_index(dy, dz, flip, *here) for dy, dz, flip in ORDER]).astype(jnp.int32)
+    own = jnp.pad(own, (0, LANES - len(ORDER)), constant_values=-1)[None, :]
+    branch = lax.axis_index("branch").astype(jnp.int32)[None]
+    rows = transfer.reshape(parent_count * CHILD * ROWS, LANES)
     coef, coef_pairs = leaf_coefs(basis, vectors, 64)
-    group = lax.all_gather(coef, "subtree", axis=0, tiled=True)
-    pos, codes = slot_order(leaf_list, leaf_mask, subtrees)
-
-    rows = transfer.reshape(parent_count * CHILD * ROWS, LANES)
-    branch = lax.axis_index("branch").astype(jnp.int32)[None]
-    parent_coef = parent_coefs(coef_pairs, rows)
-    coef_all = [parent_coef] + [
-        lax.ppermute(parent_coef, "branch", [(i, (i - by) % branches) for i in range(branches)])
-        for by in range(1, branches)
-    ]
-    down = downward_pairs(parent_list, parent_mask, branch, parent_count * subtrees, coef_all, parent_coupling, rows)
-    return products(pos, codes, group, leaf_coupling, down, basis, 32)
+    turns = Turns()
+
+    def pick(number, flips, codes, pieces):
+        devices = [key + (flip,) for flip in flips for key in STAGES[number]]
+        return picked_slots(devices, codes, pieces, leaf_count // QUARTERS, leaf_count)
+
+    def beside_first(have, others, done):
+        parent_coef = parent_coefs(coef_pairs, rows)
+        coef_all = [parent_coef]
+        order = ()
+        for by in range(1, branches):
+            perm = [(i, (i - by) % branches) for i in range(branches)]
+            coef_all.append(turns(parent_coef, "branch", perm, order))
+            if by == 1:
+                order = slot_order(leaf_list, leaf_mask, own)
+        return order, coef_all
+
+    def beside_second(have, others, done):
+        order, coef_all = done
+        down = downward_pairs(
+            parent_list, parent_mask, branch, parent_count * subtrees, coef_all, parent_coupling, rows
+        )
+        return order, down, [pick(0, (0,), order[1], have)]
+
+    def beside_third(have, others, done):
+        order, down, tiles = done
+        far = pick(0, (1,), order[1], others)
+        return order, down, tiles + [far, pick(1, (0,), order[1], have)]
+
+    def beside_fourth(have, others, done):
+        order, down, tiles = done
+        return order, down, tiles + [pick(1, (1,), order[1], others)]
+
+    pieces, ((pos, codes), down, tiles) = ring(
+        coef, leaf_count, turns, [beside_first, beside_second, beside_third, beside_fourth]
+    )
+    late = ORDER[2 * (len(STAGES[0]) + len(STAGES[1])) :]
+    return products(pos, codes, tiles, late, pieces, leaf_coupling, down, basis, 16)
 
 
 def solution(mesh):

time: 157 us -> 148 us (0.943)
  waiting for transfers between devices: 82.4 us -> 26.7 us
  starting transfers between devices: 5.65 us -> 37.5 us
  Pallas kernels: 51.4 us -> 69.2 us
  between operations: 13.5 us -> 0.54 us
  local copies, waits for them, and re-layouts: 3.06 us -> 13.7 us
    all_gather x1 -> x0, waiting for transfers between devices: 82.4 us -> none  [per_device(): group = lax.all_gather(coef, 'subtree', axis=0, tiled=True)]
    ppermute x3 -> x24, starting transfers between devices: 5.64 us -> 37.5 us  [the longest x17 23.1 us: moved(): return (send(array, 'subtree', perm), out)]
    ppermute x3 -> x24, waiting for transfers between devices: 0.01 us -> 26.7 us  [the longest x17 19.2 us: moved(): return (send(array, 'subtree', perm), out)]
    pallas_call x1 -> x12, Pallas kernels: 20.5 us -> 44.8 us  [the longest x1 17 us: products(): pl.pallas_call(functools.partial(field_kernel, slots, block, plan, len(ti...]
    unnamed x14 -> x58, local copies, waits for them, and re-layouts: 2.15 us -> 13.5 us
    pallas_call x1, Pallas kernels: 4.45 us -> 2.47 us  [parent_coefs(): pl.pallas_call(parent_coef_kernel, out_shape=jax.ShapeDtypeStruct((parent...]
    pallas_call x1, Pallas kernels: 16.2 us -> 14.6 us  [downward_pairs(): pl.pallas_call(functools.partial(parent_field_kernel, group), out_shape=j...]
  transfers between devices with their start and end apart: 4 -> 24, of which waited for: 1 -> 10; matrix products, arithmetic and copies ran while one was open for 2% -> 0% of each run, Pallas kernels for 17% -> 33%
where the time goes in v3:
time: 148 us
  Pallas kernels  69.2 us (47%)
  starting transfers between devices  37.5 us (25%)
  waiting for transfers between devices  26.7 us (18%)
  local copies, waits for them, and re-layouts  13.7 us (9%)
    ppermute x17, starting transfers between devices, moved(): return (send(array, 'subtree', perm), out)  23.1 us
    ppermute x17, waiting for transfers between devices, moved(): return (send(array, 'subtree', perm), out)  19.2 us
    pallas_call x1, Pallas kernels, products(): pl.pallas_call(functools.partial(field_kernel, slots, block, plan, len(ti...  17 us
    pallas_call x4, Pallas kernels, picked_slots(): pl.pallas_call(functools.partial(pick_kernel, plan, first), out_shape=jax...  15.9 us
    pallas_call x1, Pallas kernels, downward_pairs(): pl.pallas_call(functools.partial(parent_field_kernel, group), out_shape=j...  14.6 us
    ppermute x7, starting transfers between devices, __call__(): self.last = lax.ppermute(array, axis, perm)  14.4 us
    unnamed x58, local copies, waits for them, and re-layouts  13.5 us
    pallas_call x7, Pallas kernels, packed(): pl.pallas_call(functools.partial(pack_kernel, plan, len(arrays)), out_sha...  11.9 us
  transfers between devices with their start and end apart: 24, of which 10 were waited for; matrix products, arithmetic and copies ran while one was open for 0% of the time, Pallas kernels for 33%

profile of v3, /device:TPU:1, one launch (start us, length us, event | category | flops | bytes accessed | tf_op | source)
XLA Modules:
  0.0 147.6 jit_solution(11379395055953018485)
XLA Ops:
  0.0 1.2 copy-done.6
  1.2 1.6 %copy-done.14 = f32[64,8192]{1,0:T(8,128)S(1)} copy-done((f32[64,8192]{1,0:T(8,128)S(1)}, f32[64,8192]{1,0:T(8,128)}, u32[]{:S(2)}) %copy-start.14) | copy-done | bytes 2097176
  2.8 2.9 %leaf_coef.1 = (f32[128,16,128]{2,1,0:T(8,128)}, f32[64,32,128]{2,1,0:T(8,128)S(1)}) custom-call(f32[32,8192]{1,0:T(8,128)S(1)} %copy-done.6, f32[64,8192]{1,0:T(8,128)S(1)} %copy-done.14), custom_call_target="tpu_custom_call" | custom-call | tf_op jit(solution)/shard_map/leaf_coef/pallas_call | solution.py:74
  5.7 1.0 copy-done.16
  6.7 1.4 collective-permute-start.4
  8.1 1.4 collective-permute-start
  9.5 1.4 collective-permute-start.1
  10.9 1.7 %collective-permute-start.2 = (f32[128,16,128]{2,1,0:T(8,128)}, f32[128,16,128]{2,1,0:T(8,128)}, u32[]{:S(2)}, u32[]{:S(2)}) collective-permute-start(f32[128,16,128]{2,1,0:T(8,128)} %get-tuple-element.83.refs_0_), channel_id=1, source_target_pairs={{0,8},{1,9},{2,10},{3,11},{4,12},{5,13},{6,14},{7,15},{8,16},{9,17... | collective-permute-start | bytes 3145736 | tf_op jit(solution)/shard_map/ppermute | solution.py:317
  12.6 2.1 %collective-permute-start.3 = (f32[128,16,128]{2,1,0:T(8,128)}, f32[128,16,128]{2,1,0:T(8,128)}, u32[]{:S(2)}, u32[]{:S(2)}) collective-permute-start(f32[128,16,128]{2,1,0:T(8,128)} %get-tuple-element.83.refs_0_), channel_id=1, source_target_pairs={{0,24},{1,25},{2,26},{3,27},{4,28},{5,29},{6,30},{7,31},{8,0},{9,1... | collective-permute-start | bytes 3145736 | tf_op jit(solution)/shard_map/ppermute | solution.py:317
  14.8 1.4 copy-done.17
  16.2 2.5 %parent_coef.1.refs_0_ = f32[16,16,128]{2,1,0:T(8,128)S(1)} custom-call(f32[64,32,128]{2,1,0:T(8,128)S(1)} %copy-done.17, f32[1024,128]{1,0:T(8,128)S(1)} %reshape.3.transfer_ref.refs_5_), custom_call_target="tpu_custom_call" | custom-call | tf_op jit(solution)/shard_map/parent_coef/pallas_call | solution.py:508
  18.7 2.5 %collective-permute-start.5 = (f32[16,16,128]{2,1,0:T(8,128)S(1)}, f32[16,16,128]{2,1,0:T(8,128)S(1)}, u32[]{:S(2)}, u32[]{:S(2)}) collective-permute-start(f32[16,16,128]{2,1,0:T(8,128)S(1)} %parent_coef.1.refs_0_), channel_id=1, source_target_pairs={{0,96},{32,0},{64,32},{96,64},{1,97},{33,1},{65,33},{97,65},{2,98}... | collective-permute-start | bytes 393224 | tf_op jit(solution)/shard_map/ppermute | solution.py:327
  21.6 4.4 %slot_order.1 = (s32[128,16]{1,0:T(8,128)S(1)}, s32[32,128]{1,0:T(8,128)S(1)}) custom-call(s32[1,128]{1,0:T(1,128)S(1)} %pad_bitcast_fusion.own_ref, s32[128,16]{1,0:T(8,128)S(1)} %copy.10.list_ref, s32[128,16]{1,0:T(8,128)S(1)} %copy.11.mask_ref), custom_call_target="tpu_custom_call" | custom-call | tf_op jit(solution)/shard_map/slot_order/pallas_call | solution.py:464
  26.6 4.8 %collective-permute-done.6.refs_2_ = f32[16,16,128]{2,1,0:T(8,128)S(1)} collective-permute-done((f32[16,16,128]{2,1,0:T(8,128)S(1)}, f32[16,16,128]{2,1,0:T(8,128)S(1)}, u32[]{:S(2)}, u32[]{:S(2)}) %collective-permute-start.6) | collective-permute-done | bytes 131104 | tf_op jit(solution)/shard_map/ppermute | solution.py:327
  31.4 3.2 %collective-permute-done.refs_1_.refs_0_.refs_2_ = f32[128,16,128]{2,1,0:T(8,128)S(1)} collective-permute-done((f32[128,16,128]{2,1,0:T(8,128)}, f32[128,16,128]{2,1,0:T(8,128)S(1)}, u32[]{:S(2)}, u32[]{:S(2)}) %collective-permute-start) | collective-permute-done | bytes 1048608 | tf_op jit(solution)/shard_map/ppermute | solution.py:317
  34.6 3.5 %collective-permute-done.2.refs_2_.refs_4_ = f32[128,16,128]{2,1,0:T(8,128)} collective-permute-done((f32[128,16,128]{2,1,0:T(8,128)}, f32[128,16,128]{2,1,0:T(8,128)}, u32[]{:S(2)}, u32[]{:S(2)}) %collective-permute-start.2) | collective-permute-done | bytes 1048608 | tf_op jit(solution)/shard_map/ppermute | solution.py:317
  38.1 4.7 %pack.7 = (f32[192,16,128]{2,1,0:T(8,128)}, f32[192,16,128]{2,1,0:T(8,128)}, f32[192,16,128]{2,1,0:T(8,128)}, f32[192,16,128]{2,1,0:T(8,128)}) custom-call(f32[128,16,128]{2,1,0:T(8,128)S(1)} %collective-permute-done.1.refs_0_.refs_1_, f32[128,16,128]{2,1,0:T(8,128)S(1)} %collective-permute-done.refs_1_.refs_0_.refs_2_, ...), custom_call_target="tpu_custom_call" | custom-call | flops 99999997952 | bytes 1000000000 | tf_op jit(solution)/shard_map/pack/pallas_call | solution.py:367
  43.5 2.7 %collective-permute-start.11 = (f32[192,16,128]{2,1,0:T(8,128)}, f32[192,16,128]{2,1,0:T(8,128)S(1)}, u32[]{:S(2)}, u32[]{:S(2)}) collective-permute-start(f32[192,16,128]{2,1,0:T(8,128)} %get-tuple-element.97), channel_id=1, source_target_pairs={{0,6},{1,7},{2,0},{3,1},{4,2},{5,3},{6,4},{7,5},{8,14},{9,15},{10,... | collective-permute-start | bytes 4718600 | tf_op jit(solution)/shard_map/ppermute | solution.py:317
  46.5 2.3 %collective-permute-start.9 = (f32[192,16,128]{2,1,0:T(8,128)}, f32[192,16,128]{2,1,0:T(8,128)}, u32[]{:S(2)}, u32[]{:S(2)}) collective-permute-start(f32[192,16,128]{2,1,0:T(8,128)} %get-tuple-element.95), channel_id=1, source_target_pairs={{0,24},{1,25},{2,26},{3,27},{4,28},{5,29},{6,30},{7,31},{8,0},{9,1... | collective-permute-start | bytes 4718600 | tf_op jit(solution)/shard_map/ppermute | solution.py:317
  48.9 1.2 copy-done.9
  50.1 1.2 copy-done.12
  51.3 1.9 %pack.9 = f32[512,16,128]{2,1,0:T(8,128)S(1)} custom-call(f32[128,16,128]{2,1,0:T(8,128)S(1)} %copy-done.9, f32[128,16,128]{2,1,0:T(8,128)S(1)} %copy-done.12, f32[128,16,128]{2,1,0:T(8,128)} %collective-permute-done.2.refs_2_.refs_4_, f32[128,16,128]{2,1,0:T(8,128)} %collective-permute-done.3.refs_3_), custom_call_target="tpu_custom_call" | custom-call | tf_op jit(solution)/shard_map/pack/pallas_call | solution.py:367
  53.5 4.0 %pick.4.refs_0_ = bf16[320,32,128]{2,1,0:T(8,128)(2,1)S(1)} custom-call(s32[32,128]{1,0:T(8,128)S(1)} %get-tuple-element.149.code_ref, f32[128,16,128]{2,1,0:T(8,128)} %get-tuple-element.83.refs_0_, f32[128,16,128]{2,1,0:T(8,128)S(1)} %copy-done.13, f32[128,16,128]{2,1,0:T(8,128)S(1)} %copy-done.10, f32[128,16,128]{2,1,0:T(8,128)} %collective-permute-done.3.refs_3_, ...), custom_call_target="tpu_custom_call" | custom-call | tf_op jit(solution)/shard_map/pick/pallas_call | solution.py:143
  57.5 1.6 %copy-done.2 = bf16[320,32,128]{2,1,0:T(8,128)(2,1)} copy-done((bf16[320,32,128]{2,1,0:T(8,128)(2,1)}, bf16[320,32,128]{2,1,0:T(8,128)(2,1)S(1)}, u32[]{:S(2)}) %copy-start.2) | copy-done | bytes 2621464
  59.2 2.2 %collective-permute-start.12 = (f32[512,16,128]{2,1,0:T(8,128)S(1)}, f32[512,16,128]{2,1,0:T(8,128)S(1)}, u32[]{:S(2)}, u32[]{:S(2)}) collective-permute-start(f32[512,16,128]{2,1,0:T(8,128)S(1)} %pack.9), channel_id=1, source_target_pairs={{0,1},{1,0},{2,3},{3,2},{4,5},{5,4},{6,7},{7,6},{8,9},{9,8},{10,11... | collective-permute-start | bytes 12582920 | tf_op jit(solution)/shard_map/ppermute | solution.py:327
  61.3 14.6 %parent_field.1.refs_15_ = f32[64,32,128]{2,1,0:T(8,128)S(1)} custom-call(s32[16,32]{1,0:T(8,128)S(1)} %copy-done.22, s32[16,32]{1,0:T(8,128)S(1)} %copy-done.23, s32[1]{0:T(128)} %bitcast.33.branch_ref, f32[16,16,128]{2,1,0:T(8,128)S(1)} %parent_coef.1.refs_0_, f32[16,16,128]{2,1,0:T(8,128)S(1)} %collective-permute-done.5.refs_1_, ...), custom_call_target="tpu_custom_call" | custom-call | tf_op jit(solution)/shard_map/parent_field/pallas_call | solution.py:574
  76.0 3.9 %collective-permute-done.10.refs_0_.refs_2_.refs_3_ = f32[192,16,128]{2,1,0:T(8,128)S(1)} collective-permute-done((f32[192,16,128]{2,1,0:T(8,128)}, f32[192,16,128]{2,1,0:T(8,128)S(1)}, u32[]{:S(2)}, u32[]{:S(2)}) %collective-permute-start.10) | collective-permute-done | bytes 1572896 | tf_op jit(solution)/shard_map/ppermute | solution.py:317
  79.9 2.1 %collective-permute-done.8.refs_1_.refs_0_.refs_2_ = f32[192,16,128]{2,1,0:T(8,128)} collective-permute-done((f32[192,16,128]{2,1,0:T(8,128)}, f32[192,16,128]{2,1,0:T(8,128)}, u32[]{:S(2)}, u32[]{:S(2)}) %collective-permute-start.8) | collective-permute-done | bytes 1572896 | tf_op jit(solution)/shard_map/ppermute | solution.py:317
  82.0 1.9 %pack.8 = (f32[128,16,128]{2,1,0:T(8,128)S(1)}, f32[128,16,128]{2,1,0:T(8,128)S(1)}, f32[128,16,128]{2,1,0:T(8,128)S(1)}, f32[128,16,128]{2,1,0:T(8,128)S(1)}) custom-call(f32[192,16,128]{2,1,0:T(8,128)S(1)} %collective-permute-done.10.refs_0_.refs_2_.refs_3_, f32[192,16,128]{2,1,0:T(8,128)} %collective-permute-done.8.refs_1_.refs_0_.refs_2_, ...), custom_call_target="tpu_custom_call" | custom-call | flops 99999997952 | bytes 1000000000 | tf_op jit(solution)/shard_map/pack/pallas_call | solution.py:367
  84.0 2.7 %collective-permute-start.14 = (f32[128,16,128]{2,1,0:T(8,128)S(1)}, f32[128,16,128]{2,1,0:T(8,128)S(1)}, u32[]{:S(2)}, u32[]{:S(2)}) collective-permute-start(f32[128,16,128]{2,1,0:T(8,128)S(1)} %get-tuple-element.114), channel_id=1, source_target_pairs={{0,24},{1,25},{2,26},{3,27},{4,28},{5,29},{6,30},{7,31},{8,0},{9,1... | collective-permute-start | bytes 3145736 | tf_op jit(solution)/shard_map/ppermute | solution.py:317
  86.6 2.7 %collective-permute-start.16 = (f32[128,16,128]{2,1,0:T(8,128)S(1)}, f32[128,16,128]{2,1,0:T(8,128)S(1)}, u32[]{:S(2)}, u32[]{:S(2)}) collective-permute-start(f32[128,16,128]{2,1,0:T(8,128)S(1)} %get-tuple-element.116), channel_id=1, source_target_pairs={{0,6},{1,7},{2,0},{3,1},{4,2},{5,3},{6,4},{7,5},{8,14},{9,15},{10,... | collective-permute-start | bytes 3145736 | tf_op jit(solution)/shard_map/ppermute | solution.py:317
  89.3 2.3 %pack.11 = f32[768,16,128]{2,1,0:T(8,128)S(1)} custom-call(f32[192,16,128]{2,1,0:T(8,128)} %collective-permute-done.8.refs_1_.refs_0_.refs_2_, f32[192,16,128]{2,1,0:T(8,128)} %collective-permute-done.9.refs_2_.refs_1_.refs_0_, f32[192,16,128]{2,1,0:T(8,128)S(1)} %collective-permute-done.10.refs_0_.refs_2_.refs_3_, ...), custom_call_target="tpu_custom_call" | custom-call | tf_op jit(solution)/shard_map/pack/pallas_call | solution.py:367
  91.6 4.2 %pick.6.refs_2_ = bf16[384,32,128]{2,1,0:T(8,128)(2,1)S(1)} custom-call(s32[32,128]{1,0:T(8,128)S(1)} %get-tuple-element.149.code_ref, f32[192,16,128]{2,1,0:T(8,128)} %collective-permute-done.9.refs_2_.refs_1_.refs_0_, f32[192,16,128]{2,1,0:T(8,128)S(1)} %collective-permute-done.11.refs_3_.refs_1_, ...), custom_call_target="tpu_custom_call" | custom-call | tf_op jit(solution)/shard_map/pick/pallas_call | solution.py:143
  95.8 1.6 %copy-done = bf16[384,32,128]{2,1,0:T(8,128)(2,1)} copy-done((bf16[384,32,128]{2,1,0:T(8,128)(2,1)}, bf16[384,32,128]{2,1,0:T(8,128)(2,1)S(1)}, u32[]{:S(2)}) %copy-start) | copy-done | bytes 3145752
  97.5 3.6 %collective-permute-start.17 = (f32[768,16,128]{2,1,0:T(8,128)S(1)}, f32[768,16,128]{2,1,0:T(8,128)S(1)}, u32[]{:S(2)}, u32[]{:S(2)}) collective-permute-start(f32[768,16,128]{2,1,0:T(8,128)S(1)} %pack.11), channel_id=1, source_target_pairs={{0,1},{1,0},{2,3},{3,2},{4,5},{5,4},{6,7},{7,6},{8,9},{9,8},{10,11... | collective-permute-start | bytes 18874376 | tf_op jit(solution)/shard_map/ppermute | solution.py:327
  101.1 4.0 %pick.5.refs_1_ = bf16[320,32,128]{2,1,0:T(8,128)(2,1)S(1)} custom-call(s32[32,128]{1,0:T(8,128)S(1)} %get-tuple-element.149.code_ref, f32[128,16,128]{2,1,0:T(8,128)} %collective-permute-done.4.refs_0_, f32[512,16,128]{2,1,0:T(8,128)S(1)} %collective-permute-done.12.refs_1_), custom_call_target="tpu_custom_call" | custom-call | tf_op jit(solution)/shard_map/pick/pallas_call | solution.py:143
  105.1 2.1 %collective-permute-done.13.refs_0_.refs_7_ = f32[128,16,128]{2,1,0:T(8,128)S(1)} collective-permute-done((f32[128,16,128]{2,1,0:T(8,128)S(1)}, f32[128,16,128]{2,1,0:T(8,128)S(1)}, u32[]{:S(2)}, u32[]{:S(2)}) %collective-permute-start.13) | collective-permute-done | bytes 1048608 | tf_op jit(solution)/shard_map/ppermute | solution.py:317
  107.3 2.1 %collective-permute-done.15.refs_2_.refs_5_ = f32[128,16,128]{2,1,0:T(8,128)S(1)} collective-permute-done((f32[128,16,128]{2,1,0:T(8,128)S(1)}, f32[128,16,128]{2,1,0:T(8,128)S(1)}, u32[]{:S(2)}, u32[]{:S(2)}) %collective-permute-start.15) | collective-permute-done | bytes 1048608 | tf_op jit(solution)/shard_map/ppermute | solution.py:317
  109.6 1.3 collective-permute-done.17.refs_0_
  110.9 2.7 %collective-permute-start.19 = (f32[32,16,128]{2,1,0:T(8,128)S(1)}, f32[32,16,128]{2,1,0:T(8,128)S(1)}, u32[]{:S(2)}, u32[]{:S(2)}) collective-permute-start(f32[32,16,128]{2,1,0:T(8,128)S(1)} %get-tuple-element.133), channel_id=1, source_target_pairs={{0,24},{1,25},{2,26},{3,27},{4,28},{5,29},{6,30},{7,31},{8,0},{9,1... | collective-permute-start | bytes 786440 | tf_op jit(solution)/shard_map/ppermute | solution.py:317
  113.6 2.7 %collective-permute-start.21 = (f32[32,16,128]{2,1,0:T(8,128)S(1)}, f32[32,16,128]{2,1,0:T(8,128)S(1)}, u32[]{:S(2)}, u32[]{:S(2)}) collective-permute-start(f32[32,16,128]{2,1,0:T(8,128)S(1)} %get-tuple-element.135), channel_id=1, source_target_pairs={{0,6},{1,7},{2,0},{3,1},{4,2},{5,3},{6,4},{7,5},{8,14},{9,15},{10,... | collective-permute-start | bytes 786440 | tf_op jit(solution)/shard_map/ppermute | solution.py:317
  116.3 0.6 pack.13
  116.9 4.0 %collective-permute-start.22 = (f32[512,16,128]{2,1,0:T(8,128)S(1)}, f32[512,16,128]{2,1,0:T(8,128)S(1)}, u32[]{:S(2)}, u32[]{:S(2)}) collective-permute-start(f32[512,16,128]{2,1,0:T(8,128)S(1)} %pack.13), channel_id=1, source_target_pairs={{0,1},{1,0},{2,3},{3,2},{4,5},{5,4},{6,7},{7,6},{8,9},{9,8},{10,11... | collective-permute-start | bytes 12582920 | tf_op jit(solution)/shard_map/ppermute | solution.py:327
  120.9 3.6 %pick.7.refs_3_ = bf16[384,32,128]{2,1,0:T(8,128)(2,1)S(1)} custom-call(s32[32,128]{1,0:T(8,128)S(1)} %get-tuple-element.149.code_ref, f32[768,16,128]{2,1,0:T(8,128)S(1)} %collective-permute-done.17.refs_0_), custom_call_target="tpu_custom_call" | custom-call | tf_op jit(solution)/shard_map/pick/pallas_call | solution.py:143
  124.9 1.5 copy-done.1
  126.3 1.4 collective-permute-done.22.refs_8_
  128.1 2.3 %collective-permute-done.23.refs_13_ = f32[128,16,128]{2,1,0:T(8,128)S(1)} collective-permute-done((f32[128,16,128]{2,1,0:T(8,128)S(1)}, f32[128,16,128]{2,1,0:T(8,128)S(1)}, u32[]{:S(2)}, u32[]{:S(2)}) %collective-permute-start.23) | collective-permute-done | bytes 1048608 | tf_op jit(solution)/shard_map/ppermute | solution.py:317
  130.4 17.0 %leaf_field_product.1 = f32[64,8192]{1,0:T(8,128)} custom-call(s32[128,16]{1,0:T(8,128)S(1)} %copy-done.21, s32[32,128]{1,0:T(8,128)S(1)} %get-tuple-element.149.code_ref, bf16[320,32,128]{2,1,0:T(8,128)(2,1)} %copy-done.2, bf16[320,32,128]{2,1,0:T(8,128)(2,1)} %copy-done.3, bf16[384,32,128]{2,1,0:T(8,128)(2,1)} %copy-done, bf16[384,32,128]{2,1,0:T(8,128)(2,1)} %copy-done.1, ...), custom_call_target="tpu_custom_call" | custom-call | tf_op jit(solution)/shard_map/leaf_field_product/pallas_call | solution.py:273
  (77 shorter events, 3.3 us)
Async XLA Ops:
  1.2 1.6 %copy-start.14 = (f32[64,8192]{1,0:T(8,128)S(1)}, f32[64,8192]{1,0:T(8,128)}, u32[]{:S(2)}) copy-start(f32[64,8192]{1,0:T(8,128)} %vectors_ref.1) | copy-start | bytes 6291460
  2.8 11.9 %copy-start.25 = (f32[128,1024]{1,0:T(8,128)S(1)}, f32[128,1024]{1,0:T(8,128)}, u32[]{:S(2)}) copy-start(f32[128,1024]{1,0:T(8,128)} %param.11) | copy-start | bytes 1572868
  2.8 18.4 %copy-start.26 = (s32[128,16]{0,1:T(8,128)S(1)}, s32[128,16]{0,1:T(8,128)}, u32[]{:S(2)}) copy-start(s32[128,16]{0,1:T(8,128)} %param.13) | copy-start | bytes 24580
  2.8 18.5 %copy-start.27 = (s32[128,16]{0,1:T(8,128)S(1)}, s32[128,16]{0,1:T(8,128)}, u32[]{:S(2)}) copy-start(s32[128,16]{0,1:T(8,128)} %param.14) | copy-start | bytes 24580
  6.7 12.0 %collective-permute-start.4 = (f32[128,16,128]{2,1,0:T(8,128)}, f32[128,16,128]{2,1,0:T(8,128)}, u32[]{:S(2)}, u32[]{:S(2)}) collective-permute-start(f32[128,16,128]{2,1,0:T(8,128)} %get-tuple-element.83.refs_0_), channel_id=1, source_target_pairs={{0,1},{1,0},{2,3},{3,2},{4,5},{5,4},{6,7},{7,6},{8,9},{9,8},{10,11... | collective-permute-start | bytes 3145736 | tf_op jit(solution)/shard_map/ppermute | solution.py:327
  8.1 26.5 %collective-permute-start = (f32[128,16,128]{2,1,0:T(8,128)}, f32[128,16,128]{2,1,0:T(8,128)S(1)}, u32[]{:S(2)}, u32[]{:S(2)}) collective-permute-start(f32[128,16,128]{2,1,0:T(8,128)} %get-tuple-element.83.refs_0_), channel_id=1, source_target_pairs={{0,2},{1,3},{2,4},{3,5},{4,6},{5,7},{6,0},{7,1},{8,10},{9,11},{10,... | collective-permute-start | bytes 3145736 | tf_op jit(solution)/shard_map/ppermute | solution.py:317
  9.5 25.1 %collective-permute-start.1 = (f32[128,16,128]{2,1,0:T(8,128)}, f32[128,16,128]{2,1,0:T(8,128)S(1)}, u32[]{:S(2)}, u32[]{:S(2)}) collective-permute-start(f32[128,16,128]{2,1,0:T(8,128)} %get-tuple-element.83.refs_0_), channel_id=1, source_target_pairs={{0,6},{1,7},{2,0},{3,1},{4,2},{5,3},{6,4},{7,5},{8,14},{9,15},{10,... | collective-permute-start | bytes 3145736 | tf_op jit(solution)/shard_map/ppermute | solution.py:317
  10.9 27.2 %collective-permute-start.2 = (f32[128,16,128]{2,1,0:T(8,128)}, f32[128,16,128]{2,1,0:T(8,128)}, u32[]{:S(2)}, u32[]{:S(2)}) collective-permute-start(f32[128,16,128]{2,1,0:T(8,128)} %get-tuple-element.83.refs_0_), channel_id=1, source_target_pairs={{0,8},{1,9},{2,10},{3,11},{4,12},{5,13},{6,14},{7,15},{8,16},{9,17... | collective-permute-start | bytes 3145736 | tf_op jit(solution)/shard_map/ppermute | solution.py:317
  12.6 25.5 %collective-permute-start.3 = (f32[128,16,128]{2,1,0:T(8,128)}, f32[128,16,128]{2,1,0:T(8,128)}, u32[]{:S(2)}, u32[]{:S(2)}) collective-permute-start(f32[128,16,128]{2,1,0:T(8,128)} %get-tuple-element.83.refs_0_), channel_id=1, source_target_pairs={{0,24},{1,25},{2,26},{3,27},{4,28},{5,29},{6,30},{7,31},{8,0},{9,1... | collective-permute-start | bytes 3145736 | tf_op jit(solution)/shard_map/ppermute | solution.py:317
  14.8 28.0 %copy-start.4 = (f32[1024,128]{1,0:T(8,128)}, f32[1024,128]{1,0:T(8,128)S(1)}, u32[]{:S(2)}) copy-start(f32[1024,128]{1,0:T(8,128)S(1)} %reshape.3.transfer_ref.refs_5_) | copy-start | bytes 1572868
  14.8 1.4 copy-start.17
  18.7 7.3 %collective-permute-start.5 = (f32[16,16,128]{2,1,0:T(8,128)S(1)}, f32[16,16,128]{2,1,0:T(8,128)S(1)}, u32[]{:S(2)}, u32[]{:S(2)}) collective-permute-start(f32[16,16,128]{2,1,0:T(8,128)S(1)} %parent_coef.1.refs_0_), channel_id=1, source_target_pairs={{0,96},{32,0},{64,32},{96,64},{1,97},{33,1},{65,33},{97,65},{2,98}... | collective-permute-start | bytes 393224 | tf_op jit(solution)/shard_map/ppermute | solution.py:327
  26.0 16.8 %copy-start.20 = (s32[128,16]{1,0:T(8,128)}, s32[128,16]{1,0:T(8,128)S(1)}, u32[]{:S(2)}) copy-start(s32[128,16]{1,0:T(8,128)S(1)} %get-tuple-element.148.pos_ref) | copy-start | bytes 24580
  26.0 5.4 %collective-permute-start.6 = (f32[16,16,128]{2,1,0:T(8,128)S(1)}, f32[16,16,128]{2,1,0:T(8,128)S(1)}, u32[]{:S(2)}, u32[]{:S(2)}) collective-permute-start(f32[16,16,128]{2,1,0:T(8,128)S(1)} %parent_coef.1.refs_0_), channel_id=1, source_target_pairs={{0,64},{32,96},{64,0},{96,32},{1,65},{33,97},{65,1},{97,33},{2,66}... | collective-permute-start | bytes 393224 | tf_op jit(solution)/shard_map/ppermute | solution.py:327
  31.4 11.4 %collective-permute-start.7 = (f32[16,16,128]{2,1,0:T(8,128)S(1)}, f32[16,16,128]{2,1,0:T(8,128)S(1)}, u32[]{:S(2)}, u32[]{:S(2)}) collective-permute-start(f32[16,16,128]{2,1,0:T(8,128)S(1)} %parent_coef.1.refs_0_), channel_id=1, source_target_pairs={{0,32},{32,64},{64,96},{96,0},{1,33},{33,65},{65,97},{97,1},{2,34}... | collective-permute-start | bytes 393224 | tf_op jit(solution)/shard_map/ppermute | solution.py:327
  34.6 8.2 %copy-start.8 = (f32[128,16,128]{2,1,0:T(8,128)}, f32[128,16,128]{2,1,0:T(8,128)S(1)}, u32[]{:S(2)}) copy-start(f32[128,16,128]{2,1,0:T(8,128)S(1)} %collective-permute-done.refs_1_.refs_0_.refs_2_) | copy-start | bytes 3145732
  34.6 8.2 %copy-start.11 = (f32[128,16,128]{2,1,0:T(8,128)}, f32[128,16,128]{2,1,0:T(8,128)S(1)}, u32[]{:S(2)}) copy-start(f32[128,16,128]{2,1,0:T(8,128)S(1)} %collective-permute-done.1.refs_0_.refs_1_) | copy-start | bytes 3145732
  43.5 36.4 %collective-permute-start.10 = (f32[192,16,128]{2,1,0:T(8,128)}, f32[192,16,128]{2,1,0:T(8,128)S(1)}, u32[]{:S(2)}, u32[]{:S(2)}) collective-permute-start(f32[192,16,128]{2,1,0:T(8,128)} %get-tuple-element.96), channel_id=1, source_target_pairs={{0,2},{1,3},{2,4},{3,5},{4,6},{5,7},{6,0},{7,1},{8,10},{9,11},{10,... | collective-permute-start | bytes 4718600 | tf_op jit(solution)/shard_map/ppermute | solution.py:317
  43.5 36.4 %collective-permute-start.11 = (f32[192,16,128]{2,1,0:T(8,128)}, f32[192,16,128]{2,1,0:T(8,128)S(1)}, u32[]{:S(2)}, u32[]{:S(2)}) collective-permute-start(f32[192,16,128]{2,1,0:T(8,128)} %get-tuple-element.97), channel_id=1, source_target_pairs={{0,6},{1,7},{2,0},{3,1},{4,2},{5,3},{6,4},{7,5},{8,14},{9,15},{10,... | collective-permute-start | bytes 4718600 | tf_op jit(solution)/shard_map/ppermute | solution.py:317
  46.2 35.8 %collective-permute-start.8 = (f32[192,16,128]{2,1,0:T(8,128)}, f32[192,16,128]{2,1,0:T(8,128)}, u32[]{:S(2)}, u32[]{:S(2)}) collective-permute-start(f32[192,16,128]{2,1,0:T(8,128)} %get-tuple-element.94), channel_id=1, source_target_pairs={{0,8},{1,9},{2,10},{3,11},{4,12},{5,13},{6,14},{7,15},{8,16},{9,17... | collective-permute-start | bytes 4718600 | tf_op jit(solution)/shard_map/ppermute | solution.py:317
  46.5 35.5 %collective-permute-start.9 = (f32[192,16,128]{2,1,0:T(8,128)}, f32[192,16,128]{2,1,0:T(8,128)}, u32[]{:S(2)}, u32[]{:S(2)}) collective-permute-start(f32[192,16,128]{2,1,0:T(8,128)} %get-tuple-element.95), channel_id=1, source_target_pairs={{0,24},{1,25},{2,26},{3,27},{4,28},{5,29},{6,30},{7,31},{8,0},{9,1... | collective-permute-start | bytes 4718600 | tf_op jit(solution)/shard_map/ppermute | solution.py:317
  48.8 1.2 copy-start.9
  51.3 2.0 %copy-start.10 = (f32[128,16,128]{2,1,0:T(8,128)S(1)}, f32[128,16,128]{2,1,0:T(8,128)}, u32[]{:S(2)}) copy-start(f32[128,16,128]{2,1,0:T(8,128)} %copy-done.8) | copy-start | bytes 3145732
  51.3 2.2 %copy-start.13 = (f32[128,16,128]{2,1,0:T(8,128)S(1)}, f32[128,16,128]{2,1,0:T(8,128)}, u32[]{:S(2)}) copy-start(f32[128,16,128]{2,1,0:T(8,128)} %copy-done.11) | copy-start | bytes 3145732
  53.5 7.9 %copy-start.5 = (f32[1024,128]{1,0:T(8,128)S(1)}, f32[1024,128]{1,0:T(8,128)}, u32[]{:S(2)}) copy-start(f32[1024,128]{1,0:T(8,128)} %copy-done.4) | copy-start | bytes 1572868
  53.5 7.9 %copy-start.15 = (f32[16,32,1024]{2,1,0:T(8,128)S(1)}, f32[16,32,1024]{2,1,0:T(8,128)}, u32[]{:S(2)}) copy-start(f32[16,32,1024]{2,1,0:T(8,128)} %refs_4_.1) | copy-start | bytes 6291460
  53.5 7.9 %copy-start.19 = (f32[16,16,128]{2,1,0:T(8,128)S(1)}, f32[16,16,128]{2,1,0:T(8,128)}, u32[]{:S(2)}) copy-start(f32[16,16,128]{2,1,0:T(8,128)} %copy-done.18) | copy-start | bytes 393220
  53.5 7.9 %copy-start.22 = (s32[16,32]{1,0:T(8,128)S(1)}, s32[16,32]{1,0:T(8,128)}, u32[]{:S(2)}) copy-start(s32[16,32]{1,0:T(8,128)} %list_ref.2) | copy-start | bytes 6148
  53.5 7.9 %copy-start.23 = (s32[16,32]{1,0:T(8,128)S(1)}, s32[16,32]{1,0:T(8,128)}, u32[]{:S(2)}) copy-start(s32[16,32]{1,0:T(8,128)} %mask_ref.2) | copy-start | bytes 6148
  57.5 1.6 %copy-start.2 = (bf16[320,32,128]{2,1,0:T(8,128)(2,1)}, bf16[320,32,128]{2,1,0:T(8,128)(2,1)S(1)}, u32[]{:S(2)}) copy-start(bf16[320,32,128]{2,1,0:T(8,128)(2,1)S(1)} %pick.4.refs_0_) | copy-start | bytes 7864324
  59.2 24.7 %collective-permute-start.12 = (f32[512,16,128]{2,1,0:T(8,128)S(1)}, f32[512,16,128]{2,1,0:T(8,128)S(1)}, u32[]{:S(2)}, u32[]{:S(2)}) collective-permute-start(f32[512,16,128]{2,1,0:T(8,128)S(1)} %pack.9), channel_id=1, source_target_pairs={{0,1},{1,0},{2,3},{3,2},{4,5},{5,4},{6,7},{7,6},{8,9},{9,8},{10,11... | collective-permute-start | bytes 12582920 | tf_op jit(solution)/shard_map/ppermute | solution.py:327
  83.9 23.4 %collective-permute-start.13 = (f32[128,16,128]{2,1,0:T(8,128)S(1)}, f32[128,16,128]{2,1,0:T(8,128)S(1)}, u32[]{:S(2)}, u32[]{:S(2)}) collective-permute-start(f32[128,16,128]{2,1,0:T(8,128)S(1)} %get-tuple-element.113), channel_id=1, source_target_pairs={{0,8},{1,9},{2,10},{3,11},{4,12},{5,13},{6,14},{7,15},{8,16},{9,17... | collective-permute-start | bytes 3145736 | tf_op jit(solution)/shard_map/ppermute | solution.py:317
  84.0 23.3 %collective-permute-start.14 = (f32[128,16,128]{2,1,0:T(8,128)S(1)}, f32[128,16,128]{2,1,0:T(8,128)S(1)}, u32[]{:S(2)}, u32[]{:S(2)}) collective-permute-start(f32[128,16,128]{2,1,0:T(8,128)S(1)} %get-tuple-element.114), channel_id=1, source_target_pairs={{0,24},{1,25},{2,26},{3,27},{4,28},{5,29},{6,30},{7,31},{8,0},{9,1... | collective-permute-start | bytes 3145736 | tf_op jit(solution)/shard_map/ppermute | solution.py:317
  86.6 22.8 %collective-permute-start.15 = (f32[128,16,128]{2,1,0:T(8,128)S(1)}, f32[128,16,128]{2,1,0:T(8,128)S(1)}, u32[]{:S(2)}, u32[]{:S(2)}) collective-permute-start(f32[128,16,128]{2,1,0:T(8,128)S(1)} %get-tuple-element.115), channel_id=1, source_target_pairs={{0,2},{1,3},{2,4},{3,5},{4,6},{5,7},{6,0},{7,1},{8,10},{9,11},{10,... | collective-permute-start | bytes 3145736 | tf_op jit(solution)/shard_map/ppermute | solution.py:317
  86.6 22.8 %collective-permute-start.16 = (f32[128,16,128]{2,1,0:T(8,128)S(1)}, f32[128,16,128]{2,1,0:T(8,128)S(1)}, u32[]{:S(2)}, u32[]{:S(2)}) collective-permute-start(f32[128,16,128]{2,1,0:T(8,128)S(1)} %get-tuple-element.116), channel_id=1, source_target_pairs={{0,6},{1,7},{2,0},{3,1},{4,2},{5,3},{6,4},{7,5},{8,14},{9,15},{10,... | collective-permute-start | bytes 3145736 | tf_op jit(solution)/shard_map/ppermute | solution.py:317
  95.8 1.6 %copy-start = (bf16[384,32,128]{2,1,0:T(8,128)(2,1)}, bf16[384,32,128]{2,1,0:T(8,128)(2,1)S(1)}, u32[]{:S(2)}) copy-start(bf16[384,32,128]{2,1,0:T(8,128)(2,1)S(1)} %pick.6.refs_2_) | copy-start | bytes 9437188
  97.5 13.4 %collective-permute-start.17 = (f32[768,16,128]{2,1,0:T(8,128)S(1)}, f32[768,16,128]{2,1,0:T(8,128)S(1)}, u32[]{:S(2)}, u32[]{:S(2)}) collective-permute-start(f32[768,16,128]{2,1,0:T(8,128)S(1)} %pack.11), channel_id=1, source_target_pairs={{0,1},{1,0},{2,3},{3,2},{4,5},{5,4},{6,7},{7,6},{8,9},{9,8},{10,11... | collective-permute-start | bytes 18874376 | tf_op jit(solution)/shard_map/ppermute | solution.py:327
  105.1 4.5 %copy-start.3 = (bf16[320,32,128]{2,1,0:T(8,128)(2,1)}, bf16[320,32,128]{2,1,0:T(8,128)(2,1)S(1)}, u32[]{:S(2)}) copy-start(bf16[320,32,128]{2,1,0:T(8,128)(2,1)S(1)} %pick.5.refs_1_) | copy-start | bytes 7864324
  110.9 13.7 %collective-permute-start.18 = (f32[32,16,128]{2,1,0:T(8,128)S(1)}, f32[32,16,128]{2,1,0:T(8,128)S(1)}, u32[]{:S(2)}, u32[]{:S(2)}) collective-permute-start(f32[32,16,128]{2,1,0:T(8,128)S(1)} %get-tuple-element.132), channel_id=1, source_target_pairs={{0,8},{1,9},{2,10},{3,11},{4,12},{5,13},{6,14},{7,15},{8,16},{9,17... | collective-permute-start | bytes 786440 | tf_op jit(solution)/shard_map/ppermute | solution.py:317
  110.9 13.7 %collective-permute-start.19 = (f32[32,16,128]{2,1,0:T(8,128)S(1)}, f32[32,16,128]{2,1,0:T(8,128)S(1)}, u32[]{:S(2)}, u32[]{:S(2)}) collective-permute-start(f32[32,16,128]{2,1,0:T(8,128)S(1)} %get-tuple-element.133), channel_id=1, source_target_pairs={{0,24},{1,25},{2,26},{3,27},{4,28},{5,29},{6,30},{7,31},{8,0},{9,1... | collective-permute-start | bytes 786440 | tf_op jit(solution)/shard_map/ppermute | solution.py:317
  113.6 11.0 %collective-permute-start.20 = (f32[32,16,128]{2,1,0:T(8,128)S(1)}, f32[32,16,128]{2,1,0:T(8,128)S(1)}, u32[]{:S(2)}, u32[]{:S(2)}) collective-permute-start(f32[32,16,128]{2,1,0:T(8,128)S(1)} %get-tuple-element.134), channel_id=1, source_target_pairs={{0,2},{1,3},{2,4},{3,5},{4,6},{5,7},{6,0},{7,1},{8,10},{9,11},{10,... | collective-permute-start | bytes 786440 | tf_op jit(solution)/shard_map/ppermute | solution.py:317
  113.6 11.1 %collective-permute-start.21 = (f32[32,16,128]{2,1,0:T(8,128)S(1)}, f32[32,16,128]{2,1,0:T(8,128)S(1)}, u32[]{:S(2)}, u32[]{:S(2)}) collective-permute-start(f32[32,16,128]{2,1,0:T(8,128)S(1)} %get-tuple-element.135), channel_id=1, source_target_pairs={{0,6},{1,7},{2,0},{3,1},{4,2},{5,3},{6,4},{7,5},{8,14},{9,15},{10,... | collective-permute-start | bytes 786440 | tf_op jit(solution)/shard_map/ppermute | solution.py:317
  116.9 10.8 %collective-permute-start.22 = (f32[512,16,128]{2,1,0:T(8,128)S(1)}, f32[512,16,128]{2,1,0:T(8,128)S(1)}, u32[]{:S(2)}, u32[]{:S(2)}) collective-permute-start(f32[512,16,128]{2,1,0:T(8,128)S(1)} %pack.13), channel_id=1, source_target_pairs={{0,1},{1,0},{2,3},{3,2},{4,5},{5,4},{6,7},{7,6},{8,9},{9,8},{10,11... | collective-permute-start | bytes 12582920 | tf_op jit(solution)/shard_map/ppermute | solution.py:327
  124.6 1.8 %copy-start.1 = (bf16[384,32,128]{2,1,0:T(8,128)(2,1)}, bf16[384,32,128]{2,1,0:T(8,128)(2,1)S(1)}, u32[]{:S(2)}) copy-start(bf16[384,32,128]{2,1,0:T(8,128)(2,1)S(1)} %pick.7.refs_3_) | copy-start | bytes 9437188
  124.6 5.8 %copy-start.7 = (f32[32,8192]{1,0:T(8,128)S(1)}, f32[32,8192]{1,0:T(8,128)}, u32[]{:S(2)}) copy-start(f32[32,8192]{1,0:T(8,128)} %refs_16_.1) | copy-start | bytes 3145732
  124.6 5.8 %copy-start.21 = (s32[128,16]{1,0:T(8,128)S(1)}, s32[128,16]{1,0:T(8,128)}, u32[]{:S(2)}) copy-start(s32[128,16]{1,0:T(8,128)} %copy-done.20) | copy-start | bytes 24580
  127.7 2.7 %copy-start.24 = (f32[512,16,128]{2,1,0:T(8,128)}, f32[512,16,128]{2,1,0:T(8,128)S(1)}, u32[]{:S(2)}) copy-start(f32[512,16,128]{2,1,0:T(8,128)S(1)} %collective-permute-done.22.refs_8_) | copy-start | bytes 12582916
  127.7 2.7 %collective-permute-start.23 = (f32[128,16,128]{2,1,0:T(8,128)S(1)}, f32[128,16,128]{2,1,0:T(8,128)S(1)}, u32[]{:S(2)}, u32[]{:S(2)}) collective-permute-start(f32[128,16,128]{2,1,0:T(8,128)S(1)} %pack.12), channel_id=1, source_target_pairs={{0,1},{1,0},{2,3},{3,2},{4,5},{5,4},{6,7},{7,6},{8,9},{9,8},{10,11... | collective-permute-start | bytes 3145736 | tf_op jit(solution)/shard_map/ppermute | solution.py:317
  (4 other events, 4.1 us)

commit v4 on v3

--- a/solution.py
+++ b/solution.py
@@ -20,8 +20,9 @@
 BRANCHES = 4
 
 BRIEF = pl.CostEstimate(flops=0, bytes_accessed=0, transcendentals=0)
-FINAL_LIMIT = 44 * 2**20
-SMALL_LIMIT = 20 * 2**20
+FINAL_LIMIT = 36 * 2**20
+SMALL_LIMIT = 12 * 2**20
+WHOLE_LIMIT = 60 * 2**20
 LONG = pl.CostEstimate(flops=10**11, bytes_accessed=10**9, transcendentals=0)
 
 CROSS = [(0, 0)]
@@ -86,7 +87,7 @@
             pl.BlockSpec((block, TILE, LANES), lambda i: (i, 0, 0)),
             pl.BlockSpec((block // 2, K, LANES), lambda i: (i, 0, 0)),
         ),
-        compiler_params=pltpu.CompilerParams(vmem_limit_bytes=SMALL_LIMIT),
+        compiler_params=pltpu.CompilerParams(vmem_limit_bytes=WHOLE_LIMIT),
         name="leaf_coef",
     )(basis, vectors)
 
@@ -652,8 +653,9 @@
     pieces, ((pos, codes), down, tiles) = ring(
         coef, leaf_count, turns, [beside_first, beside_second, beside_third, beside_fourth]
     )
-    late = ORDER[2 * (len(STAGES[0]) + len(STAGES[1])) :]
-    return products(pos, codes, tiles, late, pieces, leaf_coupling, down, basis, 16)
+    tiles = tiles + [pick(2, (0,), codes, pieces)]
+    late = ORDER[2 * (len(STAGES[0]) + len(STAGES[1])) + len(STAGES[2]) :]
+    return products(pos, codes, tiles, late, pieces, leaf_coupling, down, basis, 32)
 
 
 def solution(mesh):

time: 148 us -> 141 us (0.953)
  local copies, waits for them, and re-layouts: 13.7 us -> 5.46 us
  Pallas kernels: 69.2 us -> 67.5 us
  starting transfers between devices: 37.5 us -> 39.1 us
    unnamed x58 -> x46, local copies, waits for them, and re-layouts: 13.5 us -> 5.26 us
    pallas_call x1, Pallas kernels: 17 us -> 12.3 us  [products(): pl.pallas_call(functools.partial(field_kernel, slots, block, plan, len(ti...]
    pallas_call x4 -> x5, Pallas kernels: 15.9 us -> 17.6 us  [picked_slots(): pl.pallas_call(functools.partial(pick_kernel, plan, first), out_shape=jax...]
    ppermute x7, starting transfers between devices: 14.4 us -> 16 us  [__call__(): self.last = lax.ppermute(array, axis, perm)]
  transfers between devices with their start and end apart: 24 -> 24, of which waited for: 10 -> 8; matrix products, arithmetic and copies ran while one was open for 0% -> 0% of each run, Pallas kernels for 33% -> 36%
where the time goes in v4:
time: 141 us
  Pallas kernels  67.5 us (48%)
  starting transfers between devices  39.1 us (28%)
  waiting for transfers between devices  28.1 us (20%)
  local copies, waits for them, and re-layouts  5.46 us (4%)
    ppermute x17, starting transfers between devices, moved(): return (send(array, 'subtree', perm), out)  23.2 us
    ppermute x17, waiting for transfers between devices, moved(): return (send(array, 'subtree', perm), out)  20.4 us
    pallas_call x5, Pallas kernels, picked_slots(): pl.pallas_call(functools.partial(pick_kernel, plan, first), out_shape=jax...  17.6 us
    ppermute x7, starting transfers between devices, __call__(): self.last = lax.ppermute(array, axis, perm)  16 us
    pallas_call x1, Pallas kernels, downward_pairs(): pl.pallas_call(functools.partial(parent_field_kernel, group), out_shape=j...  14.6 us
    pallas_call x1, Pallas kernels, products(): pl.pallas_call(functools.partial(field_kernel, slots, block, plan, len(ti...  12.3 us
    pallas_call x7, Pallas kernels, packed(): pl.pallas_call(functools.partial(pack_kernel, plan, len(arrays)), out_sha...  11.8 us
    ppermute x7, waiting for transfers between devices, __call__(): self.last = lax.ppermute(array, axis, perm)  7.68 us
  transfers between devices with their start and end apart: 24, of which 8 were waited for; matrix products, arithmetic and copies ran while one was open for 0% of the time, Pallas kernels for 36%

profile of v4, /device:TPU:1, one launch (start us, length us, event | category | flops | bytes accessed | tf_op | source)
XLA Modules:
  0.0 140.7 jit_solution(5167667064752028879)
XLA Ops:
  0.0 4.3 %leaf_coef.1 = (f32[128,16,128]{2,1,0:T(8,128)}, f32[64,32,128]{2,1,0:T(8,128)}) custom-call(f32[32,8192]{1,0:T(8,128)} %refs_13_.1, f32[64,8192]{1,0:T(8,128)} %vectors_ref.1), custom_call_target="tpu_custom_call" | custom-call | tf_op jit(solution)/shard_map/leaf_coef/pallas_call | solution.py:75
  4.3 1.5 %collective-permute-start.4 = (f32[128,16,128]{2,1,0:T(8,128)}, f32[128,16,128]{2,1,0:T(8,128)}, u32[]{:S(2)}, u32[]{:S(2)}) collective-permute-start(f32[128,16,128]{2,1,0:T(8,128)} %get-tuple-element.83.refs_0_), channel_id=1, source_target_pairs={{0,1},{1,0},{2,3},{3,2},{4,5},{5,4},{6,7},{7,6},{8,9},{9,8},{10,11... | collective-permute-start | bytes 3145736 | tf_op jit(solution)/shard_map/ppermute | solution.py:328
  5.8 1.4 %collective-permute-start = (f32[128,16,128]{2,1,0:T(8,128)}, f32[128,16,128]{2,1,0:T(8,128)S(1)}, u32[]{:S(2)}, u32[]{:S(2)}) collective-permute-start(f32[128,16,128]{2,1,0:T(8,128)} %get-tuple-element.83.refs_0_), channel_id=1, source_target_pairs={{0,2},{1,3},{2,4},{3,5},{4,6},{5,7},{6,0},{7,1},{8,10},{9,11},{10,... | collective-permute-start | bytes 3145736 | tf_op jit(solution)/shard_map/ppermute | solution.py:318
  7.2 1.4 %collective-permute-start.1 = (f32[128,16,128]{2,1,0:T(8,128)}, f32[128,16,128]{2,1,0:T(8,128)S(1)}, u32[]{:S(2)}, u32[]{:S(2)}) collective-permute-start(f32[128,16,128]{2,1,0:T(8,128)} %get-tuple-element.83.refs_0_), channel_id=1, source_target_pairs={{0,6},{1,7},{2,0},{3,1},{4,2},{5,3},{6,4},{7,5},{8,14},{9,15},{10,... | collective-permute-start | bytes 3145736 | tf_op jit(solution)/shard_map/ppermute | solution.py:318
  8.6 1.6 %collective-permute-start.2 = (f32[128,16,128]{2,1,0:T(8,128)}, f32[128,16,128]{2,1,0:T(8,128)}, u32[]{:S(2)}, u32[]{:S(2)}) collective-permute-start(f32[128,16,128]{2,1,0:T(8,128)} %get-tuple-element.83.refs_0_), channel_id=1, source_target_pairs={{0,8},{1,9},{2,10},{3,11},{4,12},{5,13},{6,14},{7,15},{8,16},{9,17... | collective-permute-start | bytes 3145736 | tf_op jit(solution)/shard_map/ppermute | solution.py:318
  10.2 2.1 %collective-permute-start.3 = (f32[128,16,128]{2,1,0:T(8,128)}, f32[128,16,128]{2,1,0:T(8,128)}, u32[]{:S(2)}, u32[]{:S(2)}) collective-permute-start(f32[128,16,128]{2,1,0:T(8,128)} %get-tuple-element.83.refs_0_), channel_id=1, source_target_pairs={{0,24},{1,25},{2,26},{3,27},{4,28},{5,29},{6,30},{7,31},{8,0},{9,1... | collective-permute-start | bytes 3145736 | tf_op jit(solution)/shard_map/ppermute | solution.py:318
  12.5 1.4 copy-done.11
  13.9 2.5 %parent_coef.1.refs_0_ = f32[16,16,128]{2,1,0:T(8,128)S(1)} custom-call(f32[64,32,128]{2,1,0:T(8,128)S(1)} %copy-done.11, f32[1024,128]{1,0:T(8,128)S(1)} %reshape.3.transfer_ref.refs_5_), custom_call_target="tpu_custom_call" | custom-call | tf_op jit(solution)/shard_map/parent_coef/pallas_call | solution.py:509
  16.3 2.5 %collective-permute-start.5 = (f32[16,16,128]{2,1,0:T(8,128)S(1)}, f32[16,16,128]{2,1,0:T(8,128)S(1)}, u32[]{:S(2)}, u32[]{:S(2)}) collective-permute-start(f32[16,16,128]{2,1,0:T(8,128)S(1)} %parent_coef.1.refs_0_), channel_id=1, source_target_pairs={{0,96},{32,0},{64,32},{96,64},{1,97},{33,1},{65,33},{97,65},{2,98}... | collective-permute-start | bytes 393224 | tf_op jit(solution)/shard_map/ppermute | solution.py:328
  19.2 4.4 %slot_order.1 = (s32[128,16]{1,0:T(8,128)S(1)}, s32[32,128]{1,0:T(8,128)S(1)}) custom-call(s32[1,128]{1,0:T(1,128)S(1)} %pad_bitcast_fusion.own_ref, s32[128,16]{1,0:T(8,128)S(1)} %copy.10.list_ref, s32[128,16]{1,0:T(8,128)S(1)} %copy.11.mask_ref), custom_call_target="tpu_custom_call" | custom-call | tf_op jit(solution)/shard_map/slot_order/pallas_call | solution.py:465
  23.7 0.6 collective-permute-start.6
  24.3 4.8 %collective-permute-done.6.refs_2_ = f32[16,16,128]{2,1,0:T(8,128)S(1)} collective-permute-done((f32[16,16,128]{2,1,0:T(8,128)S(1)}, f32[16,16,128]{2,1,0:T(8,128)S(1)}, u32[]{:S(2)}, u32[]{:S(2)}) %collective-permute-start.6) | collective-permute-done | bytes 131104 | tf_op jit(solution)/shard_map/ppermute | solution.py:328
  29.1 3.2 %collective-permute-done.refs_1_.refs_0_.refs_2_ = f32[128,16,128]{2,1,0:T(8,128)S(1)} collective-permute-done((f32[128,16,128]{2,1,0:T(8,128)}, f32[128,16,128]{2,1,0:T(8,128)S(1)}, u32[]{:S(2)}, u32[]{:S(2)}) %collective-permute-start) | collective-permute-done | bytes 1048608 | tf_op jit(solution)/shard_map/ppermute | solution.py:318
  32.3 3.4 %collective-permute-done.2.refs_2_.refs_4_ = f32[128,16,128]{2,1,0:T(8,128)} collective-permute-done((f32[128,16,128]{2,1,0:T(8,128)}, f32[128,16,128]{2,1,0:T(8,128)}, u32[]{:S(2)}, u32[]{:S(2)}) %collective-permute-start.2) | collective-permute-done | bytes 1048608 | tf_op jit(solution)/shard_map/ppermute | solution.py:318
  35.7 4.6 %pack.7 = (f32[192,16,128]{2,1,0:T(8,128)}, f32[192,16,128]{2,1,0:T(8,128)}, f32[192,16,128]{2,1,0:T(8,128)}, f32[192,16,128]{2,1,0:T(8,128)}) custom-call(f32[128,16,128]{2,1,0:T(8,128)S(1)} %collective-permute-done.1.refs_0_.refs_1_, f32[128,16,128]{2,1,0:T(8,128)S(1)} %collective-permute-done.refs_1_.refs_0_.refs_2_, ...), custom_call_target="tpu_custom_call" | custom-call | flops 99999997952 | bytes 1000000000 | tf_op jit(solution)/shard_map/pack/pallas_call | solution.py:368
  40.4 0.6 copy-done.12
  41.0 2.7 %collective-permute-start.11 = (f32[192,16,128]{2,1,0:T(8,128)}, f32[192,16,128]{2,1,0:T(8,128)S(1)}, u32[]{:S(2)}, u32[]{:S(2)}) collective-permute-start(f32[192,16,128]{2,1,0:T(8,128)} %get-tuple-element.97), channel_id=1, source_target_pairs={{0,6},{1,7},{2,0},{3,1},{4,2},{5,3},{6,4},{7,5},{8,14},{9,15},{10,... | collective-permute-start | bytes 4718600 | tf_op jit(solution)/shard_map/ppermute | solution.py:318
  43.7 0.3 collective-permute-start.8
  44.0 2.4 %collective-permute-start.9 = (f32[192,16,128]{2,1,0:T(8,128)}, f32[192,16,128]{2,1,0:T(8,128)}, u32[]{:S(2)}, u32[]{:S(2)}) collective-permute-start(f32[192,16,128]{2,1,0:T(8,128)} %get-tuple-element.95), channel_id=1, source_target_pairs={{0,24},{1,25},{2,26},{3,27},{4,28},{5,29},{6,30},{7,31},{8,0},{9,1... | collective-permute-start | bytes 4718600 | tf_op jit(solution)/shard_map/ppermute | solution.py:318
  46.4 1.2 copy-done.4
  47.6 1.2 copy-done.7
  48.8 2.0 %pack.9 = f32[512,16,128]{2,1,0:T(8,128)S(1)} custom-call(f32[128,16,128]{2,1,0:T(8,128)S(1)} %copy-done.4, f32[128,16,128]{2,1,0:T(8,128)S(1)} %copy-done.7, f32[128,16,128]{2,1,0:T(8,128)} %collective-permute-done.2.refs_2_.refs_4_, f32[128,16,128]{2,1,0:T(8,128)} %collective-permute-done.3.refs_3_), custom_call_target="tpu_custom_call" | custom-call | tf_op jit(solution)/shard_map/pack/pallas_call | solution.py:368
  51.0 0.3 copy-done.10
  51.3 3.1 %pick.5.refs_0_ = bf16[320,32,128]{2,1,0:T(8,128)(2,1)S(1)} custom-call(s32[32,128]{1,0:T(8,128)S(1)} %get-tuple-element.149.code_ref, f32[128,16,128]{2,1,0:T(8,128)S(1)} %copy-done.10, f32[128,16,128]{2,1,0:T(8,128)S(1)} %copy-done.8, f32[128,16,128]{2,1,0:T(8,128)S(1)} %copy-done.5, f32[128,16,128]{2,1,0:T(8,128)} %collective-permute-done.3.refs_3_, ...), custom_call_target="tpu_custom_call" | custom-call | tf_op jit(solution)/shard_map/pick/pallas_call | solution.py:144
  54.4 2.3 %collective-permute-start.12 = (f32[512,16,128]{2,1,0:T(8,128)S(1)}, f32[512,16,128]{2,1,0:T(8,128)S(1)}, u32[]{:S(2)}, u32[]{:S(2)}) collective-permute-start(f32[512,16,128]{2,1,0:T(8,128)S(1)} %pack.9), channel_id=1, source_target_pairs={{0,1},{1,0},{2,3},{3,2},{4,5},{5,4},{6,7},{7,6},{8,9},{9,8},{10,11... | collective-permute-start | bytes 12582920 | tf_op jit(solution)/shard_map/ppermute | solution.py:328
  56.7 14.6 %parent_field.1.refs_12_ = f32[64,32,128]{2,1,0:T(8,128)S(1)} custom-call(s32[16,32]{1,0:T(8,128)S(1)} %copy-done.16, s32[16,32]{1,0:T(8,128)S(1)} %copy-done.17, s32[1]{0:T(128)} %bitcast.33.branch_ref, f32[16,16,128]{2,1,0:T(8,128)S(1)} %parent_coef.1.refs_0_, f32[16,16,128]{2,1,0:T(8,128)S(1)} %collective-permute-done.5.refs_1_, ...), custom_call_target="tpu_custom_call" | custom-call | tf_op jit(solution)/shard_map/parent_field/pallas_call | solution.py:575
  71.4 6.0 %collective-permute-done.10.refs_0_.refs_2_.refs_3_ = f32[192,16,128]{2,1,0:T(8,128)S(1)} collective-permute-done((f32[192,16,128]{2,1,0:T(8,128)}, f32[192,16,128]{2,1,0:T(8,128)S(1)}, u32[]{:S(2)}, u32[]{:S(2)}) %collective-permute-start.10) | collective-permute-done | bytes 1572896 | tf_op jit(solution)/shard_map/ppermute | solution.py:318
  77.3 2.1 %collective-permute-done.8.refs_1_.refs_0_.refs_2_ = f32[192,16,128]{2,1,0:T(8,128)} collective-permute-done((f32[192,16,128]{2,1,0:T(8,128)}, f32[192,16,128]{2,1,0:T(8,128)}, u32[]{:S(2)}, u32[]{:S(2)}) %collective-permute-start.8) | collective-permute-done | bytes 1572896 | tf_op jit(solution)/shard_map/ppermute | solution.py:318
  79.4 1.9 %pack.8 = (f32[128,16,128]{2,1,0:T(8,128)S(1)}, f32[128,16,128]{2,1,0:T(8,128)S(1)}, f32[128,16,128]{2,1,0:T(8,128)S(1)}, f32[128,16,128]{2,1,0:T(8,128)S(1)}) custom-call(f32[192,16,128]{2,1,0:T(8,128)S(1)} %collective-permute-done.10.refs_0_.refs_2_.refs_3_, f32[192,16,128]{2,1,0:T(8,128)} %collective-permute-done.8.refs_1_.refs_0_.refs_2_, ...), custom_call_target="tpu_custom_call" | custom-call | flops 99999997952 | bytes 1000000000 | tf_op jit(solution)/shard_map/pack/pallas_call | solution.py:368
  81.4 2.7 %collective-permute-start.14 = (f32[128,16,128]{2,1,0:T(8,128)S(1)}, f32[128,16,128]{2,1,0:T(8,128)S(1)}, u32[]{:S(2)}, u32[]{:S(2)}) collective-permute-start(f32[128,16,128]{2,1,0:T(8,128)S(1)} %get-tuple-element.114), channel_id=1, source_target_pairs={{0,24},{1,25},{2,26},{3,27},{4,28},{5,29},{6,30},{7,31},{8,0},{9,1... | collective-permute-start | bytes 3145736 | tf_op jit(solution)/shard_map/ppermute | solution.py:318
  84.1 2.7 %collective-permute-start.16 = (f32[128,16,128]{2,1,0:T(8,128)S(1)}, f32[128,16,128]{2,1,0:T(8,128)S(1)}, u32[]{:S(2)}, u32[]{:S(2)}) collective-permute-start(f32[128,16,128]{2,1,0:T(8,128)S(1)} %get-tuple-element.116), channel_id=1, source_target_pairs={{0,6},{1,7},{2,0},{3,1},{4,2},{5,3},{6,4},{7,5},{8,14},{9,15},{10,... | collective-permute-start | bytes 3145736 | tf_op jit(solution)/shard_map/ppermute | solution.py:318
  86.8 2.3 %pack.11 = f32[768,16,128]{2,1,0:T(8,128)S(1)} custom-call(f32[192,16,128]{2,1,0:T(8,128)} %collective-permute-done.8.refs_1_.refs_0_.refs_2_, f32[192,16,128]{2,1,0:T(8,128)} %collective-permute-done.9.refs_2_.refs_1_.refs_0_, f32[192,16,128]{2,1,0:T(8,128)S(1)} %collective-permute-done.10.refs_0_.refs_2_.refs_3_, ...), custom_call_target="tpu_custom_call" | custom-call | tf_op jit(solution)/shard_map/pack/pallas_call | solution.py:368
  89.0 4.2 %pick.7.refs_2_ = bf16[384,32,128]{2,1,0:T(8,128)(2,1)S(1)} custom-call(s32[32,128]{1,0:T(8,128)S(1)} %get-tuple-element.149.code_ref, f32[192,16,128]{2,1,0:T(8,128)} %collective-permute-done.9.refs_2_.refs_1_.refs_0_, f32[192,16,128]{2,1,0:T(8,128)S(1)} %collective-permute-done.11.refs_3_.refs_1_, ...), custom_call_target="tpu_custom_call" | custom-call | tf_op jit(solution)/shard_map/pick/pallas_call | solution.py:144
  93.3 3.8 %collective-permute-start.17 = (f32[768,16,128]{2,1,0:T(8,128)S(1)}, f32[768,16,128]{2,1,0:T(8,128)S(1)}, u32[]{:S(2)}, u32[]{:S(2)}) collective-permute-start(f32[768,16,128]{2,1,0:T(8,128)S(1)} %pack.11), channel_id=1, source_target_pairs={{0,1},{1,0},{2,3},{3,2},{4,5},{5,4},{6,7},{7,6},{8,9},{9,8},{10,11... | collective-permute-start | bytes 18874376 | tf_op jit(solution)/shard_map/ppermute | solution.py:328
  97.1 4.0 %pick.6.refs_1_ = bf16[320,32,128]{2,1,0:T(8,128)(2,1)S(1)} custom-call(s32[32,128]{1,0:T(8,128)S(1)} %get-tuple-element.149.code_ref, f32[128,16,128]{2,1,0:T(8,128)} %collective-permute-done.4.refs_0_, f32[512,16,128]{2,1,0:T(8,128)S(1)} %collective-permute-done.12.refs_1_), custom_call_target="tpu_custom_call" | custom-call | tf_op jit(solution)/shard_map/pick/pallas_call | solution.py:144
  101.1 3.6 %collective-permute-done.13.refs_0_.refs_3_ = f32[128,16,128]{2,1,0:T(8,128)S(1)} collective-permute-done((f32[128,16,128]{2,1,0:T(8,128)S(1)}, f32[128,16,128]{2,1,0:T(8,128)S(1)}, u32[]{:S(2)}, u32[]{:S(2)}) %collective-permute-start.13) | collective-permute-done | bytes 1048608 | tf_op jit(solution)/shard_map/ppermute | solution.py:318
  104.7 2.1 %collective-permute-done.15.refs_2_.refs_1_ = f32[128,16,128]{2,1,0:T(8,128)S(1)} collective-permute-done((f32[128,16,128]{2,1,0:T(8,128)S(1)}, f32[128,16,128]{2,1,0:T(8,128)S(1)}, u32[]{:S(2)}, u32[]{:S(2)}) %collective-permute-start.15) | collective-permute-done | bytes 1048608 | tf_op jit(solution)/shard_map/ppermute | solution.py:318
  106.8 0.2 pack.10
  107.1 2.7 %collective-permute-start.19 = (f32[32,16,128]{2,1,0:T(8,128)S(1)}, f32[32,16,128]{2,1,0:T(8,128)S(1)}, u32[]{:S(2)}, u32[]{:S(2)}) collective-permute-start(f32[32,16,128]{2,1,0:T(8,128)S(1)} %get-tuple-element.133), channel_id=1, source_target_pairs={{0,24},{1,25},{2,26},{3,27},{4,28},{5,29},{6,30},{7,31},{8,0},{9,1... | collective-permute-start | bytes 786440 | tf_op jit(solution)/shard_map/ppermute | solution.py:318
  109.8 2.7 %collective-permute-start.21 = (f32[32,16,128]{2,1,0:T(8,128)S(1)}, f32[32,16,128]{2,1,0:T(8,128)S(1)}, u32[]{:S(2)}, u32[]{:S(2)}) collective-permute-start(f32[32,16,128]{2,1,0:T(8,128)S(1)} %get-tuple-element.135), channel_id=1, source_target_pairs={{0,6},{1,7},{2,0},{3,1},{4,2},{5,3},{6,4},{7,5},{8,14},{9,15},{10,... | collective-permute-start | bytes 786440 | tf_op jit(solution)/shard_map/ppermute | solution.py:318
  112.5 0.6 pack.13
  113.1 5.3 %collective-permute-start.22 = (f32[512,16,128]{2,1,0:T(8,128)S(1)}, f32[512,16,128]{2,1,0:T(8,128)S(1)}, u32[]{:S(2)}, u32[]{:S(2)}) collective-permute-start(f32[512,16,128]{2,1,0:T(8,128)S(1)} %pack.13), channel_id=1, source_target_pairs={{0,1},{1,0},{2,3},{3,2},{4,5},{5,4},{6,7},{7,6},{8,9},{9,8},{10,11... | collective-permute-start | bytes 12582920 | tf_op jit(solution)/shard_map/ppermute | solution.py:328
  118.4 3.6 %pick.8.refs_3_ = bf16[384,32,128]{2,1,0:T(8,128)(2,1)S(1)} custom-call(s32[32,128]{1,0:T(8,128)S(1)} %get-tuple-element.149.code_ref, f32[768,16,128]{2,1,0:T(8,128)S(1)} %collective-permute-done.17.refs_0_), custom_call_target="tpu_custom_call" | custom-call | tf_op jit(solution)/shard_map/pick/pallas_call | solution.py:144
  122.1 0.2 pack.12
  122.3 2.9 %collective-permute-done.22.refs_5_ = f32[512,16,128]{2,1,0:T(8,128)S(1)} collective-permute-done((f32[512,16,128]{2,1,0:T(8,128)S(1)}, f32[512,16,128]{2,1,0:T(8,128)S(1)}, u32[]{:S(2)}, u32[]{:S(2)}) %collective-permute-start.22) | collective-permute-done | bytes 4194336 | tf_op jit(solution)/shard_map/ppermute | solution.py:328
  125.2 0.4 collective-permute-start.23
  125.6 2.7 %pick.9.refs_4_ = bf16[256,32,128]{2,1,0:T(8,128)(2,1)S(1)} custom-call(s32[32,128]{1,0:T(8,128)S(1)} %get-tuple-element.149.code_ref, f32[128,16,128]{2,1,0:T(8,128)S(1)} %collective-permute-done.14.refs_1_.refs_0_, f32[128,16,128]{2,1,0:T(8,128)S(1)} %collective-permute-done.15.refs_2_.refs_1_, ...), custom_call_target="tpu_custom_call" | custom-call | tf_op jit(solution)/shard_map/pick/pallas_call | solution.py:144
  128.3 12.3 %leaf_field_product.1 = f32[64,8192]{1,0:T(8,128)} custom-call(s32[128,16]{1,0:T(8,128)S(1)} %copy-done.15, s32[32,128]{1,0:T(8,128)S(1)} %get-tuple-element.149.code_ref, bf16[320,32,128]{2,1,0:T(8,128)(2,1)S(1)} %pick.5.refs_0_, bf16[320,32,128]{2,1,0:T(8,128)(2,1)S(1)} %pick.6.refs_1_, bf16[384,32,128]{2,1,0:T(8,128)(2,1)S(1)} %pick.7.refs_2_, ...), custom_call_target="tpu_custom_call" | custom-call | tf_op jit(solution)/shard_map/leaf_field_product/pallas_call | solution.py:274
  (66 shorter events, 0.9 us)
Async XLA Ops:
  0.0 12.4 %copy-start.19 = (f32[128,1024]{1,0:T(8,128)S(1)}, f32[128,1024]{1,0:T(8,128)}, u32[]{:S(2)}) copy-start(f32[128,1024]{1,0:T(8,128)} %param.11) | copy-start | bytes 1572868
  4.3 14.6 %copy-start.20 = (s32[128,16]{0,1:T(8,128)S(1)}, s32[128,16]{0,1:T(8,128)}, u32[]{:S(2)}) copy-start(s32[128,16]{0,1:T(8,128)} %param.13) | copy-start | bytes 24580
  4.3 14.7 %copy-start.21 = (s32[128,16]{0,1:T(8,128)S(1)}, s32[128,16]{0,1:T(8,128)}, u32[]{:S(2)}) copy-start(s32[128,16]{0,1:T(8,128)} %param.14) | copy-start | bytes 24580
  4.3 12.1 %collective-permute-start.4 = (f32[128,16,128]{2,1,0:T(8,128)}, f32[128,16,128]{2,1,0:T(8,128)}, u32[]{:S(2)}, u32[]{:S(2)}) collective-permute-start(f32[128,16,128]{2,1,0:T(8,128)} %get-tuple-element.83.refs_0_), channel_id=1, source_target_pairs={{0,1},{1,0},{2,3},{3,2},{4,5},{5,4},{6,7},{7,6},{8,9},{9,8},{10,11... | collective-permute-start | bytes 3145736 | tf_op jit(solution)/shard_map/ppermute | solution.py:328
  5.8 26.6 %collective-permute-start = (f32[128,16,128]{2,1,0:T(8,128)}, f32[128,16,128]{2,1,0:T(8,128)S(1)}, u32[]{:S(2)}, u32[]{:S(2)}) collective-permute-start(f32[128,16,128]{2,1,0:T(8,128)} %get-tuple-element.83.refs_0_), channel_id=1, source_target_pairs={{0,2},{1,3},{2,4},{3,5},{4,6},{5,7},{6,0},{7,1},{8,10},{9,11},{10,... | collective-permute-start | bytes 3145736 | tf_op jit(solution)/shard_map/ppermute | solution.py:318
  7.2 25.2 %collective-permute-start.1 = (f32[128,16,128]{2,1,0:T(8,128)}, f32[128,16,128]{2,1,0:T(8,128)S(1)}, u32[]{:S(2)}, u32[]{:S(2)}) collective-permute-start(f32[128,16,128]{2,1,0:T(8,128)} %get-tuple-element.83.refs_0_), channel_id=1, source_target_pairs={{0,6},{1,7},{2,0},{3,1},{4,2},{5,3},{6,4},{7,5},{8,14},{9,15},{10,... | collective-permute-start | bytes 3145736 | tf_op jit(solution)/shard_map/ppermute | solution.py:318
  8.6 27.1 %collective-permute-start.2 = (f32[128,16,128]{2,1,0:T(8,128)}, f32[128,16,128]{2,1,0:T(8,128)}, u32[]{:S(2)}, u32[]{:S(2)}) collective-permute-start(f32[128,16,128]{2,1,0:T(8,128)} %get-tuple-element.83.refs_0_), channel_id=1, source_target_pairs={{0,8},{1,9},{2,10},{3,11},{4,12},{5,13},{6,14},{7,15},{8,16},{9,17... | collective-permute-start | bytes 3145736 | tf_op jit(solution)/shard_map/ppermute | solution.py:318
  10.2 25.5 %collective-permute-start.3 = (f32[128,16,128]{2,1,0:T(8,128)}, f32[128,16,128]{2,1,0:T(8,128)}, u32[]{:S(2)}, u32[]{:S(2)}) collective-permute-start(f32[128,16,128]{2,1,0:T(8,128)} %get-tuple-element.83.refs_0_), channel_id=1, source_target_pairs={{0,24},{1,25},{2,26},{3,27},{4,28},{5,29},{6,30},{7,31},{8,0},{9,1... | collective-permute-start | bytes 3145736 | tf_op jit(solution)/shard_map/ppermute | solution.py:318
  12.4 27.9 %copy-start = (f32[1024,128]{1,0:T(8,128)}, f32[1024,128]{1,0:T(8,128)S(1)}, u32[]{:S(2)}) copy-start(f32[1024,128]{1,0:T(8,128)S(1)} %reshape.3.transfer_ref.refs_5_) | copy-start | bytes 1572868
  12.5 1.4 %copy-start.11 = (f32[64,32,128]{2,1,0:T(8,128)S(1)}, f32[64,32,128]{2,1,0:T(8,128)}, u32[]{:S(2)}) copy-start(f32[64,32,128]{2,1,0:T(8,128)} %get-tuple-element.90.pair_ref) | copy-start | bytes 3145732
  16.3 7.3 %collective-permute-start.5 = (f32[16,16,128]{2,1,0:T(8,128)S(1)}, f32[16,16,128]{2,1,0:T(8,128)S(1)}, u32[]{:S(2)}, u32[]{:S(2)}) collective-permute-start(f32[16,16,128]{2,1,0:T(8,128)S(1)} %parent_coef.1.refs_0_), channel_id=1, source_target_pairs={{0,96},{32,0},{64,32},{96,64},{1,97},{33,1},{65,33},{97,65},{2,98}... | collective-permute-start | bytes 393224 | tf_op jit(solution)/shard_map/ppermute | solution.py:328
  23.7 16.7 %copy-start.14 = (s32[128,16]{1,0:T(8,128)}, s32[128,16]{1,0:T(8,128)S(1)}, u32[]{:S(2)}) copy-start(s32[128,16]{1,0:T(8,128)S(1)} %get-tuple-element.148.pos_ref) | copy-start | bytes 24580
  23.7 5.4 %collective-permute-start.6 = (f32[16,16,128]{2,1,0:T(8,128)S(1)}, f32[16,16,128]{2,1,0:T(8,128)S(1)}, u32[]{:S(2)}, u32[]{:S(2)}) collective-permute-start(f32[16,16,128]{2,1,0:T(8,128)S(1)} %parent_coef.1.refs_0_), channel_id=1, source_target_pairs={{0,64},{32,96},{64,0},{96,32},{1,65},{33,97},{65,1},{97,33},{2,66}... | collective-permute-start | bytes 393224 | tf_op jit(solution)/shard_map/ppermute | solution.py:328
  29.1 11.3 %collective-permute-start.7 = (f32[16,16,128]{2,1,0:T(8,128)S(1)}, f32[16,16,128]{2,1,0:T(8,128)S(1)}, u32[]{:S(2)}, u32[]{:S(2)}) collective-permute-start(f32[16,16,128]{2,1,0:T(8,128)S(1)} %parent_coef.1.refs_0_), channel_id=1, source_target_pairs={{0,32},{32,64},{64,96},{96,0},{1,33},{33,65},{65,97},{97,1},{2,34}... | collective-permute-start | bytes 393224 | tf_op jit(solution)/shard_map/ppermute | solution.py:328
  32.3 8.0 %copy-start.3 = (f32[128,16,128]{2,1,0:T(8,128)}, f32[128,16,128]{2,1,0:T(8,128)S(1)}, u32[]{:S(2)}) copy-start(f32[128,16,128]{2,1,0:T(8,128)S(1)} %collective-permute-done.refs_1_.refs_0_.refs_2_) | copy-start | bytes 3145732
  32.3 8.0 %copy-start.6 = (f32[128,16,128]{2,1,0:T(8,128)}, f32[128,16,128]{2,1,0:T(8,128)S(1)}, u32[]{:S(2)}) copy-start(f32[128,16,128]{2,1,0:T(8,128)S(1)} %collective-permute-done.1.refs_0_.refs_1_) | copy-start | bytes 3145732
  40.4 0.7 copy-start.12
  41.0 36.3 %collective-permute-start.10 = (f32[192,16,128]{2,1,0:T(8,128)}, f32[192,16,128]{2,1,0:T(8,128)S(1)}, u32[]{:S(2)}, u32[]{:S(2)}) collective-permute-start(f32[192,16,128]{2,1,0:T(8,128)} %get-tuple-element.96), channel_id=1, source_target_pairs={{0,2},{1,3},{2,4},{3,5},{4,6},{5,7},{6,0},{7,1},{8,10},{9,11},{10,... | collective-permute-start | bytes 4718600 | tf_op jit(solution)/shard_map/ppermute | solution.py:318
  41.0 36.3 %collective-permute-start.11 = (f32[192,16,128]{2,1,0:T(8,128)}, f32[192,16,128]{2,1,0:T(8,128)S(1)}, u32[]{:S(2)}, u32[]{:S(2)}) collective-permute-start(f32[192,16,128]{2,1,0:T(8,128)} %get-tuple-element.97), channel_id=1, source_target_pairs={{0,6},{1,7},{2,0},{3,1},{4,2},{5,3},{6,4},{7,5},{8,14},{9,15},{10,... | collective-permute-start | bytes 4718600 | tf_op jit(solution)/shard_map/ppermute | solution.py:318
  43.7 35.7 %collective-permute-start.8 = (f32[192,16,128]{2,1,0:T(8,128)}, f32[192,16,128]{2,1,0:T(8,128)}, u32[]{:S(2)}, u32[]{:S(2)}) collective-permute-start(f32[192,16,128]{2,1,0:T(8,128)} %get-tuple-element.94), channel_id=1, source_target_pairs={{0,8},{1,9},{2,10},{3,11},{4,12},{5,13},{6,14},{7,15},{8,16},{9,17... | collective-permute-start | bytes 4718600 | tf_op jit(solution)/shard_map/ppermute | solution.py:318
  44.0 35.5 %collective-permute-start.9 = (f32[192,16,128]{2,1,0:T(8,128)}, f32[192,16,128]{2,1,0:T(8,128)}, u32[]{:S(2)}, u32[]{:S(2)}) collective-permute-start(f32[192,16,128]{2,1,0:T(8,128)} %get-tuple-element.95), channel_id=1, source_target_pairs={{0,24},{1,25},{2,26},{3,27},{4,28},{5,29},{6,30},{7,31},{8,0},{9,1... | collective-permute-start | bytes 4718600 | tf_op jit(solution)/shard_map/ppermute | solution.py:318
  46.4 1.2 copy-start.4
  47.6 1.2 copy-start.7
  48.8 2.0 %copy-start.5 = (f32[128,16,128]{2,1,0:T(8,128)S(1)}, f32[128,16,128]{2,1,0:T(8,128)}, u32[]{:S(2)}) copy-start(f32[128,16,128]{2,1,0:T(8,128)} %copy-done.3) | copy-start | bytes 3145732
  48.8 2.2 %copy-start.8 = (f32[128,16,128]{2,1,0:T(8,128)S(1)}, f32[128,16,128]{2,1,0:T(8,128)}, u32[]{:S(2)}) copy-start(f32[128,16,128]{2,1,0:T(8,128)} %copy-done.6) | copy-start | bytes 3145732
  48.8 2.5 %copy-start.10 = (f32[128,16,128]{2,1,0:T(8,128)S(1)}, f32[128,16,128]{2,1,0:T(8,128)}, u32[]{:S(2)}) copy-start(f32[128,16,128]{2,1,0:T(8,128)} %get-tuple-element.83.refs_0_) | copy-start | bytes 3145732
  51.3 5.4 %copy-start.1 = (f32[1024,128]{1,0:T(8,128)S(1)}, f32[1024,128]{1,0:T(8,128)}, u32[]{:S(2)}) copy-start(f32[1024,128]{1,0:T(8,128)} %copy-done) | copy-start | bytes 1572868
  51.3 5.4 %copy-start.9 = (f32[16,32,1024]{2,1,0:T(8,128)S(1)}, f32[16,32,1024]{2,1,0:T(8,128)}, u32[]{:S(2)}) copy-start(f32[16,32,1024]{2,1,0:T(8,128)} %refs_4_.1) | copy-start | bytes 6291460
  51.3 5.4 %copy-start.13 = (f32[16,16,128]{2,1,0:T(8,128)S(1)}, f32[16,16,128]{2,1,0:T(8,128)}, u32[]{:S(2)}) copy-start(f32[16,16,128]{2,1,0:T(8,128)} %copy-done.12) | copy-start | bytes 393220
  51.3 5.4 %copy-start.16 = (s32[16,32]{1,0:T(8,128)S(1)}, s32[16,32]{1,0:T(8,128)}, u32[]{:S(2)}) copy-start(s32[16,32]{1,0:T(8,128)} %list_ref.2) | copy-start | bytes 6148
  51.3 5.4 %copy-start.17 = (s32[16,32]{1,0:T(8,128)S(1)}, s32[16,32]{1,0:T(8,128)}, u32[]{:S(2)}) copy-start(s32[16,32]{1,0:T(8,128)} %mask_ref.2) | copy-start | bytes 6148
  54.4 26.9 %collective-permute-start.12 = (f32[512,16,128]{2,1,0:T(8,128)S(1)}, f32[512,16,128]{2,1,0:T(8,128)S(1)}, u32[]{:S(2)}, u32[]{:S(2)}) collective-permute-start(f32[512,16,128]{2,1,0:T(8,128)S(1)} %pack.9), channel_id=1, source_target_pairs={{0,1},{1,0},{2,3},{3,2},{4,5},{5,4},{6,7},{7,6},{8,9},{9,8},{10,11... | collective-permute-start | bytes 12582920 | tf_op jit(solution)/shard_map/ppermute | solution.py:328
  81.3 23.3 %collective-permute-start.13 = (f32[128,16,128]{2,1,0:T(8,128)S(1)}, f32[128,16,128]{2,1,0:T(8,128)S(1)}, u32[]{:S(2)}, u32[]{:S(2)}) collective-permute-start(f32[128,16,128]{2,1,0:T(8,128)S(1)} %get-tuple-element.113), channel_id=1, source_target_pairs={{0,8},{1,9},{2,10},{3,11},{4,12},{5,13},{6,14},{7,15},{8,16},{9,17... | collective-permute-start | bytes 3145736 | tf_op jit(solution)/shard_map/ppermute | solution.py:318
  81.4 23.3 %collective-permute-start.14 = (f32[128,16,128]{2,1,0:T(8,128)S(1)}, f32[128,16,128]{2,1,0:T(8,128)S(1)}, u32[]{:S(2)}, u32[]{:S(2)}) collective-permute-start(f32[128,16,128]{2,1,0:T(8,128)S(1)} %get-tuple-element.114), channel_id=1, source_target_pairs={{0,24},{1,25},{2,26},{3,27},{4,28},{5,29},{6,30},{7,31},{8,0},{9,1... | collective-permute-start | bytes 3145736 | tf_op jit(solution)/shard_map/ppermute | solution.py:318
  84.1 22.7 %collective-permute-start.15 = (f32[128,16,128]{2,1,0:T(8,128)S(1)}, f32[128,16,128]{2,1,0:T(8,128)S(1)}, u32[]{:S(2)}, u32[]{:S(2)}) collective-permute-start(f32[128,16,128]{2,1,0:T(8,128)S(1)} %get-tuple-element.115), channel_id=1, source_target_pairs={{0,2},{1,3},{2,4},{3,5},{4,6},{5,7},{6,0},{7,1},{8,10},{9,11},{10,... | collective-permute-start | bytes 3145736 | tf_op jit(solution)/shard_map/ppermute | solution.py:318
  84.1 22.7 %collective-permute-start.16 = (f32[128,16,128]{2,1,0:T(8,128)S(1)}, f32[128,16,128]{2,1,0:T(8,128)S(1)}, u32[]{:S(2)}, u32[]{:S(2)}) collective-permute-start(f32[128,16,128]{2,1,0:T(8,128)S(1)} %get-tuple-element.116), channel_id=1, source_target_pairs={{0,6},{1,7},{2,0},{3,1},{4,2},{5,3},{6,4},{7,5},{8,14},{9,15},{10,... | collective-permute-start | bytes 3145736 | tf_op jit(solution)/shard_map/ppermute | solution.py:318
  93.3 13.7 %collective-permute-start.17 = (f32[768,16,128]{2,1,0:T(8,128)S(1)}, f32[768,16,128]{2,1,0:T(8,128)S(1)}, u32[]{:S(2)}, u32[]{:S(2)}) collective-permute-start(f32[768,16,128]{2,1,0:T(8,128)S(1)} %pack.11), channel_id=1, source_target_pairs={{0,1},{1,0},{2,3},{3,2},{4,5},{5,4},{6,7},{7,6},{8,9},{9,8},{10,11... | collective-permute-start | bytes 18874376 | tf_op jit(solution)/shard_map/ppermute | solution.py:328
  107.1 15.0 %collective-permute-start.18 = (f32[32,16,128]{2,1,0:T(8,128)S(1)}, f32[32,16,128]{2,1,0:T(8,128)S(1)}, u32[]{:S(2)}, u32[]{:S(2)}) collective-permute-start(f32[32,16,128]{2,1,0:T(8,128)S(1)} %get-tuple-element.132), channel_id=1, source_target_pairs={{0,8},{1,9},{2,10},{3,11},{4,12},{5,13},{6,14},{7,15},{8,16},{9,17... | collective-permute-start | bytes 786440 | tf_op jit(solution)/shard_map/ppermute | solution.py:318
  107.1 14.9 %collective-permute-start.19 = (f32[32,16,128]{2,1,0:T(8,128)S(1)}, f32[32,16,128]{2,1,0:T(8,128)S(1)}, u32[]{:S(2)}, u32[]{:S(2)}) collective-permute-start(f32[32,16,128]{2,1,0:T(8,128)S(1)} %get-tuple-element.133), channel_id=1, source_target_pairs={{0,24},{1,25},{2,26},{3,27},{4,28},{5,29},{6,30},{7,31},{8,0},{9,1... | collective-permute-start | bytes 786440 | tf_op jit(solution)/shard_map/ppermute | solution.py:318
  109.8 12.3 %collective-permute-start.20 = (f32[32,16,128]{2,1,0:T(8,128)S(1)}, f32[32,16,128]{2,1,0:T(8,128)S(1)}, u32[]{:S(2)}, u32[]{:S(2)}) collective-permute-start(f32[32,16,128]{2,1,0:T(8,128)S(1)} %get-tuple-element.134), channel_id=1, source_target_pairs={{0,2},{1,3},{2,4},{3,5},{4,6},{5,7},{6,0},{7,1},{8,10},{9,11},{10,... | collective-permute-start | bytes 786440 | tf_op jit(solution)/shard_map/ppermute | solution.py:318
  109.8 12.3 %collective-permute-start.21 = (f32[32,16,128]{2,1,0:T(8,128)S(1)}, f32[32,16,128]{2,1,0:T(8,128)S(1)}, u32[]{:S(2)}, u32[]{:S(2)}) collective-permute-start(f32[32,16,128]{2,1,0:T(8,128)S(1)} %get-tuple-element.135), channel_id=1, source_target_pairs={{0,6},{1,7},{2,0},{3,1},{4,2},{5,3},{6,4},{7,5},{8,14},{9,15},{10,... | collective-permute-start | bytes 786440 | tf_op jit(solution)/shard_map/ppermute | solution.py:318
  113.1 12.1 %collective-permute-start.22 = (f32[512,16,128]{2,1,0:T(8,128)S(1)}, f32[512,16,128]{2,1,0:T(8,128)S(1)}, u32[]{:S(2)}, u32[]{:S(2)}) collective-permute-start(f32[512,16,128]{2,1,0:T(8,128)S(1)} %pack.13), channel_id=1, source_target_pairs={{0,1},{1,0},{2,3},{3,2},{4,5},{5,4},{6,7},{7,6},{8,9},{9,8},{10,11... | collective-permute-start | bytes 12582920 | tf_op jit(solution)/shard_map/ppermute | solution.py:328
  122.3 6.0 %copy-start.2 = (f32[32,8192]{1,0:T(8,128)S(1)}, f32[32,8192]{1,0:T(8,128)}, u32[]{:S(2)}) copy-start(f32[32,8192]{1,0:T(8,128)} %refs_13_.1) | copy-start | bytes 3145732
  122.3 6.0 %copy-start.15 = (s32[128,16]{1,0:T(8,128)S(1)}, s32[128,16]{1,0:T(8,128)}, u32[]{:S(2)}) copy-start(s32[128,16]{1,0:T(8,128)} %copy-done.14) | copy-start | bytes 24580
  125.2 3.1 %copy-start.18 = (f32[512,16,128]{2,1,0:T(8,128)}, f32[512,16,128]{2,1,0:T(8,128)S(1)}, u32[]{:S(2)}) copy-start(f32[512,16,128]{2,1,0:T(8,128)S(1)} %collective-permute-done.22.refs_5_) | copy-start | bytes 12582916
  125.2 3.1 %collective-permute-start.23 = (f32[128,16,128]{2,1,0:T(8,128)S(1)}, f32[128,16,128]{2,1,0:T(8,128)S(1)}, u32[]{:S(2)}, u32[]{:S(2)}) collective-permute-start(f32[128,16,128]{2,1,0:T(8,128)S(1)} %pack.12), channel_id=1, source_target_pairs={{0,1},{1,0},{2,3},{3,2},{4,5},{5,4},{6,7},{7,6},{8,9},{9,8},{10,11... | collective-permute-start | bytes 3145736 | tf_op jit(solution)/shard_map/ppermute | solution.py:318

commit v5 on v4

--- a/solution.py
+++ b/solution.py
@@ -417,10 +417,10 @@
             joined = packed(fresh, [[key for p in fresh for key in p[1]]], unit)[0]
         swapped = moved(joined, "core", 1, turns)
         done = beside[number](have, others, done)
-        wanted = [[key for p in new for key in p[1]]]
         if number + 1 < len(SENDS):
-            wanted = [keys for _, _, keys in SENDS[number + 1]]
-        following = packed(have + new, wanted, unit, LONG)
+            following = packed(have + new, [keys for _, _, keys in SENDS[number + 1]], unit, LONG)
+        else:
+            following = packed(new, [[key for p in new for key in p[1]]], unit)
         arrays, ahead, other, done = lax.optimization_barrier(
             ([p[0] for p in new], [p[0] for p in following], swapped[0], done)
         )

time: 141 us -> 140 us (level)
    ppermute x7, waiting for transfers between devices: 7.68 us -> 4.83 us  [__call__(): self.last = lax.ppermute(array, axis, perm)]
    ppermute x17, waiting for transfers between devices: 20.4 us -> 22.5 us  [moved(): return (send(array, 'subtree', perm), out)]
  transfers between devices with their start and end apart: 24 -> 24, of which waited for: 8 -> 9; matrix products, arithmetic and copies ran while one was open for 0% -> 0% of each run, Pallas kernels for 36% -> 36%
where the time goes in v5:
time: 140 us
  Pallas kernels  67.5 us (48%)
  starting transfers between devices  39.2 us (28%)
  waiting for transfers between devices  27.4 us (20%)
  local copies, waits for them, and re-layouts  5.46 us (4%)
    ppermute x17, starting transfers between devices, moved(): return (send(array, 'subtree', perm), out)  24.3 us
    ppermute x17, waiting for transfers between devices, moved(): return (send(array, 'subtree', perm), out)  22.5 us
    pallas_call x5, Pallas kernels, picked_slots(): pl.pallas_call(functools.partial(pick_kernel, plan, first), out_shape=jax...  17.6 us
    ppermute x7, starting transfers between devices, __call__(): self.last = lax.ppermute(array, axis, perm)  14.9 us
    pallas_call x1, Pallas kernels, downward_pairs(): pl.pallas_call(functools.partial(parent_field_kernel, group), out_shape=j...  14.6 us
    pallas_call x1, Pallas kernels, products(): pl.pallas_call(functools.partial(field_kernel, slots, block, plan, len(ti...  12.3 us
    pallas_call x7, Pallas kernels, packed(): pl.pallas_call(functools.partial(pack_kernel, plan, len(arrays)), out_sha...  11.8 us
    unnamed x46, local copies, waits for them, and re-layouts  5.26 us
  transfers between devices with their start and end apart: 24, of which 9 were waited for; matrix products, arithmetic and copies ran while one was open for 0% of the time, Pallas kernels for 36%

profile of v5, /device:TPU:1, one launch (start us, length us, event | category | flops | bytes accessed | tf_op | source)
XLA Modules:
  0.0 140.0 jit_solution(11061585490376159425)
XLA Ops:
  0.0 4.3 %leaf_coef.1 = (f32[128,16,128]{2,1,0:T(8,128)}, f32[64,32,128]{2,1,0:T(8,128)}) custom-call(f32[32,8192]{1,0:T(8,128)} %refs_13_.1, f32[64,8192]{1,0:T(8,128)} %vectors_ref.1), custom_call_target="tpu_custom_call" | custom-call | tf_op jit(solution)/shard_map/leaf_coef/pallas_call | solution.py:75
  4.3 1.5 %collective-permute-start.4 = (f32[128,16,128]{2,1,0:T(8,128)}, f32[128,16,128]{2,1,0:T(8,128)}, u32[]{:S(2)}, u32[]{:S(2)}) collective-permute-start(f32[128,16,128]{2,1,0:T(8,128)} %get-tuple-element.83.refs_0_), channel_id=1, source_target_pairs={{0,1},{1,0},{2,3},{3,2},{4,5},{5,4},{6,7},{7,6},{8,9},{9,8},{10,11... | collective-permute-start | bytes 3145736 | tf_op jit(solution)/shard_map/ppermute | solution.py:328
  5.8 1.4 %collective-permute-start = (f32[128,16,128]{2,1,0:T(8,128)}, f32[128,16,128]{2,1,0:T(8,128)S(1)}, u32[]{:S(2)}, u32[]{:S(2)}) collective-permute-start(f32[128,16,128]{2,1,0:T(8,128)} %get-tuple-element.83.refs_0_), channel_id=1, source_target_pairs={{0,2},{1,3},{2,4},{3,5},{4,6},{5,7},{6,0},{7,1},{8,10},{9,11},{10,... | collective-permute-start | bytes 3145736 | tf_op jit(solution)/shard_map/ppermute | solution.py:318
  7.2 1.4 %collective-permute-start.1 = (f32[128,16,128]{2,1,0:T(8,128)}, f32[128,16,128]{2,1,0:T(8,128)S(1)}, u32[]{:S(2)}, u32[]{:S(2)}) collective-permute-start(f32[128,16,128]{2,1,0:T(8,128)} %get-tuple-element.83.refs_0_), channel_id=1, source_target_pairs={{0,6},{1,7},{2,0},{3,1},{4,2},{5,3},{6,4},{7,5},{8,14},{9,15},{10,... | collective-permute-start | bytes 3145736 | tf_op jit(solution)/shard_map/ppermute | solution.py:318
  8.6 1.6 %collective-permute-start.2 = (f32[128,16,128]{2,1,0:T(8,128)}, f32[128,16,128]{2,1,0:T(8,128)}, u32[]{:S(2)}, u32[]{:S(2)}) collective-permute-start(f32[128,16,128]{2,1,0:T(8,128)} %get-tuple-element.83.refs_0_), channel_id=1, source_target_pairs={{0,8},{1,9},{2,10},{3,11},{4,12},{5,13},{6,14},{7,15},{8,16},{9,17... | collective-permute-start | bytes 3145736 | tf_op jit(solution)/shard_map/ppermute | solution.py:318
  10.2 2.1 %collective-permute-start.3 = (f32[128,16,128]{2,1,0:T(8,128)}, f32[128,16,128]{2,1,0:T(8,128)}, u32[]{:S(2)}, u32[]{:S(2)}) collective-permute-start(f32[128,16,128]{2,1,0:T(8,128)} %get-tuple-element.83.refs_0_), channel_id=1, source_target_pairs={{0,24},{1,25},{2,26},{3,27},{4,28},{5,29},{6,30},{7,31},{8,0},{9,1... | collective-permute-start | bytes 3145736 | tf_op jit(solution)/shard_map/ppermute | solution.py:318
  12.5 1.4 %copy-done.11 = f32[64,32,128]{2,1,0:T(8,128)S(1)} copy-done((f32[64,32,128]{2,1,0:T(8,128)S(1)}, f32[64,32,128]{2,1,0:T(8,128)}, u32[]{:S(2)}) %copy-start.11) | copy-done | bytes 1048600
  13.9 2.5 %parent_coef.1.refs_0_ = f32[16,16,128]{2,1,0:T(8,128)S(1)} custom-call(f32[64,32,128]{2,1,0:T(8,128)S(1)} %copy-done.11, f32[1024,128]{1,0:T(8,128)S(1)} %reshape.3.transfer_ref.refs_5_), custom_call_target="tpu_custom_call" | custom-call | tf_op jit(solution)/shard_map/parent_coef/pallas_call | solution.py:509
  16.3 2.5 %collective-permute-start.5 = (f32[16,16,128]{2,1,0:T(8,128)S(1)}, f32[16,16,128]{2,1,0:T(8,128)S(1)}, u32[]{:S(2)}, u32[]{:S(2)}) collective-permute-start(f32[16,16,128]{2,1,0:T(8,128)S(1)} %parent_coef.1.refs_0_), channel_id=1, source_target_pairs={{0,96},{32,0},{64,32},{96,64},{1,97},{33,1},{65,33},{97,65},{2,98}... | collective-permute-start | bytes 393224 | tf_op jit(solution)/shard_map/ppermute | solution.py:328
  19.2 4.4 %slot_order.1 = (s32[128,16]{1,0:T(8,128)S(1)}, s32[32,128]{1,0:T(8,128)S(1)}) custom-call(s32[1,128]{1,0:T(1,128)S(1)} %pad_bitcast_fusion.own_ref, s32[128,16]{1,0:T(8,128)S(1)} %copy.10.list_ref, s32[128,16]{1,0:T(8,128)S(1)} %copy.11.mask_ref), custom_call_target="tpu_custom_call" | custom-call | tf_op jit(solution)/shard_map/slot_order/pallas_call | solution.py:465
  23.7 0.6 collective-permute-start.6
  24.3 4.8 %collective-permute-done.6.refs_2_ = f32[16,16,128]{2,1,0:T(8,128)S(1)} collective-permute-done((f32[16,16,128]{2,1,0:T(8,128)S(1)}, f32[16,16,128]{2,1,0:T(8,128)S(1)}, u32[]{:S(2)}, u32[]{:S(2)}) %collective-permute-start.6) | collective-permute-done | bytes 131104 | tf_op jit(solution)/shard_map/ppermute | solution.py:328
  29.1 3.2 %collective-permute-done.refs_1_.refs_0_.refs_2_ = f32[128,16,128]{2,1,0:T(8,128)S(1)} collective-permute-done((f32[128,16,128]{2,1,0:T(8,128)}, f32[128,16,128]{2,1,0:T(8,128)S(1)}, u32[]{:S(2)}, u32[]{:S(2)}) %collective-permute-start) | collective-permute-done | bytes 1048608 | tf_op jit(solution)/shard_map/ppermute | solution.py:318
  32.3 3.4 %collective-permute-done.2.refs_2_.refs_4_ = f32[128,16,128]{2,1,0:T(8,128)} collective-permute-done((f32[128,16,128]{2,1,0:T(8,128)}, f32[128,16,128]{2,1,0:T(8,128)}, u32[]{:S(2)}, u32[]{:S(2)}) %collective-permute-start.2) | collective-permute-done | bytes 1048608 | tf_op jit(solution)/shard_map/ppermute | solution.py:318
  35.7 4.6 %pack.7 = (f32[192,16,128]{2,1,0:T(8,128)}, f32[192,16,128]{2,1,0:T(8,128)}, f32[192,16,128]{2,1,0:T(8,128)}, f32[192,16,128]{2,1,0:T(8,128)}) custom-call(f32[128,16,128]{2,1,0:T(8,128)S(1)} %collective-permute-done.1.refs_0_.refs_1_, f32[128,16,128]{2,1,0:T(8,128)S(1)} %collective-permute-done.refs_1_.refs_0_.refs_2_, ...), custom_call_target="tpu_custom_call" | custom-call | flops 99999997952 | bytes 1000000000 | tf_op jit(solution)/shard_map/pack/pallas_call | solution.py:368
  40.4 0.6 copy-done.12
  41.0 2.7 %collective-permute-start.11 = (f32[192,16,128]{2,1,0:T(8,128)}, f32[192,16,128]{2,1,0:T(8,128)S(1)}, u32[]{:S(2)}, u32[]{:S(2)}) collective-permute-start(f32[192,16,128]{2,1,0:T(8,128)} %get-tuple-element.97), channel_id=1, source_target_pairs={{0,6},{1,7},{2,0},{3,1},{4,2},{5,3},{6,4},{7,5},{8,14},{9,15},{10,... | collective-permute-start | bytes 4718600 | tf_op jit(solution)/shard_map/ppermute | solution.py:318
  43.7 0.3 collective-permute-start.8
  44.0 2.4 %collective-permute-start.9 = (f32[192,16,128]{2,1,0:T(8,128)}, f32[192,16,128]{2,1,0:T(8,128)}, u32[]{:S(2)}, u32[]{:S(2)}) collective-permute-start(f32[192,16,128]{2,1,0:T(8,128)} %get-tuple-element.95), channel_id=1, source_target_pairs={{0,24},{1,25},{2,26},{3,27},{4,28},{5,29},{6,30},{7,31},{8,0},{9,1... | collective-permute-start | bytes 4718600 | tf_op jit(solution)/shard_map/ppermute | solution.py:318
  46.4 1.2 copy-done.4
  47.6 1.2 copy-done.7
  48.8 2.0 %pack.9 = f32[512,16,128]{2,1,0:T(8,128)S(1)} custom-call(f32[128,16,128]{2,1,0:T(8,128)S(1)} %copy-done.4, f32[128,16,128]{2,1,0:T(8,128)S(1)} %copy-done.7, f32[128,16,128]{2,1,0:T(8,128)} %collective-permute-done.2.refs_2_.refs_4_, f32[128,16,128]{2,1,0:T(8,128)} %collective-permute-done.3.refs_3_), custom_call_target="tpu_custom_call" | custom-call | tf_op jit(solution)/shard_map/pack/pallas_call | solution.py:368
  51.0 0.3 copy-done.10
  51.3 3.1 %pick.5.refs_0_ = bf16[320,32,128]{2,1,0:T(8,128)(2,1)S(1)} custom-call(s32[32,128]{1,0:T(8,128)S(1)} %get-tuple-element.149.code_ref, f32[128,16,128]{2,1,0:T(8,128)S(1)} %copy-done.10, f32[128,16,128]{2,1,0:T(8,128)S(1)} %copy-done.8, f32[128,16,128]{2,1,0:T(8,128)S(1)} %copy-done.5, f32[128,16,128]{2,1,0:T(8,128)} %collective-permute-done.3.refs_3_, ...), custom_call_target="tpu_custom_call" | custom-call | tf_op jit(solution)/shard_map/pick/pallas_call | solution.py:144
  54.4 2.3 %collective-permute-start.12 = (f32[512,16,128]{2,1,0:T(8,128)S(1)}, f32[512,16,128]{2,1,0:T(8,128)S(1)}, u32[]{:S(2)}, u32[]{:S(2)}) collective-permute-start(f32[512,16,128]{2,1,0:T(8,128)S(1)} %pack.9), channel_id=1, source_target_pairs={{0,1},{1,0},{2,3},{3,2},{4,5},{5,4},{6,7},{7,6},{8,9},{9,8},{10,11... | collective-permute-start | bytes 12582920 | tf_op jit(solution)/shard_map/ppermute | solution.py:328
  56.7 14.6 %parent_field.1.refs_12_ = f32[64,32,128]{2,1,0:T(8,128)S(1)} custom-call(s32[16,32]{1,0:T(8,128)S(1)} %copy-done.16, s32[16,32]{1,0:T(8,128)S(1)} %copy-done.17, s32[1]{0:T(128)} %bitcast.33.branch_ref, f32[16,16,128]{2,1,0:T(8,128)S(1)} %parent_coef.1.refs_0_, f32[16,16,128]{2,1,0:T(8,128)S(1)} %collective-permute-done.5.refs_1_, ...), custom_call_target="tpu_custom_call" | custom-call | tf_op jit(solution)/shard_map/parent_field/pallas_call | solution.py:575
  71.4 6.0 %collective-permute-done.10.refs_0_.refs_2_.refs_3_ = f32[192,16,128]{2,1,0:T(8,128)S(1)} collective-permute-done((f32[192,16,128]{2,1,0:T(8,128)}, f32[192,16,128]{2,1,0:T(8,128)S(1)}, u32[]{:S(2)}, u32[]{:S(2)}) %collective-permute-start.10) | collective-permute-done | bytes 1572896 | tf_op jit(solution)/shard_map/ppermute | solution.py:318
  77.3 2.1 %collective-permute-done.8.refs_1_.refs_0_.refs_2_ = f32[192,16,128]{2,1,0:T(8,128)} collective-permute-done((f32[192,16,128]{2,1,0:T(8,128)}, f32[192,16,128]{2,1,0:T(8,128)}, u32[]{:S(2)}, u32[]{:S(2)}) %collective-permute-start.8) | collective-permute-done | bytes 1572896 | tf_op jit(solution)/shard_map/ppermute | solution.py:318
  79.4 1.9 %pack.8 = (f32[128,16,128]{2,1,0:T(8,128)S(1)}, f32[128,16,128]{2,1,0:T(8,128)S(1)}, f32[128,16,128]{2,1,0:T(8,128)S(1)}, f32[128,16,128]{2,1,0:T(8,128)S(1)}) custom-call(f32[192,16,128]{2,1,0:T(8,128)S(1)} %collective-permute-done.10.refs_0_.refs_2_.refs_3_, f32[192,16,128]{2,1,0:T(8,128)} %collective-permute-done.8.refs_1_.refs_0_.refs_2_, ...), custom_call_target="tpu_custom_call" | custom-call | flops 99999997952 | bytes 1000000000 | tf_op jit(solution)/shard_map/pack/pallas_call | solution.py:368
  81.4 2.7 %collective-permute-start.14 = (f32[128,16,128]{2,1,0:T(8,128)S(1)}, f32[128,16,128]{2,1,0:T(8,128)S(1)}, u32[]{:S(2)}, u32[]{:S(2)}) collective-permute-start(f32[128,16,128]{2,1,0:T(8,128)S(1)} %get-tuple-element.114), channel_id=1, source_target_pairs={{0,24},{1,25},{2,26},{3,27},{4,28},{5,29},{6,30},{7,31},{8,0},{9,1... | collective-permute-start | bytes 3145736 | tf_op jit(solution)/shard_map/ppermute | solution.py:318
  84.1 2.7 %collective-permute-start.16 = (f32[128,16,128]{2,1,0:T(8,128)S(1)}, f32[128,16,128]{2,1,0:T(8,128)S(1)}, u32[]{:S(2)}, u32[]{:S(2)}) collective-permute-start(f32[128,16,128]{2,1,0:T(8,128)S(1)} %get-tuple-element.116), channel_id=1, source_target_pairs={{0,6},{1,7},{2,0},{3,1},{4,2},{5,3},{6,4},{7,5},{8,14},{9,15},{10,... | collective-permute-start | bytes 3145736 | tf_op jit(solution)/shard_map/ppermute | solution.py:318
  86.8 2.3 %pack.11 = f32[768,16,128]{2,1,0:T(8,128)S(1)} custom-call(f32[192,16,128]{2,1,0:T(8,128)} %collective-permute-done.8.refs_1_.refs_0_.refs_2_, f32[192,16,128]{2,1,0:T(8,128)} %collective-permute-done.9.refs_2_.refs_1_.refs_0_, f32[192,16,128]{2,1,0:T(8,128)S(1)} %collective-permute-done.10.refs_0_.refs_2_.refs_3_, ...), custom_call_target="tpu_custom_call" | custom-call | tf_op jit(solution)/shard_map/pack/pallas_call | solution.py:368
  89.0 4.2 %pick.7.refs_2_ = bf16[384,32,128]{2,1,0:T(8,128)(2,1)S(1)} custom-call(s32[32,128]{1,0:T(8,128)S(1)} %get-tuple-element.149.code_ref, f32[192,16,128]{2,1,0:T(8,128)} %collective-permute-done.9.refs_2_.refs_1_.refs_0_, f32[192,16,128]{2,1,0:T(8,128)S(1)} %collective-permute-done.11.refs_3_.refs_1_, ...), custom_call_target="tpu_custom_call" | custom-call | tf_op jit(solution)/shard_map/pick/pallas_call | solution.py:144
  93.3 3.8 %collective-permute-start.17 = (f32[768,16,128]{2,1,0:T(8,128)S(1)}, f32[768,16,128]{2,1,0:T(8,128)S(1)}, u32[]{:S(2)}, u32[]{:S(2)}) collective-permute-start(f32[768,16,128]{2,1,0:T(8,128)S(1)} %pack.11), channel_id=1, source_target_pairs={{0,1},{1,0},{2,3},{3,2},{4,5},{5,4},{6,7},{7,6},{8,9},{9,8},{10,11... | collective-permute-start | bytes 18874376 | tf_op jit(solution)/shard_map/ppermute | solution.py:328
  97.1 4.0 %pick.6.refs_1_ = bf16[320,32,128]{2,1,0:T(8,128)(2,1)S(1)} custom-call(s32[32,128]{1,0:T(8,128)S(1)} %get-tuple-element.149.code_ref, f32[128,16,128]{2,1,0:T(8,128)} %collective-permute-done.4.refs_0_, f32[512,16,128]{2,1,0:T(8,128)S(1)} %collective-permute-done.12.refs_1_), custom_call_target="tpu_custom_call" | custom-call | tf_op jit(solution)/shard_map/pick/pallas_call | solution.py:144
  101.1 3.6 %collective-permute-done.13.refs_0_.refs_3_ = f32[128,16,128]{2,1,0:T(8,128)S(1)} collective-permute-done((f32[128,16,128]{2,1,0:T(8,128)S(1)}, f32[128,16,128]{2,1,0:T(8,128)S(1)}, u32[]{:S(2)}, u32[]{:S(2)}) %collective-permute-start.13) | collective-permute-done | bytes 1048608 | tf_op jit(solution)/shard_map/ppermute | solution.py:318
  104.7 2.1 %collective-permute-done.15.refs_2_.refs_1_ = f32[128,16,128]{2,1,0:T(8,128)S(1)} collective-permute-done((f32[128,16,128]{2,1,0:T(8,128)S(1)}, f32[128,16,128]{2,1,0:T(8,128)S(1)}, u32[]{:S(2)}, u32[]{:S(2)}) %collective-permute-start.15) | collective-permute-done | bytes 1048608 | tf_op jit(solution)/shard_map/ppermute | solution.py:318
  106.8 0.2 pack.10
  107.1 0.7 pack.13
  107.7 4.2 %collective-permute-start.22 = (f32[512,16,128]{2,1,0:T(8,128)S(1)}, f32[512,16,128]{2,1,0:T(8,128)S(1)}, u32[]{:S(2)}, u32[]{:S(2)}) collective-permute-start(f32[512,16,128]{2,1,0:T(8,128)S(1)} %pack.13), channel_id=1, source_target_pairs={{0,1},{1,0},{2,3},{3,2},{4,5},{5,4},{6,7},{7,6},{8,9},{9,8},{10,11... | collective-permute-start | bytes 12582920 | tf_op jit(solution)/shard_map/ppermute | solution.py:328
  111.9 2.7 %collective-permute-start.19 = (f32[32,16,128]{2,1,0:T(8,128)S(1)}, f32[32,16,128]{2,1,0:T(8,128)S(1)}, u32[]{:S(2)}, u32[]{:S(2)}) collective-permute-start(f32[32,16,128]{2,1,0:T(8,128)S(1)} %get-tuple-element.133), channel_id=1, source_target_pairs={{0,24},{1,25},{2,26},{3,27},{4,28},{5,29},{6,30},{7,31},{8,0},{9,1... | collective-permute-start | bytes 786440 | tf_op jit(solution)/shard_map/ppermute | solution.py:318
  114.6 2.7 %collective-permute-start.21 = (f32[32,16,128]{2,1,0:T(8,128)S(1)}, f32[32,16,128]{2,1,0:T(8,128)S(1)}, u32[]{:S(2)}, u32[]{:S(2)}) collective-permute-start(f32[32,16,128]{2,1,0:T(8,128)S(1)} %get-tuple-element.135), channel_id=1, source_target_pairs={{0,6},{1,7},{2,0},{3,1},{4,2},{5,3},{6,4},{7,5},{8,14},{9,15},{10,... | collective-permute-start | bytes 786440 | tf_op jit(solution)/shard_map/ppermute | solution.py:318
  117.2 3.6 %pick.8.refs_3_ = bf16[384,32,128]{2,1,0:T(8,128)(2,1)S(1)} custom-call(s32[32,128]{1,0:T(8,128)S(1)} %get-tuple-element.149.code_ref, f32[768,16,128]{2,1,0:T(8,128)S(1)} %collective-permute-done.17.refs_0_), custom_call_target="tpu_custom_call" | custom-call | tf_op jit(solution)/shard_map/pick/pallas_call | solution.py:144
  121.0 2.0 %collective-permute-done.20.refs_2_.refs_8_ = f32[32,16,128]{2,1,0:T(8,128)S(1)} collective-permute-done((f32[32,16,128]{2,1,0:T(8,128)S(1)}, f32[32,16,128]{2,1,0:T(8,128)S(1)}, u32[]{:S(2)}, u32[]{:S(2)}) %collective-permute-start.20) | collective-permute-done | bytes 262176 | tf_op jit(solution)/shard_map/ppermute | solution.py:318
  123.0 0.2 pack.12
  123.3 1.6 %collective-permute-start.23 = (f32[128,16,128]{2,1,0:T(8,128)S(1)}, f32[128,16,128]{2,1,0:T(8,128)S(1)}, u32[]{:S(2)}, u32[]{:S(2)}) collective-permute-start(f32[128,16,128]{2,1,0:T(8,128)S(1)} %pack.12), channel_id=1, source_target_pairs={{0,1},{1,0},{2,3},{3,2},{4,5},{5,4},{6,7},{7,6},{8,9},{9,8},{10,11... | collective-permute-start | bytes 3145736 | tf_op jit(solution)/shard_map/ppermute | solution.py:318
  124.9 2.7 %pick.9.refs_4_ = bf16[256,32,128]{2,1,0:T(8,128)(2,1)S(1)} custom-call(s32[32,128]{1,0:T(8,128)S(1)} %get-tuple-element.149.code_ref, f32[128,16,128]{2,1,0:T(8,128)S(1)} %collective-permute-done.14.refs_1_.refs_0_, f32[128,16,128]{2,1,0:T(8,128)S(1)} %collective-permute-done.15.refs_2_.refs_1_, ...), custom_call_target="tpu_custom_call" | custom-call | tf_op jit(solution)/shard_map/pick/pallas_call | solution.py:144
  127.6 12.3 %leaf_field_product.1 = f32[64,8192]{1,0:T(8,128)} custom-call(s32[128,16]{1,0:T(8,128)S(1)} %copy-done.15, s32[32,128]{1,0:T(8,128)S(1)} %get-tuple-element.149.code_ref, bf16[320,32,128]{2,1,0:T(8,128)(2,1)S(1)} %pick.5.refs_0_, bf16[320,32,128]{2,1,0:T(8,128)(2,1)S(1)} %pick.6.refs_1_, bf16[384,32,128]{2,1,0:T(8,128)(2,1)S(1)} %pick.7.refs_2_, ...), custom_call_target="tpu_custom_call" | custom-call | tf_op jit(solution)/shard_map/leaf_field_product/pallas_call | solution.py:274
  (66 shorter events, 0.9 us)
Async XLA Ops:
  0.0 12.4 %copy-start.19 = (f32[128,1024]{1,0:T(8,128)S(1)}, f32[128,1024]{1,0:T(8,128)}, u32[]{:S(2)}) copy-start(f32[128,1024]{1,0:T(8,128)} %param.11) | copy-start | bytes 1572868
  4.3 14.6 %copy-start.20 = (s32[128,16]{0,1:T(8,128)S(1)}, s32[128,16]{0,1:T(8,128)}, u32[]{:S(2)}) copy-start(s32[128,16]{0,1:T(8,128)} %param.13) | copy-start | bytes 24580
  4.3 14.7 %copy-start.21 = (s32[128,16]{0,1:T(8,128)S(1)}, s32[128,16]{0,1:T(8,128)}, u32[]{:S(2)}) copy-start(s32[128,16]{0,1:T(8,128)} %param.14) | copy-start | bytes 24580
  4.3 12.1 %collective-permute-start.4 = (f32[128,16,128]{2,1,0:T(8,128)}, f32[128,16,128]{2,1,0:T(8,128)}, u32[]{:S(2)}, u32[]{:S(2)}) collective-permute-start(f32[128,16,128]{2,1,0:T(8,128)} %get-tuple-element.83.refs_0_), channel_id=1, source_target_pairs={{0,1},{1,0},{2,3},{3,2},{4,5},{5,4},{6,7},{7,6},{8,9},{9,8},{10,11... | collective-permute-start | bytes 3145736 | tf_op jit(solution)/shard_map/ppermute | solution.py:328
  5.8 26.6 %collective-permute-start = (f32[128,16,128]{2,1,0:T(8,128)}, f32[128,16,128]{2,1,0:T(8,128)S(1)}, u32[]{:S(2)}, u32[]{:S(2)}) collective-permute-start(f32[128,16,128]{2,1,0:T(8,128)} %get-tuple-element.83.refs_0_), channel_id=1, source_target_pairs={{0,2},{1,3},{2,4},{3,5},{4,6},{5,7},{6,0},{7,1},{8,10},{9,11},{10,... | collective-permute-start | bytes 3145736 | tf_op jit(solution)/shard_map/ppermute | solution.py:318
  7.2 25.2 %collective-permute-start.1 = (f32[128,16,128]{2,1,0:T(8,128)}, f32[128,16,128]{2,1,0:T(8,128)S(1)}, u32[]{:S(2)}, u32[]{:S(2)}) collective-permute-start(f32[128,16,128]{2,1,0:T(8,128)} %get-tuple-element.83.refs_0_), channel_id=1, source_target_pairs={{0,6},{1,7},{2,0},{3,1},{4,2},{5,3},{6,4},{7,5},{8,14},{9,15},{10,... | collective-permute-start | bytes 3145736 | tf_op jit(solution)/shard_map/ppermute | solution.py:318
  8.6 27.1 %collective-permute-start.2 = (f32[128,16,128]{2,1,0:T(8,128)}, f32[128,16,128]{2,1,0:T(8,128)}, u32[]{:S(2)}, u32[]{:S(2)}) collective-permute-start(f32[128,16,128]{2,1,0:T(8,128)} %get-tuple-element.83.refs_0_), channel_id=1, source_target_pairs={{0,8},{1,9},{2,10},{3,11},{4,12},{5,13},{6,14},{7,15},{8,16},{9,17... | collective-permute-start | bytes 3145736 | tf_op jit(solution)/shard_map/ppermute | solution.py:318
  10.2 25.5 %collective-permute-start.3 = (f32[128,16,128]{2,1,0:T(8,128)}, f32[128,16,128]{2,1,0:T(8,128)}, u32[]{:S(2)}, u32[]{:S(2)}) collective-permute-start(f32[128,16,128]{2,1,0:T(8,128)} %get-tuple-element.83.refs_0_), channel_id=1, source_target_pairs={{0,24},{1,25},{2,26},{3,27},{4,28},{5,29},{6,30},{7,31},{8,0},{9,1... | collective-permute-start | bytes 3145736 | tf_op jit(solution)/shard_map/ppermute | solution.py:318
  12.4 27.9 %copy-start = (f32[1024,128]{1,0:T(8,128)}, f32[1024,128]{1,0:T(8,128)S(1)}, u32[]{:S(2)}) copy-start(f32[1024,128]{1,0:T(8,128)S(1)} %reshape.3.transfer_ref.refs_5_) | copy-start | bytes 1572868
  12.5 1.4 %copy-start.11 = (f32[64,32,128]{2,1,0:T(8,128)S(1)}, f32[64,32,128]{2,1,0:T(8,128)}, u32[]{:S(2)}) copy-start(f32[64,32,128]{2,1,0:T(8,128)} %get-tuple-element.90.pair_ref) | copy-start | bytes 3145732
  16.3 7.3 %collective-permute-start.5 = (f32[16,16,128]{2,1,0:T(8,128)S(1)}, f32[16,16,128]{2,1,0:T(8,128)S(1)}, u32[]{:S(2)}, u32[]{:S(2)}) collective-permute-start(f32[16,16,128]{2,1,0:T(8,128)S(1)} %parent_coef.1.refs_0_), channel_id=1, source_target_pairs={{0,96},{32,0},{64,32},{96,64},{1,97},{33,1},{65,33},{97,65},{2,98}... | collective-permute-start | bytes 393224 | tf_op jit(solution)/shard_map/ppermute | solution.py:328
  23.7 16.7 %copy-start.14 = (s32[128,16]{1,0:T(8,128)}, s32[128,16]{1,0:T(8,128)S(1)}, u32[]{:S(2)}) copy-start(s32[128,16]{1,0:T(8,128)S(1)} %get-tuple-element.148.pos_ref) | copy-start | bytes 24580
  23.7 5.4 %collective-permute-start.6 = (f32[16,16,128]{2,1,0:T(8,128)S(1)}, f32[16,16,128]{2,1,0:T(8,128)S(1)}, u32[]{:S(2)}, u32[]{:S(2)}) collective-permute-start(f32[16,16,128]{2,1,0:T(8,128)S(1)} %parent_coef.1.refs_0_), channel_id=1, source_target_pairs={{0,64},{32,96},{64,0},{96,32},{1,65},{33,97},{65,1},{97,33},{2,66}... | collective-permute-start | bytes 393224 | tf_op jit(solution)/shard_map/ppermute | solution.py:328
  29.1 11.3 %collective-permute-start.7 = (f32[16,16,128]{2,1,0:T(8,128)S(1)}, f32[16,16,128]{2,1,0:T(8,128)S(1)}, u32[]{:S(2)}, u32[]{:S(2)}) collective-permute-start(f32[16,16,128]{2,1,0:T(8,128)S(1)} %parent_coef.1.refs_0_), channel_id=1, source_target_pairs={{0,32},{32,64},{64,96},{96,0},{1,33},{33,65},{65,97},{97,1},{2,34}... | collective-permute-start | bytes 393224 | tf_op jit(solution)/shard_map/ppermute | solution.py:328
  32.3 8.0 %copy-start.3 = (f32[128,16,128]{2,1,0:T(8,128)}, f32[128,16,128]{2,1,0:T(8,128)S(1)}, u32[]{:S(2)}) copy-start(f32[128,16,128]{2,1,0:T(8,128)S(1)} %collective-permute-done.refs_1_.refs_0_.refs_2_) | copy-start | bytes 3145732
  32.3 8.0 %copy-start.6 = (f32[128,16,128]{2,1,0:T(8,128)}, f32[128,16,128]{2,1,0:T(8,128)S(1)}, u32[]{:S(2)}) copy-start(f32[128,16,128]{2,1,0:T(8,128)S(1)} %collective-permute-done.1.refs_0_.refs_1_) | copy-start | bytes 3145732
  40.4 0.7 copy-start.12
  41.0 36.3 %collective-permute-start.10 = (f32[192,16,128]{2,1,0:T(8,128)}, f32[192,16,128]{2,1,0:T(8,128)S(1)}, u32[]{:S(2)}, u32[]{:S(2)}) collective-permute-start(f32[192,16,128]{2,1,0:T(8,128)} %get-tuple-element.96), channel_id=1, source_target_pairs={{0,2},{1,3},{2,4},{3,5},{4,6},{5,7},{6,0},{7,1},{8,10},{9,11},{10,... | collective-permute-start | bytes 4718600 | tf_op jit(solution)/shard_map/ppermute | solution.py:318
  41.0 36.3 %collective-permute-start.11 = (f32[192,16,128]{2,1,0:T(8,128)}, f32[192,16,128]{2,1,0:T(8,128)S(1)}, u32[]{:S(2)}, u32[]{:S(2)}) collective-permute-start(f32[192,16,128]{2,1,0:T(8,128)} %get-tuple-element.97), channel_id=1, source_target_pairs={{0,6},{1,7},{2,0},{3,1},{4,2},{5,3},{6,4},{7,5},{8,14},{9,15},{10,... | collective-permute-start | bytes 4718600 | tf_op jit(solution)/shard_map/ppermute | solution.py:318
  43.7 35.7 %collective-permute-start.8 = (f32[192,16,128]{2,1,0:T(8,128)}, f32[192,16,128]{2,1,0:T(8,128)}, u32[]{:S(2)}, u32[]{:S(2)}) collective-permute-start(f32[192,16,128]{2,1,0:T(8,128)} %get-tuple-element.94), channel_id=1, source_target_pairs={{0,8},{1,9},{2,10},{3,11},{4,12},{5,13},{6,14},{7,15},{8,16},{9,17... | collective-permute-start | bytes 4718600 | tf_op jit(solution)/shard_map/ppermute | solution.py:318
  44.0 35.5 %collective-permute-start.9 = (f32[192,16,128]{2,1,0:T(8,128)}, f32[192,16,128]{2,1,0:T(8,128)}, u32[]{:S(2)}, u32[]{:S(2)}) collective-permute-start(f32[192,16,128]{2,1,0:T(8,128)} %get-tuple-element.95), channel_id=1, source_target_pairs={{0,24},{1,25},{2,26},{3,27},{4,28},{5,29},{6,30},{7,31},{8,0},{9,1... | collective-permute-start | bytes 4718600 | tf_op jit(solution)/shard_map/ppermute | solution.py:318
  46.4 1.2 copy-start.4
  47.6 1.2 copy-start.7
  48.8 2.0 %copy-start.5 = (f32[128,16,128]{2,1,0:T(8,128)S(1)}, f32[128,16,128]{2,1,0:T(8,128)}, u32[]{:S(2)}) copy-start(f32[128,16,128]{2,1,0:T(8,128)} %copy-done.3) | copy-start | bytes 3145732
  48.8 2.2 %copy-start.8 = (f32[128,16,128]{2,1,0:T(8,128)S(1)}, f32[128,16,128]{2,1,0:T(8,128)}, u32[]{:S(2)}) copy-start(f32[128,16,128]{2,1,0:T(8,128)} %copy-done.6) | copy-start | bytes 3145732
  48.8 2.5 %copy-start.10 = (f32[128,16,128]{2,1,0:T(8,128)S(1)}, f32[128,16,128]{2,1,0:T(8,128)}, u32[]{:S(2)}) copy-start(f32[128,16,128]{2,1,0:T(8,128)} %get-tuple-element.83.refs_0_) | copy-start | bytes 3145732
  51.3 5.4 %copy-start.1 = (f32[1024,128]{1,0:T(8,128)S(1)}, f32[1024,128]{1,0:T(8,128)}, u32[]{:S(2)}) copy-start(f32[1024,128]{1,0:T(8,128)} %copy-done) | copy-start | bytes 1572868
  51.3 5.4 %copy-start.9 = (f32[16,32,1024]{2,1,0:T(8,128)S(1)}, f32[16,32,1024]{2,1,0:T(8,128)}, u32[]{:S(2)}) copy-start(f32[16,32,1024]{2,1,0:T(8,128)} %refs_4_.1) | copy-start | bytes 6291460
  51.3 5.4 %copy-start.13 = (f32[16,16,128]{2,1,0:T(8,128)S(1)}, f32[16,16,128]{2,1,0:T(8,128)}, u32[]{:S(2)}) copy-start(f32[16,16,128]{2,1,0:T(8,128)} %copy-done.12) | copy-start | bytes 393220
  51.3 5.4 %copy-start.16 = (s32[16,32]{1,0:T(8,128)S(1)}, s32[16,32]{1,0:T(8,128)}, u32[]{:S(2)}) copy-start(s32[16,32]{1,0:T(8,128)} %list_ref.2) | copy-start | bytes 6148
  51.3 5.4 %copy-start.17 = (s32[16,32]{1,0:T(8,128)S(1)}, s32[16,32]{1,0:T(8,128)}, u32[]{:S(2)}) copy-start(s32[16,32]{1,0:T(8,128)} %mask_ref.2) | copy-start | bytes 6148
  54.4 26.9 %collective-permute-start.12 = (f32[512,16,128]{2,1,0:T(8,128)S(1)}, f32[512,16,128]{2,1,0:T(8,128)S(1)}, u32[]{:S(2)}, u32[]{:S(2)}) collective-permute-start(f32[512,16,128]{2,1,0:T(8,128)S(1)} %pack.9), channel_id=1, source_target_pairs={{0,1},{1,0},{2,3},{3,2},{4,5},{5,4},{6,7},{7,6},{8,9},{9,8},{10,11... | collective-permute-start | bytes 12582920 | tf_op jit(solution)/shard_map/ppermute | solution.py:328
  81.3 23.3 %collective-permute-start.13 = (f32[128,16,128]{2,1,0:T(8,128)S(1)}, f32[128,16,128]{2,1,0:T(8,128)S(1)}, u32[]{:S(2)}, u32[]{:S(2)}) collective-permute-start(f32[128,16,128]{2,1,0:T(8,128)S(1)} %get-tuple-element.113), channel_id=1, source_target_pairs={{0,8},{1,9},{2,10},{3,11},{4,12},{5,13},{6,14},{7,15},{8,16},{9,17... | collective-permute-start | bytes 3145736 | tf_op jit(solution)/shard_map/ppermute | solution.py:318
  81.4 23.3 %collective-permute-start.14 = (f32[128,16,128]{2,1,0:T(8,128)S(1)}, f32[128,16,128]{2,1,0:T(8,128)S(1)}, u32[]{:S(2)}, u32[]{:S(2)}) collective-permute-start(f32[128,16,128]{2,1,0:T(8,128)S(1)} %get-tuple-element.114), channel_id=1, source_target_pairs={{0,24},{1,25},{2,26},{3,27},{4,28},{5,29},{6,30},{7,31},{8,0},{9,1... | collective-permute-start | bytes 3145736 | tf_op jit(solution)/shard_map/ppermute | solution.py:318
  84.1 22.7 %collective-permute-start.15 = (f32[128,16,128]{2,1,0:T(8,128)S(1)}, f32[128,16,128]{2,1,0:T(8,128)S(1)}, u32[]{:S(2)}, u32[]{:S(2)}) collective-permute-start(f32[128,16,128]{2,1,0:T(8,128)S(1)} %get-tuple-element.115), channel_id=1, source_target_pairs={{0,2},{1,3},{2,4},{3,5},{4,6},{5,7},{6,0},{7,1},{8,10},{9,11},{10,... | collective-permute-start | bytes 3145736 | tf_op jit(solution)/shard_map/ppermute | solution.py:318
  84.1 22.7 %collective-permute-start.16 = (f32[128,16,128]{2,1,0:T(8,128)S(1)}, f32[128,16,128]{2,1,0:T(8,128)S(1)}, u32[]{:S(2)}, u32[]{:S(2)}) collective-permute-start(f32[128,16,128]{2,1,0:T(8,128)S(1)} %get-tuple-element.116), channel_id=1, source_target_pairs={{0,6},{1,7},{2,0},{3,1},{4,2},{5,3},{6,4},{7,5},{8,14},{9,15},{10,... | collective-permute-start | bytes 3145736 | tf_op jit(solution)/shard_map/ppermute | solution.py:318
  93.3 13.7 %collective-permute-start.17 = (f32[768,16,128]{2,1,0:T(8,128)S(1)}, f32[768,16,128]{2,1,0:T(8,128)S(1)}, u32[]{:S(2)}, u32[]{:S(2)}) collective-permute-start(f32[768,16,128]{2,1,0:T(8,128)S(1)} %pack.11), channel_id=1, source_target_pairs={{0,1},{1,0},{2,3},{3,2},{4,5},{5,4},{6,7},{7,6},{8,9},{9,8},{10,11... | collective-permute-start | bytes 18874376 | tf_op jit(solution)/shard_map/ppermute | solution.py:328
  107.7 15.5 %collective-permute-start.22 = (f32[512,16,128]{2,1,0:T(8,128)S(1)}, f32[512,16,128]{2,1,0:T(8,128)S(1)}, u32[]{:S(2)}, u32[]{:S(2)}) collective-permute-start(f32[512,16,128]{2,1,0:T(8,128)S(1)} %pack.13), channel_id=1, source_target_pairs={{0,1},{1,0},{2,3},{3,2},{4,5},{5,4},{6,7},{7,6},{8,9},{9,8},{10,11... | collective-permute-start | bytes 12582920 | tf_op jit(solution)/shard_map/ppermute | solution.py:328
  111.9 9.1 %collective-permute-start.18 = (f32[32,16,128]{2,1,0:T(8,128)S(1)}, f32[32,16,128]{2,1,0:T(8,128)S(1)}, u32[]{:S(2)}, u32[]{:S(2)}) collective-permute-start(f32[32,16,128]{2,1,0:T(8,128)S(1)} %get-tuple-element.132), channel_id=1, source_target_pairs={{0,8},{1,9},{2,10},{3,11},{4,12},{5,13},{6,14},{7,15},{8,16},{9,17... | collective-permute-start | bytes 786440 | tf_op jit(solution)/shard_map/ppermute | solution.py:318
  111.9 9.1 %collective-permute-start.19 = (f32[32,16,128]{2,1,0:T(8,128)S(1)}, f32[32,16,128]{2,1,0:T(8,128)S(1)}, u32[]{:S(2)}, u32[]{:S(2)}) collective-permute-start(f32[32,16,128]{2,1,0:T(8,128)S(1)} %get-tuple-element.133), channel_id=1, source_target_pairs={{0,24},{1,25},{2,26},{3,27},{4,28},{5,29},{6,30},{7,31},{8,0},{9,1... | collective-permute-start | bytes 786440 | tf_op jit(solution)/shard_map/ppermute | solution.py:318
  114.6 8.4 %collective-permute-start.20 = (f32[32,16,128]{2,1,0:T(8,128)S(1)}, f32[32,16,128]{2,1,0:T(8,128)S(1)}, u32[]{:S(2)}, u32[]{:S(2)}) collective-permute-start(f32[32,16,128]{2,1,0:T(8,128)S(1)} %get-tuple-element.134), channel_id=1, source_target_pairs={{0,2},{1,3},{2,4},{3,5},{4,6},{5,7},{6,0},{7,1},{8,10},{9,11},{10,... | collective-permute-start | bytes 786440 | tf_op jit(solution)/shard_map/ppermute | solution.py:318
  114.6 8.4 %collective-permute-start.21 = (f32[32,16,128]{2,1,0:T(8,128)S(1)}, f32[32,16,128]{2,1,0:T(8,128)S(1)}, u32[]{:S(2)}, u32[]{:S(2)}) collective-permute-start(f32[32,16,128]{2,1,0:T(8,128)S(1)} %get-tuple-element.135), channel_id=1, source_target_pairs={{0,6},{1,7},{2,0},{3,1},{4,2},{5,3},{6,4},{7,5},{8,14},{9,15},{10,... | collective-permute-start | bytes 786440 | tf_op jit(solution)/shard_map/ppermute | solution.py:318
  123.2 4.4 %copy-start.2 = (f32[32,8192]{1,0:T(8,128)S(1)}, f32[32,8192]{1,0:T(8,128)}, u32[]{:S(2)}) copy-start(f32[32,8192]{1,0:T(8,128)} %refs_13_.1) | copy-start | bytes 3145732
  123.2 4.4 %copy-start.15 = (s32[128,16]{1,0:T(8,128)S(1)}, s32[128,16]{1,0:T(8,128)}, u32[]{:S(2)}) copy-start(s32[128,16]{1,0:T(8,128)} %copy-done.14) | copy-start | bytes 24580
  123.3 4.3 %copy-start.18 = (f32[512,16,128]{2,1,0:T(8,128)}, f32[512,16,128]{2,1,0:T(8,128)S(1)}, u32[]{:S(2)}) copy-start(f32[512,16,128]{2,1,0:T(8,128)S(1)} %collective-permute-done.22.refs_5_) | copy-start | bytes 12582916
  123.3 4.3 %collective-permute-start.23 = (f32[128,16,128]{2,1,0:T(8,128)S(1)}, f32[128,16,128]{2,1,0:T(8,128)S(1)}, u32[]{:S(2)}, u32[]{:S(2)}) collective-permute-start(f32[128,16,128]{2,1,0:T(8,128)S(1)} %pack.12), channel_id=1, source_target_pairs={{0,1},{1,0},{2,3},{3,2},{4,5},{5,4},{6,7},{7,6},{8,9},{9,8},{10,11... | collective-permute-start | bytes 3145736 | tf_op jit(solution)/shard_map/ppermute | solution.py:318

commit v6 on v5

--- a/solution.py
+++ b/solution.py
@@ -252,13 +252,13 @@
     def _():
         totals[...] = jnp.zeros_like(totals)
 
-    @pl.loop(0, quads // 2)
+    @pl.loop(0, quads // 4)
     def _(turn):
-        for n in (0, 1):
-            quad = totals_first + 2 * turn + n
-            before = totals[1 - n]
+        for n in range(4):
+            quad = totals_first + 4 * turn + n
+            before = totals[1 - n % 2]
             for pair in range(4):
-                totals[n, pair * K : (pair + 1) * K] = pair_total(8 * turn + 4 * n + pair)
+                totals[n % 2, pair * K : (pair + 1) * K] = pair_total(16 * turn + 4 * n + pair)
             product(jnp.maximum(quad - 1, 0), before)
 
     @pl.when(step == pl.num_programs(0) - 1)

time: 140 us -> 140 us (level)
  no operation moved by 1% of the time
where the time goes in v6:
time: 140 us
  Pallas kernels  67 us (48%)
  starting transfers between devices  39.2 us (28%)
  waiting for transfers between devices  27.4 us (20%)
  local copies, waits for them, and re-layouts  5.46 us (4%)
    ppermute x17, starting transfers between devices, moved(): return (send(array, 'subtree', perm), out)  24.3 us
    ppermute x17, waiting for transfers between devices, moved(): return (send(array, 'subtree', perm), out)  22.5 us
    pallas_call x5, Pallas kernels, picked_slots(): pl.pallas_call(functools.partial(pick_kernel, plan, first), out_shape=jax...  17.6 us
    ppermute x7, starting transfers between devices, __call__(): self.last = lax.ppermute(array, axis, perm)  14.9 us
    pallas_call x1, Pallas kernels, downward_pairs(): pl.pallas_call(functools.partial(parent_field_kernel, group), out_shape=j...  14.6 us
    pallas_call x7, Pallas kernels, packed(): pl.pallas_call(functools.partial(pack_kernel, plan, len(arrays)), out_sha...  11.8 us
    pallas_call x1, Pallas kernels, products(): pl.pallas_call(functools.partial(field_kernel, slots, block, plan, len(ti...  11.7 us
    unnamed x46, local copies, waits for them, and re-layouts  5.26 us
  transfers between devices with their start and end apart: 24, of which 9 were waited for; matrix products, arithmetic and copies ran while one was open for 0% of the time, Pallas kernels for 36%

profile of v6, /device:TPU:1, one launch (start us, length us, event | category | flops | bytes accessed | tf_op | source)
XLA Modules:
  0.0 139.5 jit_solution(14248649184636861048)
XLA Ops:
  0.0 4.3 %leaf_coef.1 = (f32[128,16,128]{2,1,0:T(8,128)}, f32[64,32,128]{2,1,0:T(8,128)}) custom-call(f32[32,8192]{1,0:T(8,128)} %refs_13_.1, f32[64,8192]{1,0:T(8,128)} %vectors_ref.1), custom_call_target="tpu_custom_call" | custom-call | tf_op jit(solution)/shard_map/leaf_coef/pallas_call | solution.py:75
  4.3 1.5 %collective-permute-start.4 = (f32[128,16,128]{2,1,0:T(8,128)}, f32[128,16,128]{2,1,0:T(8,128)}, u32[]{:S(2)}, u32[]{:S(2)}) collective-permute-start(f32[128,16,128]{2,1,0:T(8,128)} %get-tuple-element.83.refs_0_), channel_id=1, source_target_pairs={{0,1},{1,0},{2,3},{3,2},{4,5},{5,4},{6,7},{7,6},{8,9},{9,8},{10,11... | collective-permute-start | bytes 3145736 | tf_op jit(solution)/shard_map/ppermute | solution.py:328
  5.8 1.4 %collective-permute-start = (f32[128,16,128]{2,1,0:T(8,128)}, f32[128,16,128]{2,1,0:T(8,128)S(1)}, u32[]{:S(2)}, u32[]{:S(2)}) collective-permute-start(f32[128,16,128]{2,1,0:T(8,128)} %get-tuple-element.83.refs_0_), channel_id=1, source_target_pairs={{0,2},{1,3},{2,4},{3,5},{4,6},{5,7},{6,0},{7,1},{8,10},{9,11},{10,... | collective-permute-start | bytes 3145736 | tf_op jit(solution)/shard_map/ppermute | solution.py:318
  7.2 1.4 %collective-permute-start.1 = (f32[128,16,128]{2,1,0:T(8,128)}, f32[128,16,128]{2,1,0:T(8,128)S(1)}, u32[]{:S(2)}, u32[]{:S(2)}) collective-permute-start(f32[128,16,128]{2,1,0:T(8,128)} %get-tuple-element.83.refs_0_), channel_id=1, source_target_pairs={{0,6},{1,7},{2,0},{3,1},{4,2},{5,3},{6,4},{7,5},{8,14},{9,15},{10,... | collective-permute-start | bytes 3145736 | tf_op jit(solution)/shard_map/ppermute | solution.py:318
  8.6 1.6 %collective-permute-start.2 = (f32[128,16,128]{2,1,0:T(8,128)}, f32[128,16,128]{2,1,0:T(8,128)}, u32[]{:S(2)}, u32[]{:S(2)}) collective-permute-start(f32[128,16,128]{2,1,0:T(8,128)} %get-tuple-element.83.refs_0_), channel_id=1, source_target_pairs={{0,8},{1,9},{2,10},{3,11},{4,12},{5,13},{6,14},{7,15},{8,16},{9,17... | collective-permute-start | bytes 3145736 | tf_op jit(solution)/shard_map/ppermute | solution.py:318
  10.2 2.1 %collective-permute-start.3 = (f32[128,16,128]{2,1,0:T(8,128)}, f32[128,16,128]{2,1,0:T(8,128)}, u32[]{:S(2)}, u32[]{:S(2)}) collective-permute-start(f32[128,16,128]{2,1,0:T(8,128)} %get-tuple-element.83.refs_0_), channel_id=1, source_target_pairs={{0,24},{1,25},{2,26},{3,27},{4,28},{5,29},{6,30},{7,31},{8,0},{9,1... | collective-permute-start | bytes 3145736 | tf_op jit(solution)/shard_map/ppermute | solution.py:318
  12.5 1.4 %copy-done.11 = f32[64,32,128]{2,1,0:T(8,128)S(1)} copy-done((f32[64,32,128]{2,1,0:T(8,128)S(1)}, f32[64,32,128]{2,1,0:T(8,128)}, u32[]{:S(2)}) %copy-start.11) | copy-done | bytes 1048600
  13.9 2.5 %parent_coef.1.refs_0_ = f32[16,16,128]{2,1,0:T(8,128)S(1)} custom-call(f32[64,32,128]{2,1,0:T(8,128)S(1)} %copy-done.11, f32[1024,128]{1,0:T(8,128)S(1)} %reshape.3.transfer_ref.refs_5_), custom_call_target="tpu_custom_call" | custom-call | tf_op jit(solution)/shard_map/parent_coef/pallas_call | solution.py:509
  16.3 2.5 %collective-permute-start.5 = (f32[16,16,128]{2,1,0:T(8,128)S(1)}, f32[16,16,128]{2,1,0:T(8,128)S(1)}, u32[]{:S(2)}, u32[]{:S(2)}) collective-permute-start(f32[16,16,128]{2,1,0:T(8,128)S(1)} %parent_coef.1.refs_0_), channel_id=1, source_target_pairs={{0,96},{32,0},{64,32},{96,64},{1,97},{33,1},{65,33},{97,65},{2,98}... | collective-permute-start | bytes 393224 | tf_op jit(solution)/shard_map/ppermute | solution.py:328
  19.2 4.4 %slot_order.1 = (s32[128,16]{1,0:T(8,128)S(1)}, s32[32,128]{1,0:T(8,128)S(1)}) custom-call(s32[1,128]{1,0:T(1,128)S(1)} %pad_bitcast_fusion.own_ref, s32[128,16]{1,0:T(8,128)S(1)} %copy.10.list_ref, s32[128,16]{1,0:T(8,128)S(1)} %copy.11.mask_ref), custom_call_target="tpu_custom_call" | custom-call | tf_op jit(solution)/shard_map/slot_order/pallas_call | solution.py:465
  23.7 0.6 collective-permute-start.6
  24.3 4.8 %collective-permute-done.6.refs_2_ = f32[16,16,128]{2,1,0:T(8,128)S(1)} collective-permute-done((f32[16,16,128]{2,1,0:T(8,128)S(1)}, f32[16,16,128]{2,1,0:T(8,128)S(1)}, u32[]{:S(2)}, u32[]{:S(2)}) %collective-permute-start.6) | collective-permute-done | bytes 131104 | tf_op jit(solution)/shard_map/ppermute | solution.py:328
  29.1 3.2 %collective-permute-done.refs_1_.refs_0_.refs_2_ = f32[128,16,128]{2,1,0:T(8,128)S(1)} collective-permute-done((f32[128,16,128]{2,1,0:T(8,128)}, f32[128,16,128]{2,1,0:T(8,128)S(1)}, u32[]{:S(2)}, u32[]{:S(2)}) %collective-permute-start) | collective-permute-done | bytes 1048608 | tf_op jit(solution)/shard_map/ppermute | solution.py:318
  32.3 3.4 %collective-permute-done.2.refs_2_.refs_4_ = f32[128,16,128]{2,1,0:T(8,128)} collective-permute-done((f32[128,16,128]{2,1,0:T(8,128)}, f32[128,16,128]{2,1,0:T(8,128)}, u32[]{:S(2)}, u32[]{:S(2)}) %collective-permute-start.2) | collective-permute-done | bytes 1048608 | tf_op jit(solution)/shard_map/ppermute | solution.py:318
  35.7 4.6 %pack.7 = (f32[192,16,128]{2,1,0:T(8,128)}, f32[192,16,128]{2,1,0:T(8,128)}, f32[192,16,128]{2,1,0:T(8,128)}, f32[192,16,128]{2,1,0:T(8,128)}) custom-call(f32[128,16,128]{2,1,0:T(8,128)S(1)} %collective-permute-done.1.refs_0_.refs_1_, f32[128,16,128]{2,1,0:T(8,128)S(1)} %collective-permute-done.refs_1_.refs_0_.refs_2_, ...), custom_call_target="tpu_custom_call" | custom-call | flops 99999997952 | bytes 1000000000 | tf_op jit(solution)/shard_map/pack/pallas_call | solution.py:368
  40.4 0.6 copy-done.12
  41.0 2.7 %collective-permute-start.11 = (f32[192,16,128]{2,1,0:T(8,128)}, f32[192,16,128]{2,1,0:T(8,128)S(1)}, u32[]{:S(2)}, u32[]{:S(2)}) collective-permute-start(f32[192,16,128]{2,1,0:T(8,128)} %get-tuple-element.97), channel_id=1, source_target_pairs={{0,6},{1,7},{2,0},{3,1},{4,2},{5,3},{6,4},{7,5},{8,14},{9,15},{10,... | collective-permute-start | bytes 4718600 | tf_op jit(solution)/shard_map/ppermute | solution.py:318
  43.7 0.3 collective-permute-start.8
  44.0 2.4 %collective-permute-start.9 = (f32[192,16,128]{2,1,0:T(8,128)}, f32[192,16,128]{2,1,0:T(8,128)}, u32[]{:S(2)}, u32[]{:S(2)}) collective-permute-start(f32[192,16,128]{2,1,0:T(8,128)} %get-tuple-element.95), channel_id=1, source_target_pairs={{0,24},{1,25},{2,26},{3,27},{4,28},{5,29},{6,30},{7,31},{8,0},{9,1... | collective-permute-start | bytes 4718600 | tf_op jit(solution)/shard_map/ppermute | solution.py:318
  46.4 1.2 copy-done.4
  47.6 1.2 copy-done.7
  48.8 2.0 %pack.9 = f32[512,16,128]{2,1,0:T(8,128)S(1)} custom-call(f32[128,16,128]{2,1,0:T(8,128)S(1)} %copy-done.4, f32[128,16,128]{2,1,0:T(8,128)S(1)} %copy-done.7, f32[128,16,128]{2,1,0:T(8,128)} %collective-permute-done.2.refs_2_.refs_4_, f32[128,16,128]{2,1,0:T(8,128)} %collective-permute-done.3.refs_3_), custom_call_target="tpu_custom_call" | custom-call | tf_op jit(solution)/shard_map/pack/pallas_call | solution.py:368
  51.0 0.3 copy-done.10
  51.3 3.1 %pick.5.refs_0_ = bf16[320,32,128]{2,1,0:T(8,128)(2,1)S(1)} custom-call(s32[32,128]{1,0:T(8,128)S(1)} %get-tuple-element.149.code_ref, f32[128,16,128]{2,1,0:T(8,128)S(1)} %copy-done.10, f32[128,16,128]{2,1,0:T(8,128)S(1)} %copy-done.8, f32[128,16,128]{2,1,0:T(8,128)S(1)} %copy-done.5, f32[128,16,128]{2,1,0:T(8,128)} %collective-permute-done.3.refs_3_, ...), custom_call_target="tpu_custom_call" | custom-call | tf_op jit(solution)/shard_map/pick/pallas_call | solution.py:144
  54.4 2.3 %collective-permute-start.12 = (f32[512,16,128]{2,1,0:T(8,128)S(1)}, f32[512,16,128]{2,1,0:T(8,128)S(1)}, u32[]{:S(2)}, u32[]{:S(2)}) collective-permute-start(f32[512,16,128]{2,1,0:T(8,128)S(1)} %pack.9), channel_id=1, source_target_pairs={{0,1},{1,0},{2,3},{3,2},{4,5},{5,4},{6,7},{7,6},{8,9},{9,8},{10,11... | collective-permute-start | bytes 12582920 | tf_op jit(solution)/shard_map/ppermute | solution.py:328
  56.7 14.6 %parent_field.1.refs_12_ = f32[64,32,128]{2,1,0:T(8,128)S(1)} custom-call(s32[16,32]{1,0:T(8,128)S(1)} %copy-done.16, s32[16,32]{1,0:T(8,128)S(1)} %copy-done.17, s32[1]{0:T(128)} %bitcast.33.branch_ref, f32[16,16,128]{2,1,0:T(8,128)S(1)} %parent_coef.1.refs_0_, f32[16,16,128]{2,1,0:T(8,128)S(1)} %collective-permute-done.5.refs_1_, ...), custom_call_target="tpu_custom_call" | custom-call | tf_op jit(solution)/shard_map/parent_field/pallas_call | solution.py:575
  71.4 6.0 %collective-permute-done.10.refs_0_.refs_2_.refs_3_ = f32[192,16,128]{2,1,0:T(8,128)S(1)} collective-permute-done((f32[192,16,128]{2,1,0:T(8,128)}, f32[192,16,128]{2,1,0:T(8,128)S(1)}, u32[]{:S(2)}, u32[]{:S(2)}) %collective-permute-start.10) | collective-permute-done | bytes 1572896 | tf_op jit(solution)/shard_map/ppermute | solution.py:318
  77.3 2.1 %collective-permute-done.8.refs_1_.refs_0_.refs_2_ = f32[192,16,128]{2,1,0:T(8,128)} collective-permute-done((f32[192,16,128]{2,1,0:T(8,128)}, f32[192,16,128]{2,1,0:T(8,128)}, u32[]{:S(2)}, u32[]{:S(2)}) %collective-permute-start.8) | collective-permute-done | bytes 1572896 | tf_op jit(solution)/shard_map/ppermute | solution.py:318
  79.4 1.9 %pack.8 = (f32[128,16,128]{2,1,0:T(8,128)S(1)}, f32[128,16,128]{2,1,0:T(8,128)S(1)}, f32[128,16,128]{2,1,0:T(8,128)S(1)}, f32[128,16,128]{2,1,0:T(8,128)S(1)}) custom-call(f32[192,16,128]{2,1,0:T(8,128)S(1)} %collective-permute-done.10.refs_0_.refs_2_.refs_3_, f32[192,16,128]{2,1,0:T(8,128)} %collective-permute-done.8.refs_1_.refs_0_.refs_2_, ...), custom_call_target="tpu_custom_call" | custom-call | flops 99999997952 | bytes 1000000000 | tf_op jit(solution)/shard_map/pack/pallas_call | solution.py:368
  81.4 2.7 %collective-permute-start.14 = (f32[128,16,128]{2,1,0:T(8,128)S(1)}, f32[128,16,128]{2,1,0:T(8,128)S(1)}, u32[]{:S(2)}, u32[]{:S(2)}) collective-permute-start(f32[128,16,128]{2,1,0:T(8,128)S(1)} %get-tuple-element.114), channel_id=1, source_target_pairs={{0,24},{1,25},{2,26},{3,27},{4,28},{5,29},{6,30},{7,31},{8,0},{9,1... | collective-permute-start | bytes 3145736 | tf_op jit(solution)/shard_map/ppermute | solution.py:318
  84.1 2.7 %collective-permute-start.16 = (f32[128,16,128]{2,1,0:T(8,128)S(1)}, f32[128,16,128]{2,1,0:T(8,128)S(1)}, u32[]{:S(2)}, u32[]{:S(2)}) collective-permute-start(f32[128,16,128]{2,1,0:T(8,128)S(1)} %get-tuple-element.116), channel_id=1, source_target_pairs={{0,6},{1,7},{2,0},{3,1},{4,2},{5,3},{6,4},{7,5},{8,14},{9,15},{10,... | collective-permute-start | bytes 3145736 | tf_op jit(solution)/shard_map/ppermute | solution.py:318
  86.8 2.3 %pack.11 = f32[768,16,128]{2,1,0:T(8,128)S(1)} custom-call(f32[192,16,128]{2,1,0:T(8,128)} %collective-permute-done.8.refs_1_.refs_0_.refs_2_, f32[192,16,128]{2,1,0:T(8,128)} %collective-permute-done.9.refs_2_.refs_1_.refs_0_, f32[192,16,128]{2,1,0:T(8,128)S(1)} %collective-permute-done.10.refs_0_.refs_2_.refs_3_, ...), custom_call_target="tpu_custom_call" | custom-call | tf_op jit(solution)/shard_map/pack/pallas_call | solution.py:368
  89.0 4.2 %pick.7.refs_2_ = bf16[384,32,128]{2,1,0:T(8,128)(2,1)S(1)} custom-call(s32[32,128]{1,0:T(8,128)S(1)} %get-tuple-element.149.code_ref, f32[192,16,128]{2,1,0:T(8,128)} %collective-permute-done.9.refs_2_.refs_1_.refs_0_, f32[192,16,128]{2,1,0:T(8,128)S(1)} %collective-permute-done.11.refs_3_.refs_1_, ...), custom_call_target="tpu_custom_call" | custom-call | tf_op jit(solution)/shard_map/pick/pallas_call | solution.py:144
  93.3 3.8 %collective-permute-start.17 = (f32[768,16,128]{2,1,0:T(8,128)S(1)}, f32[768,16,128]{2,1,0:T(8,128)S(1)}, u32[]{:S(2)}, u32[]{:S(2)}) collective-permute-start(f32[768,16,128]{2,1,0:T(8,128)S(1)} %pack.11), channel_id=1, source_target_pairs={{0,1},{1,0},{2,3},{3,2},{4,5},{5,4},{6,7},{7,6},{8,9},{9,8},{10,11... | collective-permute-start | bytes 18874376 | tf_op jit(solution)/shard_map/ppermute | solution.py:328
  97.1 4.0 %pick.6.refs_1_ = bf16[320,32,128]{2,1,0:T(8,128)(2,1)S(1)} custom-call(s32[32,128]{1,0:T(8,128)S(1)} %get-tuple-element.149.code_ref, f32[128,16,128]{2,1,0:T(8,128)} %collective-permute-done.4.refs_0_, f32[512,16,128]{2,1,0:T(8,128)S(1)} %collective-permute-done.12.refs_1_), custom_call_target="tpu_custom_call" | custom-call | tf_op jit(solution)/shard_map/pick/pallas_call | solution.py:144
  101.1 3.6 %collective-permute-done.13.refs_0_.refs_3_ = f32[128,16,128]{2,1,0:T(8,128)S(1)} collective-permute-done((f32[128,16,128]{2,1,0:T(8,128)S(1)}, f32[128,16,128]{2,1,0:T(8,128)S(1)}, u32[]{:S(2)}, u32[]{:S(2)}) %collective-permute-start.13) | collective-permute-done | bytes 1048608 | tf_op jit(solution)/shard_map/ppermute | solution.py:318
  104.7 2.1 %collective-permute-done.15.refs_2_.refs_1_ = f32[128,16,128]{2,1,0:T(8,128)S(1)} collective-permute-done((f32[128,16,128]{2,1,0:T(8,128)S(1)}, f32[128,16,128]{2,1,0:T(8,128)S(1)}, u32[]{:S(2)}, u32[]{:S(2)}) %collective-permute-start.15) | collective-permute-done | bytes 1048608 | tf_op jit(solution)/shard_map/ppermute | solution.py:318
  106.8 0.2 pack.10
  107.1 0.7 pack.13
  107.7 4.2 %collective-permute-start.22 = (f32[512,16,128]{2,1,0:T(8,128)S(1)}, f32[512,16,128]{2,1,0:T(8,128)S(1)}, u32[]{:S(2)}, u32[]{:S(2)}) collective-permute-start(f32[512,16,128]{2,1,0:T(8,128)S(1)} %pack.13), channel_id=1, source_target_pairs={{0,1},{1,0},{2,3},{3,2},{4,5},{5,4},{6,7},{7,6},{8,9},{9,8},{10,11... | collective-permute-start | bytes 12582920 | tf_op jit(solution)/shard_map/ppermute | solution.py:328
  111.9 2.7 %collective-permute-start.19 = (f32[32,16,128]{2,1,0:T(8,128)S(1)}, f32[32,16,128]{2,1,0:T(8,128)S(1)}, u32[]{:S(2)}, u32[]{:S(2)}) collective-permute-start(f32[32,16,128]{2,1,0:T(8,128)S(1)} %get-tuple-element.133), channel_id=1, source_target_pairs={{0,24},{1,25},{2,26},{3,27},{4,28},{5,29},{6,30},{7,31},{8,0},{9,1... | collective-permute-start | bytes 786440 | tf_op jit(solution)/shard_map/ppermute | solution.py:318
  114.6 2.7 %collective-permute-start.21 = (f32[32,16,128]{2,1,0:T(8,128)S(1)}, f32[32,16,128]{2,1,0:T(8,128)S(1)}, u32[]{:S(2)}, u32[]{:S(2)}) collective-permute-start(f32[32,16,128]{2,1,0:T(8,128)S(1)} %get-tuple-element.135), channel_id=1, source_target_pairs={{0,6},{1,7},{2,0},{3,1},{4,2},{5,3},{6,4},{7,5},{8,14},{9,15},{10,... | collective-permute-start | bytes 786440 | tf_op jit(solution)/shard_map/ppermute | solution.py:318
  117.2 3.6 %pick.8.refs_3_ = bf16[384,32,128]{2,1,0:T(8,128)(2,1)S(1)} custom-call(s32[32,128]{1,0:T(8,128)S(1)} %get-tuple-element.149.code_ref, f32[768,16,128]{2,1,0:T(8,128)S(1)} %collective-permute-done.17.refs_0_), custom_call_target="tpu_custom_call" | custom-call | tf_op jit(solution)/shard_map/pick/pallas_call | solution.py:144
  121.0 2.0 %collective-permute-done.20.refs_2_.refs_8_ = f32[32,16,128]{2,1,0:T(8,128)S(1)} collective-permute-done((f32[32,16,128]{2,1,0:T(8,128)S(1)}, f32[32,16,128]{2,1,0:T(8,128)S(1)}, u32[]{:S(2)}, u32[]{:S(2)}) %collective-permute-start.20) | collective-permute-done | bytes 262176 | tf_op jit(solution)/shard_map/ppermute | solution.py:318
  123.0 0.2 pack.12
  123.3 1.6 %collective-permute-start.23 = (f32[128,16,128]{2,1,0:T(8,128)S(1)}, f32[128,16,128]{2,1,0:T(8,128)S(1)}, u32[]{:S(2)}, u32[]{:S(2)}) collective-permute-start(f32[128,16,128]{2,1,0:T(8,128)S(1)} %pack.12), channel_id=1, source_target_pairs={{0,1},{1,0},{2,3},{3,2},{4,5},{5,4},{6,7},{7,6},{8,9},{9,8},{10,11... | collective-permute-start | bytes 3145736 | tf_op jit(solution)/shard_map/ppermute | solution.py:318
  124.9 2.7 %pick.9.refs_4_ = bf16[256,32,128]{2,1,0:T(8,128)(2,1)S(1)} custom-call(s32[32,128]{1,0:T(8,128)S(1)} %get-tuple-element.149.code_ref, f32[128,16,128]{2,1,0:T(8,128)S(1)} %collective-permute-done.14.refs_1_.refs_0_, f32[128,16,128]{2,1,0:T(8,128)S(1)} %collective-permute-done.15.refs_2_.refs_1_, ...), custom_call_target="tpu_custom_call" | custom-call | tf_op jit(solution)/shard_map/pick/pallas_call | solution.py:144
  127.6 11.7 %leaf_field_product.1 = f32[64,8192]{1,0:T(8,128)} custom-call(s32[128,16]{1,0:T(8,128)S(1)} %copy-done.15, s32[32,128]{1,0:T(8,128)S(1)} %get-tuple-element.149.code_ref, bf16[320,32,128]{2,1,0:T(8,128)(2,1)S(1)} %pick.5.refs_0_, bf16[320,32,128]{2,1,0:T(8,128)(2,1)S(1)} %pick.6.refs_1_, bf16[384,32,128]{2,1,0:T(8,128)(2,1)S(1)} %pick.7.refs_2_, ...), custom_call_target="tpu_custom_call" | custom-call | tf_op jit(solution)/shard_map/leaf_field_product/pallas_call | solution.py:274
  (66 shorter events, 0.9 us)
Async XLA Ops:
  0.0 12.4 %copy-start.19 = (f32[128,1024]{1,0:T(8,128)S(1)}, f32[128,1024]{1,0:T(8,128)}, u32[]{:S(2)}) copy-start(f32[128,1024]{1,0:T(8,128)} %param.11) | copy-start | bytes 1572868
  4.3 14.6 %copy-start.20 = (s32[128,16]{0,1:T(8,128)S(1)}, s32[128,16]{0,1:T(8,128)}, u32[]{:S(2)}) copy-start(s32[128,16]{0,1:T(8,128)} %param.13) | copy-start | bytes 24580
  4.3 14.7 %copy-start.21 = (s32[128,16]{0,1:T(8,128)S(1)}, s32[128,16]{0,1:T(8,128)}, u32[]{:S(2)}) copy-start(s32[128,16]{0,1:T(8,128)} %param.14) | copy-start | bytes 24580
  4.3 12.1 %collective-permute-start.4 = (f32[128,16,128]{2,1,0:T(8,128)}, f32[128,16,128]{2,1,0:T(8,128)}, u32[]{:S(2)}, u32[]{:S(2)}) collective-permute-start(f32[128,16,128]{2,1,0:T(8,128)} %get-tuple-element.83.refs_0_), channel_id=1, source_target_pairs={{0,1},{1,0},{2,3},{3,2},{4,5},{5,4},{6,7},{7,6},{8,9},{9,8},{10,11... | collective-permute-start | bytes 3145736 | tf_op jit(solution)/shard_map/ppermute | solution.py:328
  5.8 26.6 %collective-permute-start = (f32[128,16,128]{2,1,0:T(8,128)}, f32[128,16,128]{2,1,0:T(8,128)S(1)}, u32[]{:S(2)}, u32[]{:S(2)}) collective-permute-start(f32[128,16,128]{2,1,0:T(8,128)} %get-tuple-element.83.refs_0_), channel_id=1, source_target_pairs={{0,2},{1,3},{2,4},{3,5},{4,6},{5,7},{6,0},{7,1},{8,10},{9,11},{10,... | collective-permute-start | bytes 3145736 | tf_op jit(solution)/shard_map/ppermute | solution.py:318
  7.2 25.2 %collective-permute-start.1 = (f32[128,16,128]{2,1,0:T(8,128)}, f32[128,16,128]{2,1,0:T(8,128)S(1)}, u32[]{:S(2)}, u32[]{:S(2)}) collective-permute-start(f32[128,16,128]{2,1,0:T(8,128)} %get-tuple-element.83.refs_0_), channel_id=1, source_target_pairs={{0,6},{1,7},{2,0},{3,1},{4,2},{5,3},{6,4},{7,5},{8,14},{9,15},{10,... | collective-permute-start | bytes 3145736 | tf_op jit(solution)/shard_map/ppermute | solution.py:318
  8.6 27.1 %collective-permute-start.2 = (f32[128,16,128]{2,1,0:T(8,128)}, f32[128,16,128]{2,1,0:T(8,128)}, u32[]{:S(2)}, u32[]{:S(2)}) collective-permute-start(f32[128,16,128]{2,1,0:T(8,128)} %get-tuple-element.83.refs_0_), channel_id=1, source_target_pairs={{0,8},{1,9},{2,10},{3,11},{4,12},{5,13},{6,14},{7,15},{8,16},{9,17... | collective-permute-start | bytes 3145736 | tf_op jit(solution)/shard_map/ppermute | solution.py:318
  10.2 25.5 %collective-permute-start.3 = (f32[128,16,128]{2,1,0:T(8,128)}, f32[128,16,128]{2,1,0:T(8,128)}, u32[]{:S(2)}, u32[]{:S(2)}) collective-permute-start(f32[128,16,128]{2,1,0:T(8,128)} %get-tuple-element.83.refs_0_), channel_id=1, source_target_pairs={{0,24},{1,25},{2,26},{3,27},{4,28},{5,29},{6,30},{7,31},{8,0},{9,1... | collective-permute-start | bytes 3145736 | tf_op jit(solution)/shard_map/ppermute | solution.py:318
  12.4 27.9 %copy-start = (f32[1024,128]{1,0:T(8,128)}, f32[1024,128]{1,0:T(8,128)S(1)}, u32[]{:S(2)}) copy-start(f32[1024,128]{1,0:T(8,128)S(1)} %reshape.3.transfer_ref.refs_5_) | copy-start | bytes 1572868
  12.5 1.4 %copy-start.11 = (f32[64,32,128]{2,1,0:T(8,128)S(1)}, f32[64,32,128]{2,1,0:T(8,128)}, u32[]{:S(2)}) copy-start(f32[64,32,128]{2,1,0:T(8,128)} %get-tuple-element.90.pair_ref) | copy-start | bytes 3145732
  16.3 7.3 %collective-permute-start.5 = (f32[16,16,128]{2,1,0:T(8,128)S(1)}, f32[16,16,128]{2,1,0:T(8,128)S(1)}, u32[]{:S(2)}, u32[]{:S(2)}) collective-permute-start(f32[16,16,128]{2,1,0:T(8,128)S(1)} %parent_coef.1.refs_0_), channel_id=1, source_target_pairs={{0,96},{32,0},{64,32},{96,64},{1,97},{33,1},{65,33},{97,65},{2,98}... | collective-permute-start | bytes 393224 | tf_op jit(solution)/shard_map/ppermute | solution.py:328
  23.7 16.7 %copy-start.14 = (s32[128,16]{1,0:T(8,128)}, s32[128,16]{1,0:T(8,128)S(1)}, u32[]{:S(2)}) copy-start(s32[128,16]{1,0:T(8,128)S(1)} %get-tuple-element.148.pos_ref) | copy-start | bytes 24580
  23.7 5.4 %collective-permute-start.6 = (f32[16,16,128]{2,1,0:T(8,128)S(1)}, f32[16,16,128]{2,1,0:T(8,128)S(1)}, u32[]{:S(2)}, u32[]{:S(2)}) collective-permute-start(f32[16,16,128]{2,1,0:T(8,128)S(1)} %parent_coef.1.refs_0_), channel_id=1, source_target_pairs={{0,64},{32,96},{64,0},{96,32},{1,65},{33,97},{65,1},{97,33},{2,66}... | collective-permute-start | bytes 393224 | tf_op jit(solution)/shard_map/ppermute | solution.py:328
  29.1 11.3 %collective-permute-start.7 = (f32[16,16,128]{2,1,0:T(8,128)S(1)}, f32[16,16,128]{2,1,0:T(8,128)S(1)}, u32[]{:S(2)}, u32[]{:S(2)}) collective-permute-start(f32[16,16,128]{2,1,0:T(8,128)S(1)} %parent_coef.1.refs_0_), channel_id=1, source_target_pairs={{0,32},{32,64},{64,96},{96,0},{1,33},{33,65},{65,97},{97,1},{2,34}... | collective-permute-start | bytes 393224 | tf_op jit(solution)/shard_map/ppermute | solution.py:328
  32.3 8.0 %copy-start.3 = (f32[128,16,128]{2,1,0:T(8,128)}, f32[128,16,128]{2,1,0:T(8,128)S(1)}, u32[]{:S(2)}) copy-start(f32[128,16,128]{2,1,0:T(8,128)S(1)} %collective-permute-done.refs_1_.refs_0_.refs_2_) | copy-start | bytes 3145732
  32.3 8.0 %copy-start.6 = (f32[128,16,128]{2,1,0:T(8,128)}, f32[128,16,128]{2,1,0:T(8,128)S(1)}, u32[]{:S(2)}) copy-start(f32[128,16,128]{2,1,0:T(8,128)S(1)} %collective-permute-done.1.refs_0_.refs_1_) | copy-start | bytes 3145732
  40.4 0.7 copy-start.12
  41.0 36.3 %collective-permute-start.10 = (f32[192,16,128]{2,1,0:T(8,128)}, f32[192,16,128]{2,1,0:T(8,128)S(1)}, u32[]{:S(2)}, u32[]{:S(2)}) collective-permute-start(f32[192,16,128]{2,1,0:T(8,128)} %get-tuple-element.96), channel_id=1, source_target_pairs={{0,2},{1,3},{2,4},{3,5},{4,6},{5,7},{6,0},{7,1},{8,10},{9,11},{10,... | collective-permute-start | bytes 4718600 | tf_op jit(solution)/shard_map/ppermute | solution.py:318
  41.0 36.3 %collective-permute-start.11 = (f32[192,16,128]{2,1,0:T(8,128)}, f32[192,16,128]{2,1,0:T(8,128)S(1)}, u32[]{:S(2)}, u32[]{:S(2)}) collective-permute-start(f32[192,16,128]{2,1,0:T(8,128)} %get-tuple-element.97), channel_id=1, source_target_pairs={{0,6},{1,7},{2,0},{3,1},{4,2},{5,3},{6,4},{7,5},{8,14},{9,15},{10,... | collective-permute-start | bytes 4718600 | tf_op jit(solution)/shard_map/ppermute | solution.py:318
  43.7 35.7 %collective-permute-start.8 = (f32[192,16,128]{2,1,0:T(8,128)}, f32[192,16,128]{2,1,0:T(8,128)}, u32[]{:S(2)}, u32[]{:S(2)}) collective-permute-start(f32[192,16,128]{2,1,0:T(8,128)} %get-tuple-element.94), channel_id=1, source_target_pairs={{0,8},{1,9},{2,10},{3,11},{4,12},{5,13},{6,14},{7,15},{8,16},{9,17... | collective-permute-start | bytes 4718600 | tf_op jit(solution)/shard_map/ppermute | solution.py:318
  44.0 35.5 %collective-permute-start.9 = (f32[192,16,128]{2,1,0:T(8,128)}, f32[192,16,128]{2,1,0:T(8,128)}, u32[]{:S(2)}, u32[]{:S(2)}) collective-permute-start(f32[192,16,128]{2,1,0:T(8,128)} %get-tuple-element.95), channel_id=1, source_target_pairs={{0,24},{1,25},{2,26},{3,27},{4,28},{5,29},{6,30},{7,31},{8,0},{9,1... | collective-permute-start | bytes 4718600 | tf_op jit(solution)/shard_map/ppermute | solution.py:318
  46.4 1.2 copy-start.4
  47.6 1.2 copy-start.7
  48.8 2.0 %copy-start.5 = (f32[128,16,128]{2,1,0:T(8,128)S(1)}, f32[128,16,128]{2,1,0:T(8,128)}, u32[]{:S(2)}) copy-start(f32[128,16,128]{2,1,0:T(8,128)} %copy-done.3) | copy-start | bytes 3145732
  48.8 2.2 %copy-start.8 = (f32[128,16,128]{2,1,0:T(8,128)S(1)}, f32[128,16,128]{2,1,0:T(8,128)}, u32[]{:S(2)}) copy-start(f32[128,16,128]{2,1,0:T(8,128)} %copy-done.6) | copy-start | bytes 3145732
  48.8 2.5 %copy-start.10 = (f32[128,16,128]{2,1,0:T(8,128)S(1)}, f32[128,16,128]{2,1,0:T(8,128)}, u32[]{:S(2)}) copy-start(f32[128,16,128]{2,1,0:T(8,128)} %get-tuple-element.83.refs_0_) | copy-start | bytes 3145732
  51.3 5.4 %copy-start.1 = (f32[1024,128]{1,0:T(8,128)S(1)}, f32[1024,128]{1,0:T(8,128)}, u32[]{:S(2)}) copy-start(f32[1024,128]{1,0:T(8,128)} %copy-done) | copy-start | bytes 1572868
  51.3 5.4 %copy-start.9 = (f32[16,32,1024]{2,1,0:T(8,128)S(1)}, f32[16,32,1024]{2,1,0:T(8,128)}, u32[]{:S(2)}) copy-start(f32[16,32,1024]{2,1,0:T(8,128)} %refs_4_.1) | copy-start | bytes 6291460
  51.3 5.4 %copy-start.13 = (f32[16,16,128]{2,1,0:T(8,128)S(1)}, f32[16,16,128]{2,1,0:T(8,128)}, u32[]{:S(2)}) copy-start(f32[16,16,128]{2,1,0:T(8,128)} %copy-done.12) | copy-start | bytes 393220
  51.3 5.4 %copy-start.16 = (s32[16,32]{1,0:T(8,128)S(1)}, s32[16,32]{1,0:T(8,128)}, u32[]{:S(2)}) copy-start(s32[16,32]{1,0:T(8,128)} %list_ref.2) | copy-start | bytes 6148
  51.3 5.4 %copy-start.17 = (s32[16,32]{1,0:T(8,128)S(1)}, s32[16,32]{1,0:T(8,128)}, u32[]{:S(2)}) copy-start(s32[16,32]{1,0:T(8,128)} %mask_ref.2) | copy-start | bytes 6148
  54.4 26.9 %collective-permute-start.12 = (f32[512,16,128]{2,1,0:T(8,128)S(1)}, f32[512,16,128]{2,1,0:T(8,128)S(1)}, u32[]{:S(2)}, u32[]{:S(2)}) collective-permute-start(f32[512,16,128]{2,1,0:T(8,128)S(1)} %pack.9), channel_id=1, source_target_pairs={{0,1},{1,0},{2,3},{3,2},{4,5},{5,4},{6,7},{7,6},{8,9},{9,8},{10,11... | collective-permute-start | bytes 12582920 | tf_op jit(solution)/shard_map/ppermute | solution.py:328
  81.3 23.3 %collective-permute-start.13 = (f32[128,16,128]{2,1,0:T(8,128)S(1)}, f32[128,16,128]{2,1,0:T(8,128)S(1)}, u32[]{:S(2)}, u32[]{:S(2)}) collective-permute-start(f32[128,16,128]{2,1,0:T(8,128)S(1)} %get-tuple-element.113), channel_id=1, source_target_pairs={{0,8},{1,9},{2,10},{3,11},{4,12},{5,13},{6,14},{7,15},{8,16},{9,17... | collective-permute-start | bytes 3145736 | tf_op jit(solution)/shard_map/ppermute | solution.py:318
  81.4 23.3 %collective-permute-start.14 = (f32[128,16,128]{2,1,0:T(8,128)S(1)}, f32[128,16,128]{2,1,0:T(8,128)S(1)}, u32[]{:S(2)}, u32[]{:S(2)}) collective-permute-start(f32[128,16,128]{2,1,0:T(8,128)S(1)} %get-tuple-element.114), channel_id=1, source_target_pairs={{0,24},{1,25},{2,26},{3,27},{4,28},{5,29},{6,30},{7,31},{8,0},{9,1... | collective-permute-start | bytes 3145736 | tf_op jit(solution)/shard_map/ppermute | solution.py:318
  84.1 22.7 %collective-permute-start.15 = (f32[128,16,128]{2,1,0:T(8,128)S(1)}, f32[128,16,128]{2,1,0:T(8,128)S(1)}, u32[]{:S(2)}, u32[]{:S(2)}) collective-permute-start(f32[128,16,128]{2,1,0:T(8,128)S(1)} %get-tuple-element.115), channel_id=1, source_target_pairs={{0,2},{1,3},{2,4},{3,5},{4,6},{5,7},{6,0},{7,1},{8,10},{9,11},{10,... | collective-permute-start | bytes 3145736 | tf_op jit(solution)/shard_map/ppermute | solution.py:318
  84.1 22.7 %collective-permute-start.16 = (f32[128,16,128]{2,1,0:T(8,128)S(1)}, f32[128,16,128]{2,1,0:T(8,128)S(1)}, u32[]{:S(2)}, u32[]{:S(2)}) collective-permute-start(f32[128,16,128]{2,1,0:T(8,128)S(1)} %get-tuple-element.116), channel_id=1, source_target_pairs={{0,6},{1,7},{2,0},{3,1},{4,2},{5,3},{6,4},{7,5},{8,14},{9,15},{10,... | collective-permute-start | bytes 3145736 | tf_op jit(solution)/shard_map/ppermute | solution.py:318
  93.3 13.7 %collective-permute-start.17 = (f32[768,16,128]{2,1,0:T(8,128)S(1)}, f32[768,16,128]{2,1,0:T(8,128)S(1)}, u32[]{:S(2)}, u32[]{:S(2)}) collective-permute-start(f32[768,16,128]{2,1,0:T(8,128)S(1)} %pack.11), channel_id=1, source_target_pairs={{0,1},{1,0},{2,3},{3,2},{4,5},{5,4},{6,7},{7,6},{8,9},{9,8},{10,11... | collective-permute-start | bytes 18874376 | tf_op jit(solution)/shard_map/ppermute | solution.py:328
  107.7 15.5 %collective-permute-start.22 = (f32[512,16,128]{2,1,0:T(8,128)S(1)}, f32[512,16,128]{2,1,0:T(8,128)S(1)}, u32[]{:S(2)}, u32[]{:S(2)}) collective-permute-start(f32[512,16,128]{2,1,0:T(8,128)S(1)} %pack.13), channel_id=1, source_target_pairs={{0,1},{1,0},{2,3},{3,2},{4,5},{5,4},{6,7},{7,6},{8,9},{9,8},{10,11... | collective-permute-start | bytes 12582920 | tf_op jit(solution)/shard_map/ppermute | solution.py:328
  111.9 9.1 %collective-permute-start.18 = (f32[32,16,128]{2,1,0:T(8,128)S(1)}, f32[32,16,128]{2,1,0:T(8,128)S(1)}, u32[]{:S(2)}, u32[]{:S(2)}) collective-permute-start(f32[32,16,128]{2,1,0:T(8,128)S(1)} %get-tuple-element.132), channel_id=1, source_target_pairs={{0,8},{1,9},{2,10},{3,11},{4,12},{5,13},{6,14},{7,15},{8,16},{9,17... | collective-permute-start | bytes 786440 | tf_op jit(solution)/shard_map/ppermute | solution.py:318
  111.9 9.1 %collective-permute-start.19 = (f32[32,16,128]{2,1,0:T(8,128)S(1)}, f32[32,16,128]{2,1,0:T(8,128)S(1)}, u32[]{:S(2)}, u32[]{:S(2)}) collective-permute-start(f32[32,16,128]{2,1,0:T(8,128)S(1)} %get-tuple-element.133), channel_id=1, source_target_pairs={{0,24},{1,25},{2,26},{3,27},{4,28},{5,29},{6,30},{7,31},{8,0},{9,1... | collective-permute-start | bytes 786440 | tf_op jit(solution)/shard_map/ppermute | solution.py:318
  114.6 8.4 %collective-permute-start.20 = (f32[32,16,128]{2,1,0:T(8,128)S(1)}, f32[32,16,128]{2,1,0:T(8,128)S(1)}, u32[]{:S(2)}, u32[]{:S(2)}) collective-permute-start(f32[32,16,128]{2,1,0:T(8,128)S(1)} %get-tuple-element.134), channel_id=1, source_target_pairs={{0,2},{1,3},{2,4},{3,5},{4,6},{5,7},{6,0},{7,1},{8,10},{9,11},{10,... | collective-permute-start | bytes 786440 | tf_op jit(solution)/shard_map/ppermute | solution.py:318
  114.6 8.4 %collective-permute-start.21 = (f32[32,16,128]{2,1,0:T(8,128)S(1)}, f32[32,16,128]{2,1,0:T(8,128)S(1)}, u32[]{:S(2)}, u32[]{:S(2)}) collective-permute-start(f32[32,16,128]{2,1,0:T(8,128)S(1)} %get-tuple-element.135), channel_id=1, source_target_pairs={{0,6},{1,7},{2,0},{3,1},{4,2},{5,3},{6,4},{7,5},{8,14},{9,15},{10,... | collective-permute-start | bytes 786440 | tf_op jit(solution)/shard_map/ppermute | solution.py:318
  123.2 4.4 %copy-start.2 = (f32[32,8192]{1,0:T(8,128)S(1)}, f32[32,8192]{1,0:T(8,128)}, u32[]{:S(2)}) copy-start(f32[32,8192]{1,0:T(8,128)} %refs_13_.1) | copy-start | bytes 3145732
  123.2 4.4 %copy-start.15 = (s32[128,16]{1,0:T(8,128)S(1)}, s32[128,16]{1,0:T(8,128)}, u32[]{:S(2)}) copy-start(s32[128,16]{1,0:T(8,128)} %copy-done.14) | copy-start | bytes 24580
  123.3 4.3 %copy-start.18 = (f32[512,16,128]{2,1,0:T(8,128)}, f32[512,16,128]{2,1,0:T(8,128)S(1)}, u32[]{:S(2)}) copy-start(f32[512,16,128]{2,1,0:T(8,128)S(1)} %collective-permute-done.22.refs_5_) | copy-start | bytes 12582916
  123.3 4.3 %collective-permute-start.23 = (f32[128,16,128]{2,1,0:T(8,128)S(1)}, f32[128,16,128]{2,1,0:T(8,128)S(1)}, u32[]{:S(2)}, u32[]{:S(2)}) collective-permute-start(f32[128,16,128]{2,1,0:T(8,128)S(1)} %pack.12), channel_id=1, source_target_pairs={{0,1},{1,0},{2,3},{3,2},{4,5},{5,4},{6,7},{7,6},{8,9},{9,8},{10,11... | collective-permute-start | bytes 3145736 | tf_op jit(solution)/shard_map/ppermute | solution.py:318
